TPU v7x, 32 devices: a whole 2x2x4 slice. The times are simulated.
32 devices in a mesh: frame: 2 (over x), row: 8 (over z, y), head: 2 (over core).
Axes of the slice: x: 2, y: 2, z: 4, core: 2. Of those that a mesh axis runs over, the one named last changes fastest.
Arguments:
- q_pre: bfloat16 [2, 16, 64, 2560], P('frame', 'row', None, 'head'), may hold values from -60 to 60
- k_pre: bfloat16 [2, 16, 64, 2560], P('frame', 'row', None, 'head'), may hold values from -60 to 60
- values: bfloat16 [2, 16, 64, 2560], P('frame', 'row', None, 'head'), may hold values from -6 to 6
- target: bfloat16 [2, 16, 64, 2560], P('frame', 'row', None, 'head'), may hold values from -6 to 6
- gain_q: float32 [2560], P('head'), may hold values from 0.5 to 2
- gain_k: float32 [2560], P('head'), may hold values from 0.5 to 2
- kept: int32 [2, 16, 4], replicated, may hold values 0 or 1
Outputs:
- grad_q: bfloat16 [2, 16, 64, 2560], P('frame', 'row', None, 'head')
- grad_k: bfloat16 [2, 16, 64, 2560], P('frame', 'row', None, 'head')
- grad_v: bfloat16 [2, 16, 64, 2560], P('frame', 'row', None, 'head')
All inputs are finite; a program needn't handle non-finite values.
Results may differ from a plain program's by a relative error of at most 0.0107.
The roundings to bfloat16 on the way count: a program that leaves them out, or rounds other values in their place, can miss the bound.
Values may be sent and summed in bfloat16 or wider, within the bound.
No kernel may reach another device: no remote copies, remote signals or barrier semaphores. Data moves between devices by JAX's collectives and lax.ppermute only.
A program may use at most 128 MiB of HBM per device.

v0:
```python
import jax
import jax.numpy as jnp
from jax import lax
from jax.sharding import PartitionSpec as P

TC = 16
HEADS = 20
HD = 128


norm_eps = 1e-06


def padded(x, sides, width):
    for axis, dim in sides:
        size, length = (lax.axis_size(axis), x.shape[dim])
        up = [(i, (i + 1) % size) for i in range(size - 1)]
        down = [(j, i) for i, j in up]
        last = lax.slice_in_dim(x, length - width, length, axis=dim)
        first = lax.slice_in_dim(x, 0, width, axis=dim)
        before = lax.ppermute(last, axis, up)
        after = lax.ppermute(first, axis, down)
        x = jnp.concatenate([before, x, after], axis=dim)
    return x


def from_behind(value, axis, steps):
    count = lax.axis_size(axis)
    first, last = (max(0, -steps), min(count, count - steps))
    return lax.ppermute(value, axis, [(source, source + steps) for source in range(first, last)])


def query_mask(kept_win, col_tile, tiles):
    near_cols = jnp.abs(col_tile[:, None] - col_tile[None, :]) <= 1
    same_tile = col_tile[:, None] == col_tile[None, :]
    one_hot = col_tile[:, None] == jnp.arange(tiles)[None, :]
    key_kept = jnp.any(one_hot[None, None] & (kept_win[:, :, None, :] > 0), axis=-1)
    centre = (jnp.arange(3)[:, None] == 1) & (jnp.arange(3)[None, :] == 1)
    allowed = near_cols[:, None, None, :] & (
        key_kept[None] | centre[None, :, :, None] & same_tile[:, None, None, :]
    )
    return allowed.reshape(col_tile.shape[0], -1)


def attend_line(query, kv_win, t_line, allowed):
    width, heads_dev, _ = query.shape
    score_scale = HD ** (-0.5)
    key_block = kv_win[0].reshape(9 * width, heads_dev, HD)
    value_block = kv_win[1].reshape(9 * width, heads_dev, HD)
    mask = allowed[None]
    scores = (
        jnp.einsum("qhd,khd->hqk", query, key_block, preferred_element_type=jnp.float32)
        * score_scale
    )
    scores = jnp.where(mask, scores, -jnp.inf)
    row_max = jnp.max(scores, -1, keepdims=True)
    expo = jnp.where(mask, jnp.exp(scores - row_max), 0.0)
    denominator = jnp.sum(expo, -1, keepdims=True)
    probability = expo / denominator
    prob_b = probability.astype(jnp.bfloat16)
    attended = jnp.einsum("hqk,khd->qhd", prob_b, value_block, preferred_element_type=jnp.float32)
    d_out = (attended - t_line.astype(jnp.float32)).astype(jnp.bfloat16)
    delta_sum = jnp.sum(d_out.astype(jnp.float32) * attended, -1).T
    prob_grad = jnp.einsum("qhd,khd->hqk", d_out, value_block, preferred_element_type=jnp.float32)
    score_grad = (probability * (prob_grad - delta_sum[:, :, None]) * score_scale).astype(
        jnp.bfloat16
    )
    dq_line = jnp.einsum("hqk,khd->qhd", score_grad, key_block, preferred_element_type=jnp.float32)
    log_total = row_max[..., 0] + jnp.log(denominator[..., 0])
    return (dq_line.reshape(width, heads_dev * HD), d_out, log_total, delta_sum, prob_b, score_grad)


def per_device(q_pre, k_pre, values, target, gain_q, gain_k, kept):
    frames, rows, width, feat_dev = q_pre.shape
    heads_dev = feat_dev // HD
    tiles = width // TC
    features = HEADS * HD
    line_count = frames * rows
    col_tile = jnp.arange(width) // TC
    q_float = q_pre.astype(jnp.float32)
    k_float = k_pre.astype(jnp.float32)
    square_q, square_k = lax.psum(
        (jnp.sum(q_float * q_float, -1), jnp.sum(k_float * k_float, -1)), "head"
    )
    scale_q = lax.rsqrt(square_q[..., None] / features + norm_eps)
    scale_k = lax.rsqrt(square_k[..., None] / features + norm_eps)
    q_norm = (q_float * scale_q * gain_q).astype(jnp.bfloat16)
    k_norm = (k_float * scale_k * gain_k).astype(jnp.bfloat16)
    kv_ext = padded(jnp.stack([k_norm, values]), (("frame", 1), ("row", 2)), 1)
    frame_at = lax.axis_index("frame")
    row_at = lax.axis_index("row")
    zero = jnp.int32(0)
    kept_pad = jnp.pad(kept, ((1, 1), (1, 1), (0, 0)))
    kept_ext = lax.dynamic_slice(
        kept_pad, (frame_at * frames, row_at * rows, zero), (frames + 2, rows + 2, tiles)
    )
    line_ids = jnp.arange(line_count, dtype=jnp.int32)
    q_lines = q_norm.reshape(line_count, width, heads_dev, HD)
    t_lines = target.reshape(line_count, width, heads_dev, HD)

    def query_window(line):
        f_at = line // rows
        r_at = line % rows
        kv_win = lax.dynamic_slice(
            kv_ext, (zero, f_at, r_at, zero, zero), (2, 3, 3, width, feat_dev)
        )
        kept_win = lax.dynamic_slice(kept_ext, (f_at, r_at, zero), (3, 3, tiles))
        return (f_at, r_at, kv_win, query_mask(kept_win, col_tile, tiles))

    def returned_step(totals, inputs):
        line, query, t_line = inputs
        f_at, r_at, kv_win, allowed = query_window(line)
        dq_line, d_out, log_total, delta_sum, prob_b, score_grad = attend_line(
            query, kv_win, t_line, allowed
        )
        key_grad = jnp.einsum("hqk,qhd->khd", score_grad, query, preferred_element_type=jnp.float32)
        value_grad = jnp.einsum("hqk,qhd->khd", prob_b, d_out, preferred_element_type=jnp.float32)
        both = jnp.stack(
            [key_grad.reshape(3, 3, width, feat_dev), value_grad.reshape(3, 3, width, feat_dev)]
        )
        start = (zero, f_at, r_at, zero, zero)
        current = lax.dynamic_slice(totals, start, (2, 3, 3, width, feat_dev))
        totals = lax.dynamic_update_slice(totals, current + both, start)
        return (totals, dq_line)

    empty = jnp.zeros((2, frames + 2, rows + 2, width, feat_dev), jnp.float32)
    totals, dq_lines = lax.scan(returned_step, empty, (line_ids, q_lines, t_lines))
    inner = totals[:, :, 1 : rows + 1]
    row_edges = (totals[:, :, 0:1], totals[:, :, rows + 1 : rows + 2])
    row_moved = [
        from_behind(row_edges[side], "row", by_value) for side, by_value in ((0, -1), (1, 1))
    ]
    inner = inner.at[:, :, rows - 1 : rows].add(row_moved[0])
    inner = inner.at[:, :, 0:1].add(row_moved[1])
    middle = inner[:, 1 : frames + 1]
    frame_edges = (inner[:, 0:1], inner[:, frames + 1 : frames + 2])
    frame_moved = [
        from_behind(frame_edges[side], "frame", by_value) for side, by_value in ((0, -1), (1, 1))
    ]
    middle = middle.at[:, frames - 1 : frames].add(frame_moved[0])
    middle = middle.at[:, 0:1].add(frame_moved[1])
    dk_norm = middle[0]
    value_total = middle[1]
    dq_norm = dq_lines.reshape(frames, rows, width, feat_dev)
    gated_q = gain_q * dq_norm
    gated_k = gain_k * dk_norm
    sum_q, sum_k = lax.psum(
        (jnp.sum(q_float * gated_q, -1), jnp.sum(k_float * gated_k, -1)), "head"
    )
    grad_q = (scale_q * gated_q - q_float * scale_q**3 * sum_q[..., None] / features).astype(
        jnp.bfloat16
    )
    grad_k = (scale_k * gated_k - k_float * scale_k**3 * sum_k[..., None] / features).astype(
        jnp.bfloat16
    )
    return (grad_q, grad_k, value_total.astype(jnp.bfloat16))


def solution(mesh):
    return jax.shard_map(
        per_device,
        mesh=mesh,
        in_specs=(
            P("frame", "row", None, "head"),
            P("frame", "row", None, "head"),
            P("frame", "row", None, "head"),
            P("frame", "row", None, "head"),
            P("head"),
            P("head"),
            P(),
        ),
        out_specs=(
            P("frame", "row", None, "head"),
            P("frame", "row", None, "head"),
            P("frame", "row", None, "head"),
        ),
        check_vma=False,
    )
```

profile of v0, /device:TPU:13, one launch (start us, length us, event | category | flops | bytes accessed | tf_op | source)
XLA Modules:
  0.0 310.1 jit_solution(15757480001772327974)
XLA Ops:
  0.6 1.2 fusion.36
  1.8 1.1 fusion.44
  2.9 2.8 all-reduce.2
  5.8 1.1 fusion.54
  6.9 1.0 pad_maximum_fusion.2
  7.9 1.3 collective-permute-start.1
  9.2 4.1 %collective-permute-start = (bf16[2,1,2,64,1280]{4,3,2,1,0:T(8,128)(2,1)S(1)}, bf16[2,1,2,64,1280]{4,3,2,1,0:T(8,128)(2,1)S(1)}, u32[]{:S(2)}, u32[]{:S(2)}) collective-permute-start(bf16[2,1,2,64,1280]{4,3,2,1,0:T(8,128)(2,1)S(1)} %pad_maximum_fusion.2), channel_id=1, source_target_pairs={{0,16},{1,17},{2,18},{3,19},{4,20},{5,21},{6,22},{7,23},{8,24},{9,... | collective-permute-start | bytes 1966088 | tf_op jit(solution)/shard_map/ppermute | solution.py:21
  13.3 12.5 %collective-permute-done.1 = bf16[2,1,2,64,1280]{4,3,2,1,0:T(8,128)(2,1)S(1)} collective-permute-done((bf16[2,1,2,64,1280]{4,3,2,1,0:T(8,128)(2,1)S(1)}, bf16[2,1,2,64,1280]{4,3,2,1,0:T(8,128)(2,1)S(1)}, u32[]{:S(2)}, u32[]{:S(2)}) %collective-permute-start.1) | collective-permute-done | bytes 655392 | tf_op jit(solution)/shard_map/ppermute | solution.py:22
  25.8 0.9 collective-permute-done
  27.0 1.4 fusion.63
  28.4 3.1 %collective-permute-start.2 = (bf16[2,3,1,64,1280]{4,3,2,1,0:T(8,128)(2,1)}, bf16[2,3,1,64,1280]{4,3,2,1,0:T(8,128)(2,1)}, u32[]{:S(2)}, u32[]{:S(2)}) collective-permute-start(bf16[2,3,1,64,1280]{4,3,2,1,0:T(8,128)(2,1)} %get-tuple-element.287), channel_id=1, source_target_pairs={{0,2},{2,4},{4,6},{6,8},{8,10},{10,12},{12,14},{1,3},{3,5},{5,7},{... | collective-permute-start | bytes 2949128 | tf_op jit(solution)/shard_map/ppermute | solution.py:21
  31.5 2.1 collective-permute-start.3
  34.2 1.2 reshape.461
  35.4 0.8 copy.33
  36.2 37.1 %collective-permute-done.2 = bf16[2,3,1,64,1280]{4,3,2,1,0:T(8,128)(2,1)} collective-permute-done((bf16[2,3,1,64,1280]{4,3,2,1,0:T(8,128)(2,1)}, bf16[2,3,1,64,1280]{4,3,2,1,0:T(8,128)(2,1)}, u32[]{:S(2)}, u32[]{:S(2)}) %collective-permute-start.2) | collective-permute-done | bytes 983072 | tf_op jit(solution)/shard_map/ppermute | solution.py:21
  73.4 0.8 collective-permute-done.3
  74.2 3.3 %pad_maximum_fusion = bf16[2,3,4,64,1280]{4,3,2,1,0:T(8,128)(2,1)} fusion(bf16[2,3,1,64,1280]{4,3,2,1,0:T(8,128)(2,1)} %collective-permute-done.3, bf16[2,1,2,64,1280]{4,3,2,1,0:T(8,128)(2,1)S(1)} %collective-permute-done.1, bf16[1,1,2,64,1280]{4,3,2,1,0:T(8,128)(2,1)S(1)} %bitcast.100, bf16[1,1,2,64,1280]{4,3,2,1,0:T(8,128)(2,1)S(1)} %fusion.54, ...), kind=kLoop, calls=%fused_computation.48 | loop fusion | flops 9830400 | bytes 7864320 | tf_op jit(solution)/shard_map/concatenate | solution.py:23
  77.5 3.9 %broadcast_in_dim.66 = f32[2,3,4,64,1280]{4,3,2,1,0:T(8,128)} broadcast(f32[]{:T(128)} %constant.234.clone.1), dimensions={} | broadcast | bytes 7864324 | tf_op jit(solution)/shard_map/broadcast_in_dim | solution.py:126
  81.5 93.6 %while.22 = (s32[]{:T(128)}, f32[2,3,4,64,1280]{4,3,2,1,0:T(8,128)}, f32[2,64,1280]{2,1,0:T(8,128)}, s32[2]{0:T(128)S(1)}, bf16[2,64,10,128]{3,1,2,0:T(8,128)(2,...) while((s32[]{:T(128)}, ...), condition=%wide.region_9.10_spmd.clone.clone, body=%wide.region_4.9_spmd.clone.clone.sunk | while | flops 574964416 | bytes 103695864 | solution.py:127
  81.5 0.6 dynamic_slice.85
  84.7 2.0 constant_dynamic-slice_fusion.3
  86.7 2.5 squeeze.45
  89.2 2.4 squeeze.46
  91.6 4.2 %fusion.92 = (f32[10,64]{1,0:T(8,128)S(1)}, f32[10,64,576]{2,1,0:T(8,128)}) fusion(bf16[576,10,128]{2,1,0:T(8,128)(2,1)} %squeeze.46, pred[64,576]{1,0:T(8,128)(4,1)S(1)} %copy.62, bf16[2,64,10,128]{3,1,2,0:T(8,128)(2,1)S(1)} %get-tuple-element.388, s32[]{:T(128)S(6)} %copy.71), kind=kOutput, calls=%fused_computation.90.clone.1 | convolution fusion | flops 96215616 | bytes 3197444 | tf_op jit(solution)/shard_map/while/body/eval_jaxpr/sub | solution.py:57
  95.8 2.5 multiply_reduce_fusion.2
  98.3 1.0 multiply_convert_fusion.2
  99.3 0.7 copy-done.1
  100.0 0.7 convolution_bitcast_fusion.9
  101.4 2.6 convolution_bitcast_fusion.7
  104.0 3.9 %copy.63 = f32[576,10,128]{2,1,0:T(8,128)} copy(f32[576,10,128]{2,0,1:T(8,128)S(1)} %convolution_bitcast_fusion.7) | data formatting | bytes 5898240 | tf_op jit(solution)/shard_map/while/body/eval_jaxpr/hqk,qhd->khd/transpose | solution.py:117
  107.9 3.2 %reshape.472 = f32[1,3,3,64,1280]{4,3,2,1,0:T(8,128)S(1)} reshape(f32[576,10,128]{2,1,0:T(8,128)} %copy.63) | data formatting | bytes 5898240 | tf_op jit(solution)/shard_map/while/body/eval_jaxpr/stack;while/body/eval_jaxpr/reshape | solution.py:118
  111.1 1.8 convolution_bitcast_fusion.8
  112.9 3.9 %copy.64 = f32[576,10,128]{2,1,0:T(8,128)} copy(f32[576,10,128]{2,0,1:T(8,128)S(1)} %convolution_bitcast_fusion.8) | data formatting | bytes 5898240 | tf_op jit(solution)/shard_map/while/body/eval_jaxpr/hqk,qhd->khd/transpose | solution.py:116
  116.8 4.7 %reshape.473 = f32[1,3,3,64,1280]{4,3,2,1,0:T(8,128)} reshape(f32[576,10,128]{2,1,0:T(8,128)} %copy.64) | data formatting | bytes 5898240 | tf_op jit(solution)/shard_map/while/body/eval_jaxpr/stack;while/body/eval_jaxpr/reshape | solution.py:118
  121.5 6.8 %fusion.93 = f32[2,3,4,64,1280]{4,3,2,1,0:T(8,128)} fusion(f32[2,3,4,64,1280]{4,3,2,1,0:T(8,128)} %get-tuple-element.372, s32[]{:T(128)S(6)} %select_n.86, f32[1,3,3,64,1280]{4,3,2,1,0:T(8,128)S(1)} %reshape.472, f32[1,3,3,64,1280]{4,3,2,1,0:T(8,128)} %reshape.473), kind=kLoop, calls=%fused_computation.3.clone.1 | loop fusion | flops 2949120 | bytes 17694724 | tf_op jit(solution)/shard_map/while/body/eval_jaxpr/dynamic_update_slice | solution.py:123
  131.5 2.0 constant_dynamic-slice_fusion.3
  133.6 2.5 squeeze.45
  136.0 2.4 squeeze.46
  138.4 4.2 %fusion.92 = (f32[10,64]{1,0:T(8,128)S(1)}, f32[10,64,576]{2,1,0:T(8,128)}) fusion(bf16[576,10,128]{2,1,0:T(8,128)(2,1)} %squeeze.46, pred[64,576]{1,0:T(8,128)(4,1)S(1)} %copy.62, bf16[2,64,10,128]{3,1,2,0:T(8,128)(2,1)S(1)} %get-tuple-element.388, s32[]{:T(128)S(6)} %copy.71), kind=kOutput, calls=%fused_computation.90.clone.1 | convolution fusion | flops 96215616 | bytes 3197444 | tf_op jit(solution)/shard_map/while/body/eval_jaxpr/sub | solution.py:57
  142.6 2.5 multiply_reduce_fusion.2
  145.1 1.0 multiply_convert_fusion.2
  146.1 0.7 copy-done.1
  146.8 0.7 convolution_bitcast_fusion.9
  148.2 2.6 convolution_bitcast_fusion.7
  150.8 3.9 %copy.63 = f32[576,10,128]{2,1,0:T(8,128)} copy(f32[576,10,128]{2,0,1:T(8,128)S(1)} %convolution_bitcast_fusion.7) | data formatting | bytes 5898240 | tf_op jit(solution)/shard_map/while/body/eval_jaxpr/hqk,qhd->khd/transpose | solution.py:117
  154.7 3.2 %reshape.472 = f32[1,3,3,64,1280]{4,3,2,1,0:T(8,128)S(1)} reshape(f32[576,10,128]{2,1,0:T(8,128)} %copy.63) | data formatting | bytes 5898240 | tf_op jit(solution)/shard_map/while/body/eval_jaxpr/stack;while/body/eval_jaxpr/reshape | solution.py:118
  157.9 1.8 convolution_bitcast_fusion.8
  159.7 3.9 %copy.64 = f32[576,10,128]{2,1,0:T(8,128)} copy(f32[576,10,128]{2,0,1:T(8,128)S(1)} %convolution_bitcast_fusion.8) | data formatting | bytes 5898240 | tf_op jit(solution)/shard_map/while/body/eval_jaxpr/hqk,qhd->khd/transpose | solution.py:116
  163.6 4.7 %reshape.473 = f32[1,3,3,64,1280]{4,3,2,1,0:T(8,128)} reshape(f32[576,10,128]{2,1,0:T(8,128)} %copy.64) | data formatting | bytes 5898240 | tf_op jit(solution)/shard_map/while/body/eval_jaxpr/stack;while/body/eval_jaxpr/reshape | solution.py:118
  168.3 6.8 %fusion.93 = f32[2,3,4,64,1280]{4,3,2,1,0:T(8,128)} fusion(f32[2,3,4,64,1280]{4,3,2,1,0:T(8,128)} %get-tuple-element.372, s32[]{:T(128)S(6)} %select_n.86, f32[1,3,3,64,1280]{4,3,2,1,0:T(8,128)S(1)} %reshape.472, f32[1,3,3,64,1280]{4,3,2,1,0:T(8,128)} %reshape.473), kind=kLoop, calls=%fused_computation.3.clone.1 | loop fusion | flops 2949120 | bytes 17694724 | tf_op jit(solution)/shard_map/while/body/eval_jaxpr/dynamic_update_slice | solution.py:123
  175.0 1.7 slice.174
  176.7 4.6 %collective-permute-start.4 = (f32[2,3,1,64,1280]{4,3,2,1,0:T(8,128)S(1)}, f32[2,3,1,64,1280]{4,3,2,1,0:T(8,128)S(1)}, u32[]{:S(2)}, u32[]{:S(2)}) collective-permute-start(f32[2,3,1,64,1280]{4,3,2,1,0:T(8,128)S(1)} %slice.174), channel_id=1, source_target_pairs={{2,0},{4,2},{6,4},{8,6},{10,8},{12,10},{14,12},{3,1},{5,3},{7,5},{... | collective-permute-start | bytes 5898248 | tf_op jit(solution)/shard_map/ppermute | solution.py:30
  181.3 2.4 slice.172
  183.7 40.7 %collective-permute-done.4 = f32[2,3,1,64,1280]{4,3,2,1,0:T(8,128)S(1)} collective-permute-done((f32[2,3,1,64,1280]{4,3,2,1,0:T(8,128)S(1)}, f32[2,3,1,64,1280]{4,3,2,1,0:T(8,128)S(1)}, u32[]{:S(2)}, u32[]{:S(2)}) %collective-permute-start.4) | collective-permute-done | bytes 1966112 | tf_op jit(solution)/shard_map/ppermute | solution.py:30
  224.8 3.5 %collective-permute-start.5 = (f32[2,3,1,64,1280]{4,3,2,1,0:T(8,128)S(1)}, f32[2,3,1,64,1280]{4,3,2,1,0:T(8,128)S(1)}, u32[]{:S(2)}, u32[]{:S(2)}) collective-permute-start(f32[2,3,1,64,1280]{4,3,2,1,0:T(8,128)S(1)} %get-tuple-element.283), channel_id=1, source_target_pairs={{0,2},{2,4},{4,6},{6,8},{8,10},{10,12},{12,14},{1,3},{3,5},{5,7},{... | collective-permute-start | bytes 5898248 | tf_op jit(solution)/shard_map/ppermute | solution.py:30
  228.3 41.1 %collective-permute-done.5 = f32[2,3,1,64,1280]{4,3,2,1,0:T(8,128)S(1)} collective-permute-done((f32[2,3,1,64,1280]{4,3,2,1,0:T(8,128)S(1)}, f32[2,3,1,64,1280]{4,3,2,1,0:T(8,128)S(1)}, u32[]{:S(2)}, u32[]{:S(2)}) %collective-permute-start.5) | collective-permute-done | bytes 1966112 | tf_op jit(solution)/shard_map/ppermute | solution.py:30
  270.1 1.4 collective-permute-start.6
  271.6 4.3 %collective-permute-start.7 = (f32[2,1,2,64,1280]{4,3,2,1,0:T(8,128)S(1)}, f32[2,1,2,64,1280]{4,3,2,1,0:T(8,128)S(1)}, u32[]{:S(2)}, u32[]{:S(2)}) collective-permute-start(f32[2,1,2,64,1280]{4,3,2,1,0:T(8,128)S(1)} %get-tuple-element.286), channel_id=1, source_target_pairs={{0,16},{1,17},{2,18},{3,19},{4,20},{5,21},{6,22},{7,23},{8,24},{9,... | collective-permute-start | bytes 3932168 | tf_op jit(solution)/shard_map/ppermute | solution.py:30
  276.1 24.1 %collective-permute-done.6 = f32[2,1,2,64,1280]{4,3,2,1,0:T(8,128)S(1)} collective-permute-done((f32[2,1,2,64,1280]{4,3,2,1,0:T(8,128)S(1)}, f32[2,1,2,64,1280]{4,3,2,1,0:T(8,128)S(1)}, u32[]{:S(2)}, u32[]{:S(2)}) %collective-permute-start.6) | collective-permute-done | bytes 1310752 | tf_op jit(solution)/shard_map/ppermute | solution.py:30
  300.2 1.0 collective-permute-done.7
  301.7 0.8 fusion.53
  302.4 5.7 %all-reduce.1 = (f32[2,64]{1,0:T(2,128)S(1)}, f32[2,64]{1,0:T(2,128)S(1)}) all-reduce(f32[2,64]{1,0:T(2,128)S(1)} %fusion.43, f32[2,64]{1,0:T(2,128)S(1)} %fusion.51), channel_id=1, replica_groups=mesh['frame'=2,'row'=8,'head'=2] {'head'}, use_global_device_ids=true, to_apply=%region_11.12 | all-reduce | flops 256 | bytes 2048 | tf_op jit(solution)/shard_map/psum | solution.py:147
  308.1 1.0 fusion.42
  309.1 1.0 fusion.50
  (109 shorter events, 6.3 us)
Async XLA Ops:
  0.6 26.1 %copy-start.7 = (bf16[1,2,64,1280]{3,2,1,0:T(8,128)(2,1)S(1)}, bf16[1,2,64,1280]{3,2,1,0:T(8,128)(2,1)}, u32[]{:S(2)}) copy-start(bf16[1,2,64,1280]{3,2,1,0:T(8,128)(2,1)} %param.23) | copy-start | bytes 983044
  5.7 21.0 %copy-start.20 = (f32[1,2,64]{2,1,0:T(2,128)}, f32[1,2,64]{2,1,0:T(2,128)S(1)}, u32[]{:S(2)}) copy-start(f32[1,2,64]{2,1,0:T(2,128)S(1)} %get-tuple-element.273) | copy-start | bytes 1540
  5.7 21.0 %copy-start.22 = (f32[1,2,64]{2,1,0:T(2,128)}, f32[1,2,64]{2,1,0:T(2,128)S(1)}, u32[]{:S(2)}) copy-start(f32[1,2,64]{2,1,0:T(2,128)S(1)} %get-tuple-element.274) | copy-start | bytes 1540
  5.7 1.1 copy-start.15
  5.7 28.0 %copy-start.17 = (f32[2,64]{1,0:T(2,128)}, f32[2,64]{1,0:T(2,128)S(1)}, u32[]{:S(2)}) copy-start(f32[2,64]{1,0:T(2,128)S(1)} %get-tuple-element.292) | copy-start | bytes 1540
  7.9 17.9 %collective-permute-start.1 = (bf16[2,1,2,64,1280]{4,3,2,1,0:T(8,128)(2,1)S(1)}, bf16[2,1,2,64,1280]{4,3,2,1,0:T(8,128)(2,1)S(1)}, u32[]{:S(2)}, u32[]{:S(2)}) collective-permute-start(bf16[2,1,2,64,1280]{4,3,2,1,0:T(8,128)(2,1)S(1)} %pad_maximum_fusion.2), channel_id=1, source_target_pairs={{16,0},{17,1},{18,2},{19,3},{20,4},{21,5},{22,6},{23,7},{24,8},{25... | collective-permute-start | bytes 1966088 | tf_op jit(solution)/shard_map/ppermute | solution.py:22
  9.2 17.5 %collective-permute-start = (bf16[2,1,2,64,1280]{4,3,2,1,0:T(8,128)(2,1)S(1)}, bf16[2,1,2,64,1280]{4,3,2,1,0:T(8,128)(2,1)S(1)}, u32[]{:S(2)}, u32[]{:S(2)}) collective-permute-start(bf16[2,1,2,64,1280]{4,3,2,1,0:T(8,128)(2,1)S(1)} %pad_maximum_fusion.2), channel_id=1, source_target_pairs={{0,16},{1,17},{2,18},{3,19},{4,20},{5,21},{6,22},{7,23},{8,24},{9,... | collective-permute-start | bytes 1966088 | tf_op jit(solution)/shard_map/ppermute | solution.py:21
  26.9 6.7 %copy-start.19 = (s32[2,16,4]{1,2,0:T(4,128)S(1)}, s32[2,16,4]{1,2,0:T(4,128)}, u32[]{:S(2)}) copy-start(s32[2,16,4]{1,2,0:T(4,128)} %param.27) | copy-start | bytes 1540
  26.9 6.8 %copy-start.4 = (bf16[1,2,64,1280]{3,2,1,0:T(8,128)(2,1)S(1)}, bf16[1,2,64,1280]{3,2,1,0:T(8,128)(2,1)}, u32[]{:S(2)}) copy-start(bf16[1,2,64,1280]{3,2,1,0:T(8,128)(2,1)} %param.21) | copy-start | bytes 983044
  27.0 6.8 %copy-start.12 = (f32[1280]{0:T(1024)S(1)}, f32[1280]{0:T(1024)}, u32[]{:S(2)}) copy-start(f32[1280]{0:T(1024)} %param.25) | copy-start | bytes 15364
  28.4 45.0 %collective-permute-start.2 = (bf16[2,3,1,64,1280]{4,3,2,1,0:T(8,128)(2,1)}, bf16[2,3,1,64,1280]{4,3,2,1,0:T(8,128)(2,1)}, u32[]{:S(2)}, u32[]{:S(2)}) collective-permute-start(bf16[2,3,1,64,1280]{4,3,2,1,0:T(8,128)(2,1)} %get-tuple-element.287), channel_id=1, source_target_pairs={{0,2},{2,4},{4,6},{6,8},{8,10},{10,12},{12,14},{1,3},{3,5},{5,7},{... | collective-permute-start | bytes 2949128 | tf_op jit(solution)/shard_map/ppermute | solution.py:21
  31.5 42.7 %collective-permute-start.3 = (bf16[2,3,1,64,1280]{4,3,2,1,0:T(8,128)(2,1)}, bf16[2,3,1,64,1280]{4,3,2,1,0:T(8,128)(2,1)}, u32[]{:S(2)}, u32[]{:S(2)}) collective-permute-start(bf16[2,3,1,64,1280]{4,3,2,1,0:T(8,128)(2,1)} %get-tuple-element.288), channel_id=1, source_target_pairs={{2,0},{4,2},{6,4},{8,6},{10,8},{12,10},{14,12},{3,1},{5,3},{7,5},{... | collective-permute-start | bytes 2949128 | tf_op jit(solution)/shard_map/ppermute | solution.py:22
  91.6 4.2 %copy-start.2 = (bf16[576,10,128]{2,1,0:T(8,128)(2,1)S(1)}, bf16[576,10,128]{2,1,0:T(8,128)(2,1)}, u32[]{:S(2)}) copy-start(bf16[576,10,128]{2,1,0:T(8,128)(2,1)} %squeeze.45) | copy-start | bytes 4423684 | tf_op jit(solution)/shard_map/while
  91.6 4.2 %copy-start.11 = (bf16[2,64,10,128]{3,1,2,0:T(8,128)(2,1)S(1)}, bf16[2,64,10,128]{3,1,2,0:T(8,128)(2,1)}, u32[]{:S(2)}) copy-start(bf16[2,64,10,128]{3,1,2,0:T(8,128)(2,1)} %get-tuple-element.391) | copy-start | bytes 983044 | tf_op jit(solution)/shard_map/while
  95.8 2.5 copy-start.24
  98.3 1.7 copy-start.1
  100.0 0.9 copy-start.3
  100.0 1.4 copy-start.8
  101.4 2.6 copy-start.9
  138.4 4.2 %copy-start.2 = (bf16[576,10,128]{2,1,0:T(8,128)(2,1)S(1)}, bf16[576,10,128]{2,1,0:T(8,128)(2,1)}, u32[]{:S(2)}) copy-start(bf16[576,10,128]{2,1,0:T(8,128)(2,1)} %squeeze.45) | copy-start | bytes 4423684 | tf_op jit(solution)/shard_map/while
  138.4 4.2 %copy-start.11 = (bf16[2,64,10,128]{3,1,2,0:T(8,128)(2,1)S(1)}, bf16[2,64,10,128]{3,1,2,0:T(8,128)(2,1)}, u32[]{:S(2)}) copy-start(bf16[2,64,10,128]{3,1,2,0:T(8,128)(2,1)} %get-tuple-element.391) | copy-start | bytes 983044 | tf_op jit(solution)/shard_map/while
  142.6 2.5 copy-start.24
  145.1 1.7 copy-start.1
  146.8 0.9 copy-start.3
  146.8 1.4 copy-start.8
  148.2 2.6 copy-start.9
  176.7 47.7 %copy-start = (f32[2,3,4,64,1280]{4,3,2,1,0:T(8,128)S(1)}, f32[2,3,4,64,1280]{4,3,2,1,0:T(8,128)}, u32[]{:S(2)}) copy-start(f32[2,3,4,64,1280]{4,3,2,1,0:T(8,128)} %get-tuple-element.189) | copy-start | bytes 23592964
  176.7 47.7 %collective-permute-start.4 = (f32[2,3,1,64,1280]{4,3,2,1,0:T(8,128)S(1)}, f32[2,3,1,64,1280]{4,3,2,1,0:T(8,128)S(1)}, u32[]{:S(2)}, u32[]{:S(2)}) collective-permute-start(f32[2,3,1,64,1280]{4,3,2,1,0:T(8,128)S(1)} %slice.174), channel_id=1, source_target_pairs={{2,0},{4,2},{6,4},{8,6},{10,8},{12,10},{14,12},{3,1},{5,3},{7,5},{... | collective-permute-start | bytes 5898248 | tf_op jit(solution)/shard_map/ppermute | solution.py:30
  224.8 44.6 %collective-permute-start.5 = (f32[2,3,1,64,1280]{4,3,2,1,0:T(8,128)S(1)}, f32[2,3,1,64,1280]{4,3,2,1,0:T(8,128)S(1)}, u32[]{:S(2)}, u32[]{:S(2)}) collective-permute-start(f32[2,3,1,64,1280]{4,3,2,1,0:T(8,128)S(1)} %get-tuple-element.283), channel_id=1, source_target_pairs={{0,2},{2,4},{4,6},{6,8},{8,10},{10,12},{12,14},{1,3},{3,5},{5,7},{... | collective-permute-start | bytes 5898248 | tf_op jit(solution)/shard_map/ppermute | solution.py:30
  269.9 6.0 %copy-start.21 = (f32[1,2,64]{2,1,0:T(2,128)S(1)}, f32[1,2,64]{2,1,0:T(2,128)}, u32[]{:S(2)}) copy-start(f32[1,2,64]{2,1,0:T(2,128)} %copy-done.20) | copy-start | bytes 1540
  269.9 6.0 %copy-start.23 = (f32[1,2,64]{2,1,0:T(2,128)S(1)}, f32[1,2,64]{2,1,0:T(2,128)}, u32[]{:S(2)}) copy-start(f32[1,2,64]{2,1,0:T(2,128)} %copy-done.22) | copy-start | bytes 1540
  269.9 6.0 %copy-start.5 = (bf16[1,2,64,1280]{3,2,1,0:T(8,128)(2,1)S(1)}, bf16[1,2,64,1280]{3,2,1,0:T(8,128)(2,1)}, u32[]{:S(2)}) copy-start(bf16[1,2,64,1280]{3,2,1,0:T(8,128)(2,1)} %param.21) | copy-start | bytes 983044
  269.9 6.0 %copy-start.10 = (f32[2,64,1280]{2,1,0:T(8,128)S(1)}, f32[2,64,1280]{2,1,0:T(8,128)}, u32[]{:S(2)}) copy-start(f32[2,64,1280]{2,1,0:T(8,128)} %get-tuple-element.188) | copy-start | bytes 1966084
  269.9 6.0 %copy-start.13 = (f32[1280]{0:T(1024)S(1)}, f32[1280]{0:T(1024)}, u32[]{:S(2)}) copy-start(f32[1280]{0:T(1024)} %param.25) | copy-start | bytes 15364
  270.1 30.1 %collective-permute-start.6 = (f32[2,1,2,64,1280]{4,3,2,1,0:T(8,128)S(1)}, f32[2,1,2,64,1280]{4,3,2,1,0:T(8,128)S(1)}, u32[]{:S(2)}, u32[]{:S(2)}) collective-permute-start(f32[2,1,2,64,1280]{4,3,2,1,0:T(8,128)S(1)} %get-tuple-element.285), channel_id=1, source_target_pairs={{16,0},{17,1},{18,2},{19,3},{20,4},{21,5},{22,6},{23,7},{24,8},{25... | collective-permute-start | bytes 3932168 | tf_op jit(solution)/shard_map/ppermute | solution.py:30
  271.6 29.6 %collective-permute-start.7 = (f32[2,1,2,64,1280]{4,3,2,1,0:T(8,128)S(1)}, f32[2,1,2,64,1280]{4,3,2,1,0:T(8,128)S(1)}, u32[]{:S(2)}, u32[]{:S(2)}) collective-permute-start(f32[2,1,2,64,1280]{4,3,2,1,0:T(8,128)S(1)} %get-tuple-element.286), channel_id=1, source_target_pairs={{0,16},{1,17},{2,18},{3,19},{4,20},{5,21},{6,22},{7,23},{8,24},{9,... | collective-permute-start | bytes 3932168 | tf_op jit(solution)/shard_map/ppermute | solution.py:30
  276.1 25.3 %copy-start.6 = (bf16[1,2,64,1280]{3,2,1,0:T(8,128)(2,1)S(1)}, bf16[1,2,64,1280]{3,2,1,0:T(8,128)(2,1)}, u32[]{:S(2)}) copy-start(bf16[1,2,64,1280]{3,2,1,0:T(8,128)(2,1)} %param.22) | copy-start | bytes 983044
  276.1 25.3 %copy-start.14 = (f32[1280]{0:T(1024)S(1)}, f32[1280]{0:T(1024)}, u32[]{:S(2)}) copy-start(f32[1280]{0:T(1024)} %param.26) | copy-start | bytes 15364
  276.1 32.0 %copy-start.18 = (f32[2,64]{1,0:T(2,128)S(1)}, f32[2,64]{1,0:T(2,128)}, u32[]{:S(2)}) copy-start(f32[2,64]{1,0:T(2,128)} %copy-done.17) | copy-start | bytes 1540
  301.5 7.7 %copy-start.16 = (f32[2,64]{1,0:T(2,128)S(1)}, f32[2,64]{1,0:T(2,128)}, u32[]{:S(2)}) copy-start(f32[2,64]{1,0:T(2,128)} %copy-done.15) | copy-start | bytes 1540
where the time goes:
time: 314 us; the launch traced here: 310 us
  waiting for transfers between devices  158 us (50%)
  local copies, waits for them, and re-layouts  62.5 us (20%)
  other arithmetic  26.2 us (8%)
  matrix products  25.5 us (8%)
  starting transfers between devices  24.4 us (8%)
  blocking collectives  8.46 us (3%)
  loops' own time  3.7 us (1%)
    ppermute x4, waiting for transfers between devices, from_behind(): lax.ppermute(value, axis, [(source, source + steps) for source in range(f...  107 us
    ppermute x2, waiting for transfers between devices, padded(): before = lax.ppermute(last, axis, up)  38 us
    reshape x4, local copies, waits for them, and re-layouts, returned_step(): jnp.stack([key_grad.reshape(3, 3, width, feat_dev), value_grad.reshape(3,...  15.7 us
    ppermute x4, starting transfers between devices, from_behind(): lax.ppermute(value, axis, [(source, source + steps) for source in range(f...  13.8 us
    dynamic_update_slice x2, other arithmetic, returned_step(): totals = lax.dynamic_update_slice(totals, current + both, start)  13.6 us
    ppermute x2, waiting for transfers between devices, padded(): after = lax.ppermute(first, axis, down)  13.3 us
    sub x2, matrix products, attend_line(): expo = jnp.where(mask, jnp.exp(scores - row_max), 0.0)  8.45 us
    transpose x2, local copies, waits for them, and re-layouts, returned_step(): jnp.einsum('hqk,qhd->khd', prob_b, d_out, preferred_element_type=jnp.floa...  7.81 us
  transfers between devices with their start and end apart: 8, of which 8 were waited for; matrix products, arithmetic and copies ran while one was open for 2% of the time, Pallas kernels for 0%

commit v1 on v0

--- a/solution.py
+++ b/solution.py
@@ -1,6 +1,10 @@
+import functools
+
 import jax
 import jax.numpy as jnp
 from jax import lax
+from jax.experimental import pallas as pl
+from jax.experimental.pallas import tpu as pltpu
 from jax.sharding import PartitionSpec as P
 
 TC = 16
@@ -156,9 +160,352 @@
     return (grad_q, grad_k, value_total.astype(jnp.bfloat16))
 
 
+SWAP = [(0, 1), (1, 0)]
+F32 = jnp.float32
+BF16 = jnp.bfloat16
+VMEM_LIMIT = 48 * 1024 * 1024
+
+
+def call(body, out_shape, **kw):
+    flops = kw.pop("flops", 10**6)
+    moved = kw.pop("moved", 10**6)
+    return pl.pallas_call(
+        body,
+        out_shape=out_shape,
+        compiler_params=pltpu.CompilerParams(vmem_limit_bytes=VMEM_LIMIT),
+        cost_estimate=pl.CostEstimate(flops=flops, bytes_accessed=moved, transcendentals=0),
+        **kw,
+    )
+
+
+def halves(half):
+    frame_at = lax.axis_index("frame")
+    mine = pl.multiple_of(frame_at * half, HD)
+    theirs = pl.multiple_of((1 - frame_at) * half, HD)
+    return (pl.ds(mine, half), pl.ds(theirs, half))
+
+
+def squares_kernel(q_ref, k_ref, v_ref, t_ref, sums_ref, vt_ref):
+    tokens, feat_dev = q_ref.shape
+    _, theirs = halves(feat_dev // 2)
+    vt_ref[:tokens] = v_ref[:, theirs]
+    vt_ref[tokens:] = t_ref[:, theirs]
+    q_float = q_ref[...].astype(F32)
+    k_float = k_ref[...].astype(F32)
+    sums_ref[:tokens] = jnp.sum(q_float * q_float, -1, keepdims=True)
+    sums_ref[tokens:] = jnp.sum(k_float * k_float, -1, keepdims=True)
+
+
+def norm_kernel(
+    width,
+    q_ref,
+    k_ref,
+    v_ref,
+    sums_ref,
+    peer_ref,
+    gain_q_ref,
+    gain_k_ref,
+    scale_ref,
+    own_ref,
+    swap_ref,
+    up_ref,
+    down_ref,
+    swap_up_ref,
+    swap_down_ref,
+):
+    tokens, feat_dev = q_ref.shape
+    features = HEADS * HD
+    mine, theirs = halves(feat_dev // 2)
+    scale = lax.rsqrt((sums_ref[...] + peer_ref[...]) / features + norm_eps)
+    scale_ref[...] = scale
+    scale_q, scale_k = (scale[:tokens], scale[tokens:])
+    for part, qk_ref, last_ref, first_ref in (
+        (mine, own_ref, up_ref, down_ref),
+        (theirs, swap_ref, swap_up_ref, swap_down_ref),
+    ):
+        q_norm = (q_ref[:, part].astype(F32) * scale_q * gain_q_ref[:, part]).astype(BF16)
+        k_norm = (k_ref[:, part].astype(F32) * scale_k * gain_k_ref[:, part]).astype(BF16)
+        qk_ref[:tokens] = q_norm
+        qk_ref[tokens:] = k_norm
+        last_ref[:width] = k_norm[tokens - width :]
+        last_ref[width:] = v_ref[tokens - width :, part]
+        first_ref[:width] = k_norm[:width]
+        first_ref[width:] = v_ref[:width, part]
+
+
+def attend_kernel(
+    width,
+    frame_ref,
+    own_qk_ref,
+    v_ref,
+    t_ref,
+    swap_qk_ref,
+    swap_vt_ref,
+    before_ref,
+    after_ref,
+    swap_before_ref,
+    swap_after_ref,
+    bias_ref,
+    own_grad_ref,
+    swap_grad_ref,
+    before_grad_ref,
+    after_grad_ref,
+    swap_before_grad_ref,
+    swap_after_grad_ref,
+):
+    tokens = v_ref.shape[0]
+    score_scale = HD ** (-0.5)
+    query = jnp.concatenate([own_qk_ref[:tokens], swap_qk_ref[:tokens]], 0)
+    target = jnp.concatenate([t_ref[...], swap_vt_ref[tokens:]], 0)
+    key = jnp.concatenate(
+        [
+            before_ref[:width],
+            own_qk_ref[tokens:],
+            after_ref[:width],
+            swap_before_ref[:width],
+            swap_qk_ref[tokens:],
+            swap_after_ref[:width],
+        ],
+        0,
+    )
+    value = jnp.concatenate(
+        [
+            before_ref[width:],
+            v_ref[...],
+            after_ref[width:],
+            swap_before_ref[width:],
+            swap_vt_ref[:tokens],
+            swap_after_ref[width:],
+        ],
+        0,
+    )
+
+    def product(a, b, a_dim, b_dim):
+        return lax.dot_general(a, b, (((a_dim,), (b_dim,)), ((), ())), preferred_element_type=F32)
+
+    scores = product(query, key, 1, 1) * score_scale + bias_ref[...]
+    row_max = jnp.max(scores, -1, keepdims=True)
+    expo = jnp.exp(scores - row_max)
+    probability = expo * (1.0 / jnp.sum(expo, -1, keepdims=True))
+    prob_b = probability.astype(BF16)
+    attended = product(prob_b, value, 1, 0)
+    d_out = (attended - target.astype(F32)).astype(BF16)
+    delta_sum = jnp.sum(d_out.astype(F32) * attended, -1, keepdims=True)
+    prob_grad = product(d_out, value, 1, 1)
+    score_grad = (probability * (prob_grad - delta_sum) * score_scale).astype(BF16)
+    dq = product(score_grad, key, 1, 0)
+    dk = product(score_grad, query, 0, 0)
+    dv = product(prob_b, d_out, 0, 0)
+    side = tokens + 2 * width
+    own_grad_ref[:tokens] = dq[:tokens]
+    swap_grad_ref[:tokens] = dq[tokens:].astype(BF16)
+    for at, grad in ((1, dk), (2, dv)):
+        own_grad_ref[at * tokens : (at + 1) * tokens] = grad[width : width + tokens]
+        swap_grad_ref[at * tokens : (at + 1) * tokens] = grad[
+            side + width : side + width + tokens
+        ].astype(BF16)
+        to = slice((at - 1) * width, at * width)
+        before_grad_ref[to] = grad[:width].astype(BF16)
+        after_grad_ref[to] = grad[width + tokens : side].astype(BF16)
+        swap_before_grad_ref[to] = grad[side : side + width].astype(BF16)
+        swap_after_grad_ref[to] = grad[side + width + tokens :].astype(BF16)
+
+
+def gather_kernel(
+    width,
+    q_ref,
+    k_ref,
+    gain_q_ref,
+    gain_k_ref,
+    own_ref,
+    swap_ref,
+    before_ref,
+    after_ref,
+    swap_before_ref,
+    swap_after_ref,
+    gated_q_ref,
+    gated_k_ref,
+    grad_v_ref,
+    sums_ref,
+):
+    tokens, feat_dev = q_ref.shape
+    mine, theirs = halves(feat_dev // 2)
+    sum_q = jnp.zeros((tokens, 1), F32)
+    sum_k = jnp.zeros((tokens, 1), F32)
+    for part, grad_ref, last_ref, first_ref in (
+        (mine, own_ref, before_ref, after_ref),
+        (theirs, swap_ref, swap_before_ref, swap_after_ref),
+    ):
+        half = feat_dev // 2
+        middle = jnp.zeros((tokens - 2 * width, half), F32)
+
+        def total(at):
+            sides = slice((at - 1) * width, at * width)
+            edge = [last_ref[sides].astype(F32), middle, first_ref[sides].astype(F32)]
+            if tokens == 2 * width:
+                edge = [edge[0], edge[2]]
+            grad = grad_ref[at * tokens : (at + 1) * tokens].astype(F32)
+            return grad + jnp.concatenate(edge, 0)
+
+        gated_q = gain_q_ref[:, part] * grad_ref[:tokens].astype(F32)
+        gated_k = gain_k_ref[:, part] * total(1)
+        grad_v_ref[:, part] = total(2).astype(BF16)
+        gated_q_ref[:, part] = gated_q
+        gated_k_ref[:, part] = gated_k
+        sum_q += jnp.sum(q_ref[:, part].astype(F32) * gated_q, -1, keepdims=True)
+        sum_k += jnp.sum(k_ref[:, part].astype(F32) * gated_k, -1, keepdims=True)
+    sums_ref[:tokens] = sum_q
+    sums_ref[tokens:] = sum_k
+
+
+def finish_kernel(
+    q_ref, k_ref, gated_q_ref, gated_k_ref, scale_ref, sums_ref, peer_ref, grad_q_ref, grad_k_ref
+):
+    tokens = q_ref.shape[0]
+    features = HEADS * HD
+    scale = scale_ref[...]
+    slope = scale * scale * scale * (sums_ref[...] + peer_ref[...]) / features
+    for rows, pre_ref, gated_ref, out_ref in (
+        (slice(0, tokens), q_ref, gated_q_ref, grad_q_ref),
+        (slice(tokens, 2 * tokens), k_ref, gated_k_ref, grad_k_ref),
+    ):
+        out_ref[...] = (
+            scale[rows] * gated_ref[...] - pre_ref[...].astype(F32) * slope[rows]
+        ).astype(BF16)
+
+
+def window_bias(kept, rows, width, tiles):
+    frame_at = lax.axis_index("frame")
+    row_at = lax.axis_index("row")
+    kept_pad = jnp.pad(kept, ((0, 0), (1, 1), (0, 0)))
+    kept_win = lax.dynamic_slice_in_dim(kept_pad, row_at * rows, rows + 2, 1)
+    kept_win = jnp.where(frame_at == 0, kept_win, kept_win[::-1])
+    key_kept = jnp.repeat(kept_win.reshape(-1), width // tiles)
+    query_at = jnp.arange(2 * rows * width)
+    key_at = jnp.arange(2 * (rows + 2) * width)
+    query_row, query_tile = (query_at // width, query_at % width // TC)
+    key_row, key_tile = (key_at // width, key_at % width // TC)
+    near_cols = jnp.abs(query_tile[:, None] - key_tile[None, :]) <= 1
+    near_rows = jnp.abs((query_row % rows)[:, None] + 1 - (key_row % (rows + 2))[None, :]) <= 1
+    same_line = (query_row // rows * (rows + 2) + query_row % rows + 1)[:, None] == key_row[None, :]
+    same = same_line & (query_tile[:, None] == key_tile[None, :])
+    allowed = near_cols & near_rows & ((key_kept > 0)[None, :] | same)
+    return jnp.where(allowed, 0.0, -1e30).astype(F32)
+
+
+def swapped_device(q_pre, k_pre, values, target, gain_q, gain_k, kept):
+    frames, rows, width, feat_dev = q_pre.shape
+    tokens = rows * width
+    half = feat_dev // 2
+    half_heads = half // HD
+    row_blocks = lax.axis_size("row")
+    q_all, k_all, v_all, t_all = (
+        array.reshape(tokens, feat_dev) for array in (q_pre, k_pre, values, target)
+    )
+    gain_q = gain_q.reshape(1, feat_dev)
+    gain_k = gain_k.reshape(1, feat_dev)
+    up = [(r, r + 1) for r in range(row_blocks - 1)]
+    down = [(r + 1, r) for r in range(row_blocks - 1)]
+    swap_up, swap_down = (
+        [(f * row_blocks + a, (1 - f) * row_blocks + b) for f in range(2) for a, b in pairs]
+        for pairs in (up, down)
+    )
+
+    def shape(first, last, dtype=BF16):
+        return jax.ShapeDtypeStruct((first, last), dtype)
+
+    sums, vt_out = call(squares_kernel, (shape(2 * tokens, 1, F32), shape(2 * tokens, half)))(
+        q_all, k_all, v_all, t_all
+    )
+    swap_vt = lax.ppermute(vt_out, "frame", SWAP)
+    peer = lax.ppermute(sums, "head", SWAP)
+    scale, own_qk, qk_out, last, first, swap_last, swap_first = call(
+        functools.partial(norm_kernel, width),
+        (shape(2 * tokens, 1, F32),)
+        + (shape(2 * tokens, half),) * 2
+        + (shape(2 * width, half),) * 4,
+    )(q_all, k_all, v_all, sums, peer, gain_q, gain_k)
+    swap_qk = lax.ppermute(qk_out, "frame", SWAP)
+    swap_before = lax.ppermute(swap_last, ("frame", "row"), swap_up)
+    swap_after = lax.ppermute(swap_first, ("frame", "row"), swap_down)
+    before = lax.ppermute(last, "row", up)
+    after = lax.ppermute(first, "row", down)
+    bias = window_bias(kept, rows, width, kept.shape[-1])
+    frame_at = lax.axis_index("frame").reshape(1).astype(jnp.int32)
+
+    def by_head(size):
+        return pl.BlockSpec((size, HD), lambda h, f: (0, h))
+
+    own_half = pl.BlockSpec((tokens, HD), lambda h, f: (0, f[0] * half_heads + h))
+    own_grad, swap_grad, before_grad, after_grad, swap_before_grad, swap_after_grad = call(
+        functools.partial(attend_kernel, width),
+        (shape(3 * tokens, half, F32), shape(3 * tokens, half))
+        + (shape(2 * width, half),) * 4,
+        grid_spec=pltpu.PrefetchScalarGridSpec(
+            num_scalar_prefetch=1,
+            grid=(half_heads,),
+            in_specs=[
+                by_head(2 * tokens),
+                own_half,
+                own_half,
+                by_head(2 * tokens),
+                by_head(2 * tokens),
+                by_head(2 * width),
+                by_head(2 * width),
+                by_head(2 * width),
+                by_head(2 * width),
+                pl.BlockSpec(bias.shape, lambda h, f: (0, 0)),
+            ],
+            out_specs=[by_head(3 * tokens)] * 2 + [by_head(2 * width)] * 4,
+        ),
+        flops=10**9,
+        moved=4 * 10**6,
+    )(
+        frame_at,
+        own_qk,
+        v_all,
+        t_all,
+        swap_qk,
+        swap_vt,
+        before,
+        after,
+        swap_before,
+        swap_after,
+        bias,
+    )
+    swap_total = lax.ppermute(swap_grad, "frame", SWAP)
+    swap_last_in = lax.ppermute(swap_before_grad, ("frame", "row"), swap_down)
+    swap_first_in = lax.ppermute(swap_after_grad, ("frame", "row"), swap_up)
+    last_in = lax.ppermute(before_grad, "row", down)
+    first_in = lax.ppermute(after_grad, "row", up)
+    gated_q, gated_k, grad_v, sum_terms = call(
+        functools.partial(gather_kernel, width),
+        (shape(tokens, feat_dev, F32),) * 2
+        + (shape(tokens, feat_dev), shape(2 * tokens, 1, F32)),
+    )(
+        q_all,
+        k_all,
+        gain_q,
+        gain_k,
+        own_grad,
+        swap_total,
+        first_in,
+        last_in,
+        swap_first_in,
+        swap_last_in,
+    )
+    sum_peer = lax.ppermute(sum_terms, "head", SWAP)
+    grad_q, grad_k = call(finish_kernel, (shape(tokens, feat_dev),) * 2)(
+        q_all, k_all, gated_q, gated_k, scale, sum_terms, sum_peer
+    )
+    return tuple(
+        array.reshape(frames, rows, width, feat_dev) for array in (grad_q, grad_k, grad_v)
+    )
+
+
 def solution(mesh):
     return jax.shard_map(
-        per_device,
+        swapped_device if mesh.shape["frame"] == 2 else per_device,
         mesh=mesh,
         in_specs=(
             P("frame", "row", None, "head"),

time: 314 us -> 61.3 us (0.20); the launches traced: 310 us -> 60.7 us
  waiting for transfers between devices: 158 us -> 12.4 us
  local copies, waits for them, and re-layouts: 62.5 us -> 5.72 us
  other arithmetic: 26.2 us -> 0.45 us
  matrix products: 25.5 us -> 0 us
  Pallas kernels: 0 us -> 9.23 us
  blocking collectives: 8.46 us -> 0 us
  starting transfers between devices: 24.4 us -> 32.1 us
  loops' own time: 3.7 us -> 0 us
    ppermute x8 -> x13, waiting for transfers between devices: 158 us -> 12.4 us  [the longest x1 3.23 us: swapped_device(): swap_first_in = lax.ppermute(swap_after_grad, ('frame', 'row'), swap_up)]
    dot_general x10 -> x0, matrix products: 17.1 us -> none  [the longest x2 5.11 us: returned_step(): jnp.einsum('hqk,qhd->khd', prob_b, d_out, preferred_element_type=jnp.floa...]
    reshape x6 -> x2, local copies, waits for them, and re-layouts: 17.1 us -> 0.01 us  [the longest x1 0.01 us: swapped_device(): gain_q = gain_q.reshape(1, feat_dev)]
    transpose x6 -> x0, local copies, waits for them, and re-layouts: 16 us -> none  [the longest x2 7.81 us: returned_step(): jnp.einsum('hqk,qhd->khd', prob_b, d_out, preferred_element_type=jnp.floa...]
    dynamic_update_slice x2 -> x0, other arithmetic: 13.6 us -> none  [returned_step(): totals = lax.dynamic_update_slice(totals, current + both, start)]
    squeeze x4 -> x0, local copies, waits for them, and re-layouts: 9.68 us -> none  [the longest x2 4.94 us: attend_line(): value_block = kv_win[1].reshape(9 * width, heads_dev, HD)]
    slice x6 -> x0, local copies, waits for them, and re-layouts: 9.66 us -> none  [the longest x2 4.04 us: attend_line(): key_block = kv_win[0].reshape(9 * width, heads_dev, HD)]
    pallas_call x0 -> x5, Pallas kernels: none -> 9.23 us  [the longest x1 6.04 us: swapped_device(): call(functools.partial(attend_kernel, width), (shape(3 * tokens, half, F3...]
  transfers between devices with their start and end apart: 8 -> 13, of which waited for: 8 -> 5; matrix products, arithmetic and copies ran while one was open for 2% -> 1% of each run, Pallas kernels for 0% -> 1%
where the time goes in v1:
time: 61.3 us; the launch traced here: 60.7 us
  starting transfers between devices  32.1 us (52%)
  waiting for transfers between devices  12.4 us (20%)
  Pallas kernels  9.23 us (15%)
  local copies, waits for them, and re-layouts  5.72 us (9%)
  between operations  0.8 us (1%)
    pallas_call x1, Pallas kernels, swapped_device(): call(functools.partial(attend_kernel, width), (shape(3 * tokens, half, F3...  6.04 us
    ppermute x1, starting transfers between devices, swapped_device(): first_in = lax.ppermute(after_grad, 'row', up)  5.75 us
    unnamed x22, local copies, waits for them, and re-layouts  5.27 us
    ppermute x1, starting transfers between devices, swapped_device(): swap_before = lax.ppermute(swap_last, ('frame', 'row'), swap_up)  4.97 us
    ppermute x1, starting transfers between devices, swapped_device(): swap_first_in = lax.ppermute(swap_after_grad, ('frame', 'row'), swap_up)  4.1 us
    ppermute x1, starting transfers between devices, swapped_device(): sum_peer = lax.ppermute(sum_terms, 'head', SWAP)  3.34 us
    ppermute x1, starting transfers between devices, swapped_device(): before = lax.ppermute(last, 'row', up)  3.27 us
    ppermute x1, waiting for transfers between devices, swapped_device(): swap_first_in = lax.ppermute(swap_after_grad, ('frame', 'row'), swap_up)  3.23 us
  transfers between devices with their start and end apart: 13, of which 5 were waited for; matrix products, arithmetic and copies ran while one was open for 1% of the time, Pallas kernels for 1%

profile of v1, /device:TPU:13, one launch (start us, length us, event | category | flops | bytes accessed | tf_op | source)
XLA Modules:
  0.0 60.7 jit_solution(14894597182429380866)
XLA Ops:
  0.6 0.0 copy-start
  0.6 1.0 %copy-done = bf16[1,2,64,1280]{3,2,1,0:T(8,128)(2,1)S(1)} copy-done((bf16[1,2,64,1280]{3,2,1,0:T(8,128)(2,1)S(1)}, bf16[1,2,64,1280]{3,2,1,0:T(8,128)(2,1)}, u32[]{:S(2)}) %copy-start) | copy-done | bytes 327704
  1.6 0.0 copy-start.2
  1.6 1.0 %copy-done.2 = bf16[1,2,64,1280]{3,2,1,0:T(8,128)(2,1)S(1)} copy-done((bf16[1,2,64,1280]{3,2,1,0:T(8,128)(2,1)S(1)}, bf16[1,2,64,1280]{3,2,1,0:T(8,128)(2,1)}, u32[]{:S(2)}) %copy-start.2) | copy-done | bytes 327704
  2.6 0.0 copy-start.4
  2.6 1.0 %copy-done.4 = bf16[1,2,64,1280]{3,2,1,0:T(8,128)(2,1)S(1)} copy-done((bf16[1,2,64,1280]{3,2,1,0:T(8,128)(2,1)S(1)}, bf16[1,2,64,1280]{3,2,1,0:T(8,128)(2,1)}, u32[]{:S(2)}) %copy-start.4) | copy-done | bytes 327704
  3.6 0.0 copy-start.6
  3.6 1.0 %copy-done.6 = bf16[1,2,64,1280]{3,2,1,0:T(8,128)(2,1)S(1)} copy-done((bf16[1,2,64,1280]{3,2,1,0:T(8,128)(2,1)S(1)}, bf16[1,2,64,1280]{3,2,1,0:T(8,128)(2,1)}, u32[]{:S(2)}) %copy-start.6) | copy-done | bytes 327704
  4.5 0.0 copy-start.1
  4.5 0.0 copy-start.3
  4.5 0.0 copy-start.5
  4.5 0.2 shard_map.94
  4.7 0.7 %collective-permute-start = (f32[256,1]{1,0:T(8,128)S(1)}, f32[256,1]{1,0:T(8,128)S(1)}, u32[]{:S(2)}, u32[]{:S(2)}) collective-permute-start(f32[256,1]{1,0:T(8,128)S(1)} %get-tuple-element.24.sums_ref), channel_id=1, source_target_pairs={{0,1},{1,0},{2,3},{3,2},{4,5},{5,4},{6,7},{7,6},{8,9},{9,8},{10,11... | collective-permute-start | bytes 3080 | tf_op jit(solution)/shard_map/ppermute | solution.py:421
  5.5 1.2 %collective-permute-start.2 = (bf16[256,640]{1,0:T(8,128)(2,1)S(1)}, bf16[256,640]{1,0:T(8,128)(2,1)S(1)}, u32[]{:S(2)}, u32[]{:S(2)}) collective-permute-start(bf16[256,640]{1,0:T(8,128)(2,1)S(1)} %get-tuple-element.27), channel_id=1, source_target_pairs={{0,16},{16,0},{1,17},{17,1},{2,18},{18,2},{3,19},{19,3},{4,20},{20... | collective-permute-start | bytes 983048 | tf_op jit(solution)/shard_map/ppermute | solution.py:420
  6.7 0.0 copy-start.10
  6.7 0.7 %copy-done.10 = s32[2,16,4]{1,2,0:T(4,128)S(1)} copy-done((s32[2,16,4]{1,2,0:T(4,128)S(1)}, s32[2,16,4]{1,2,0:T(4,128)}, u32[]{:S(2)}) %copy-start.10) | copy-done | bytes 536
  7.4 0.0 copy-start.8
  7.4 0.1 pad_dynamic-slice_fusion
  7.5 0.0 copy-start.9
  7.5 0.6 copy-done.8
  8.1 0.1 copy-done.9
  8.2 0.0 collective-permute-done.peer_ref
  8.2 0.0 copy-done.1
  8.2 0.0 copy-done.3
  8.2 0.0 copy-done.5
  8.2 0.9 %shard_map.95 = (f32[256,1]{1,0:T(8,128)S(1)}, bf16[256,640]{1,0:T(8,128)(2,1)S(1)}, bf16[256,640]{1,0:T(8,128)(2,1)S(1)}, bf16[128,640]{1,0:T(8,128)(2,1)}, bf1...) custom-call(bf16[128,1280]{1,0:T(8,128)(2,1)S(1)} %bitcast.9, ...), custom_call_target="tpu_custom_call" | custom-call | flops 1000000 | bytes 1000000 | tf_op jit(solution)/shard_map/pallas_call | solution.py:422
  9.1 0.0 copy-start.7
  9.1 3.3 %collective-permute-start.3 = (bf16[128,640]{1,0:T(8,128)(2,1)}, bf16[128,640]{1,0:T(8,128)(2,1)S(1)}, u32[]{:S(2)}, u32[]{:S(2)}) collective-permute-start(bf16[128,640]{1,0:T(8,128)(2,1)} %get-tuple-element.28), channel_id=1, source_target_pairs={{0,2},{2,4},{4,6},{6,8},{8,10},{10,12},{12,14},{1,3},{3,5},{5,7},{... | collective-permute-start | bytes 491528 | tf_op jit(solution)/shard_map/ppermute | solution.py:431
  12.3 0.1 copy.11
  12.5 0.1 gt.16
  12.6 0.1 broadcast_in_dim.8
  12.6 0.1 gt.17
  12.7 0.3 collective-permute-start.1
  13.0 2.1 %collective-permute-start.4 = (bf16[128,640]{1,0:T(8,128)(2,1)S(1)}, bf16[128,640]{1,0:T(8,128)(2,1)S(1)}, u32[]{:S(2)}, u32[]{:S(2)}) collective-permute-start(bf16[128,640]{1,0:T(8,128)(2,1)S(1)} %get-tuple-element.29), channel_id=1, source_target_pairs={{2,0},{4,2},{6,4},{8,6},{10,8},{12,10},{14,12},{3,1},{5,3},{7,5},{... | collective-permute-start | bytes 491528 | tf_op jit(solution)/shard_map/ppermute | solution.py:432
  15.1 5.0 %collective-permute-start.5 = (bf16[128,640]{1,0:T(8,128)(2,1)S(1)}, bf16[128,640]{1,0:T(8,128)(2,1)S(1)}, u32[]{:S(2)}, u32[]{:S(2)}) collective-permute-start(bf16[128,640]{1,0:T(8,128)(2,1)S(1)} %get-tuple-element.30), channel_id=1, source_target_pairs={{0,18},{2,20},{4,22},{6,24},{8,26},{10,28},{12,30},{16,2},{18,4},{... | collective-permute-start | bytes 491528 | tf_op jit(solution)/shard_map/ppermute | solution.py:429
  20.1 0.0 collective-permute-done.3.before_ref
  20.1 1.9 %collective-permute-start.6 = (bf16[128,640]{1,0:T(8,128)(2,1)S(1)}, bf16[128,640]{1,0:T(8,128)(2,1)S(1)}, u32[]{:S(2)}, u32[]{:S(2)}) collective-permute-start(bf16[128,640]{1,0:T(8,128)(2,1)S(1)} %get-tuple-element.31), channel_id=1, source_target_pairs={{2,16},{4,18},{6,20},{8,22},{10,24},{12,26},{14,28},{18,0},{20,2},... | collective-permute-start | bytes 491528 | tf_op jit(solution)/shard_map/ppermute | solution.py:430
  22.1 0.4 fusion.2.bias_ref
  22.5 0.0 collective-permute-done.4.after_ref
  22.5 2.3 %collective-permute-done.5.swap_before_ref = bf16[128,640]{1,0:T(8,128)(2,1)S(1)} collective-permute-done((bf16[128,640]{1,0:T(8,128)(2,1)S(1)}, bf16[128,640]{1,0:T(8,128)(2,1)S(1)}, u32[]{:S(2)}, u32[]{:S(2)}) %collective-permute-start.5) | collective-permute-done | bytes 163872 | tf_op jit(solution)/shard_map/ppermute | solution.py:429
  24.8 3.2 %collective-permute-done.6.swap_after_ref = bf16[128,640]{1,0:T(8,128)(2,1)S(1)} collective-permute-done((bf16[128,640]{1,0:T(8,128)(2,1)S(1)}, bf16[128,640]{1,0:T(8,128)(2,1)S(1)}, u32[]{:S(2)}, u32[]{:S(2)}) %collective-permute-start.6) | collective-permute-done | bytes 163872 | tf_op jit(solution)/shard_map/ppermute | solution.py:430
  28.0 0.0 collective-permute-done.2.swap_vt_ref
  28.0 0.0 collective-permute-done.1.swap_qk_ref
  28.0 0.0 copy-done.7
  28.0 6.0 %shard_map.96 = (f32[384,640]{1,0:T(8,128)S(1)}, bf16[384,640]{1,0:T(8,128)(2,1)S(1)}, bf16[128,640]{1,0:T(8,128)(2,1)S(1)}, bf16[128,640]{1,0:T(8,128)(2,1)S(1)...) custom-call(s32[1]{0:T(128)} %bitcast.2.frame_ref, bf16[256,640]{1,0:T(8,128)(2,1)S(1)} %get-tuple-element.25.own_qk_ref, ...), custom_call_target="tpu_custom_call" | custom-call | flops 1000000000 | bytes 4000000 | tf_op jit(solution)/shard_map/pallas_call | solution.py:440
  34.1 0.4 collective-permute-start.7
  34.5 5.7 %collective-permute-start.8 = (bf16[128,640]{1,0:T(8,128)(2,1)S(1)}, bf16[128,640]{1,0:T(8,128)(2,1)S(1)}, u32[]{:S(2)}, u32[]{:S(2)}) collective-permute-start(bf16[128,640]{1,0:T(8,128)(2,1)S(1)} %get-tuple-element.34), channel_id=1, source_target_pairs={{0,2},{2,4},{4,6},{6,8},{8,10},{10,12},{12,14},{1,3},{3,5},{5,7},{... | collective-permute-start | bytes 491528 | tf_op jit(solution)/shard_map/ppermute | solution.py:480
  40.2 1.9 %collective-permute-start.9 = (bf16[128,640]{1,0:T(8,128)(2,1)S(1)}, bf16[128,640]{1,0:T(8,128)(2,1)S(1)}, u32[]{:S(2)}, u32[]{:S(2)}) collective-permute-start(bf16[128,640]{1,0:T(8,128)(2,1)S(1)} %get-tuple-element.35), channel_id=1, source_target_pairs={{2,0},{4,2},{6,4},{8,6},{10,8},{12,10},{14,12},{3,1},{5,3},{7,5},{... | collective-permute-start | bytes 491528 | tf_op jit(solution)/shard_map/ppermute | solution.py:479
  42.2 4.1 %collective-permute-start.10 = (bf16[128,640]{1,0:T(8,128)(2,1)S(1)}, bf16[128,640]{1,0:T(8,128)(2,1)S(1)}, u32[]{:S(2)}, u32[]{:S(2)}) collective-permute-start(bf16[128,640]{1,0:T(8,128)(2,1)S(1)} %get-tuple-element.36), channel_id=1, source_target_pairs={{0,18},{2,20},{4,22},{6,24},{8,26},{10,28},{12,30},{16,2},{18,4},{... | collective-permute-start | bytes 491528 | tf_op jit(solution)/shard_map/ppermute | solution.py:478
  46.3 2.1 %collective-permute-start.11 = (bf16[128,640]{1,0:T(8,128)(2,1)S(1)}, bf16[128,640]{1,0:T(8,128)(2,1)S(1)}, u32[]{:S(2)}, u32[]{:S(2)}) collective-permute-start(bf16[128,640]{1,0:T(8,128)(2,1)S(1)} %get-tuple-element.37), channel_id=1, source_target_pairs={{2,16},{4,18},{6,20},{8,22},{10,24},{12,26},{14,28},{18,0},{20,2},... | collective-permute-start | bytes 491528 | tf_op jit(solution)/shard_map/ppermute | solution.py:477
  48.4 0.0 collective-permute-done.8.before_ref
  48.4 0.0 collective-permute-done.9.after_ref
  48.4 3.2 %collective-permute-done.10.swap_before_ref = bf16[128,640]{1,0:T(8,128)(2,1)S(1)} collective-permute-done((bf16[128,640]{1,0:T(8,128)(2,1)S(1)}, bf16[128,640]{1,0:T(8,128)(2,1)S(1)}, u32[]{:S(2)}, u32[]{:S(2)}) %collective-permute-start.10) | collective-permute-done | bytes 163872 | tf_op jit(solution)/shard_map/ppermute | solution.py:478
  51.6 2.7 %collective-permute-done.11.swap_after_ref = bf16[128,640]{1,0:T(8,128)(2,1)S(1)} collective-permute-done((bf16[128,640]{1,0:T(8,128)(2,1)S(1)}, bf16[128,640]{1,0:T(8,128)(2,1)S(1)}, u32[]{:S(2)}, u32[]{:S(2)}) %collective-permute-start.11) | collective-permute-done | bytes 163872 | tf_op jit(solution)/shard_map/ppermute | solution.py:477
  54.3 0.0 collective-permute-done.7.swap_ref
  54.3 1.1 %shard_map.97 = (f32[128,1280]{1,0:T(8,128)S(1)}, f32[128,1280]{1,0:T(8,128)S(1)}, bf16[128,1280]{1,0:T(8,128)(2,1)}, f32[256,1]{1,0:T(8,128)S(1)}) custom-call(bf16[128,1280]{1,0:T(8,128)(2,1)S(1)} %bitcast.10, bf16[128,1280]{1,0:T(8,128)(2,1)S(1)} %bitcast.14, f32[1,1280]{1,0:T(1,128)S(1)} %reshape.169.gain_q_ref, f32[1,1280]{1,0:T(1,128)S(1)} %reshape.170.gain_k_ref, ...), custom_call_target="tpu_custom_call" | custom-call | flops 1000000 | bytes 1000000 | tf_op jit(solution)/shard_map/pallas_call | solution.py:481
  55.4 3.3 %collective-permute-start.12 = (f32[256,1]{1,0:T(8,128)S(1)}, f32[256,1]{1,0:T(8,128)S(1)}, u32[]{:S(2)}, u32[]{:S(2)}) collective-permute-start(f32[256,1]{1,0:T(8,128)S(1)} %get-tuple-element.41.sums_ref), channel_id=1, source_target_pairs={{0,1},{1,0},{2,3},{3,2},{4,5},{5,4},{6,7},{7,6},{8,9},{9,8},{10,11... | collective-permute-start | bytes 3080 | tf_op jit(solution)/shard_map/ppermute | solution.py:497
  58.7 1.0 %collective-permute-done.12.peer_ref = f32[256,1]{1,0:T(8,128)S(1)} collective-permute-done((f32[256,1]{1,0:T(8,128)S(1)}, f32[256,1]{1,0:T(8,128)S(1)}, u32[]{:S(2)}, u32[]{:S(2)}) %collective-permute-start.12) | collective-permute-done | bytes 1056 | tf_op jit(solution)/shard_map/ppermute | solution.py:497
  59.7 1.0 %shard_map.98 = (bf16[128,1280]{1,0:T(8,128)(2,1)}, bf16[128,1280]{1,0:T(8,128)(2,1)}) custom-call(bf16[128,1280]{1,0:T(8,128)(2,1)S(1)} %bitcast.11, bf16[128,1280]{1,0:T(8,128)(2,1)S(1)} %bitcast.15, f32[128,1280]{1,0:T(8,128)S(1)} %get-tuple-element.38.gated_q_ref, f32[128,1280]{1,0:T(8,128)S(1)} %get-tuple-element.39.gated_k_ref, ...), custom_call_target="tpu_custom_call" | custom-call | flops 1000000 | bytes 1000000 | tf_op jit(solution)/shard_map/pallas_call | solution.py:498
  (7 shorter events, 0.0 us)
Async XLA Ops:
  0.6 1.0 %copy-start = (bf16[1,2,64,1280]{3,2,1,0:T(8,128)(2,1)S(1)}, bf16[1,2,64,1280]{3,2,1,0:T(8,128)(2,1)}, u32[]{:S(2)}) copy-start(bf16[1,2,64,1280]{3,2,1,0:T(8,128)(2,1)} %param.7) | copy-start | bytes 983044
  1.6 1.0 %copy-start.2 = (bf16[1,2,64,1280]{3,2,1,0:T(8,128)(2,1)S(1)}, bf16[1,2,64,1280]{3,2,1,0:T(8,128)(2,1)}, u32[]{:S(2)}) copy-start(bf16[1,2,64,1280]{3,2,1,0:T(8,128)(2,1)} %param.8) | copy-start | bytes 983044
  2.6 1.0 %copy-start.4 = (bf16[1,2,64,1280]{3,2,1,0:T(8,128)(2,1)S(1)}, bf16[1,2,64,1280]{3,2,1,0:T(8,128)(2,1)}, u32[]{:S(2)}) copy-start(bf16[1,2,64,1280]{3,2,1,0:T(8,128)(2,1)} %param.9) | copy-start | bytes 983044
  3.6 1.0 %copy-start.6 = (bf16[1,2,64,1280]{3,2,1,0:T(8,128)(2,1)S(1)}, bf16[1,2,64,1280]{3,2,1,0:T(8,128)(2,1)}, u32[]{:S(2)}) copy-start(bf16[1,2,64,1280]{3,2,1,0:T(8,128)(2,1)} %param.10) | copy-start | bytes 983044
  4.5 3.7 %copy-start.1 = (bf16[1,2,64,1280]{3,2,1,0:T(8,128)(2,1)S(1)}, bf16[1,2,64,1280]{3,2,1,0:T(8,128)(2,1)}, u32[]{:S(2)}) copy-start(bf16[1,2,64,1280]{3,2,1,0:T(8,128)(2,1)} %param.7) | copy-start | bytes 983044
  4.5 3.7 %copy-start.3 = (bf16[1,2,64,1280]{3,2,1,0:T(8,128)(2,1)S(1)}, bf16[1,2,64,1280]{3,2,1,0:T(8,128)(2,1)}, u32[]{:S(2)}) copy-start(bf16[1,2,64,1280]{3,2,1,0:T(8,128)(2,1)} %param.8) | copy-start | bytes 983044
  4.5 3.7 %copy-start.5 = (bf16[1,2,64,1280]{3,2,1,0:T(8,128)(2,1)S(1)}, bf16[1,2,64,1280]{3,2,1,0:T(8,128)(2,1)}, u32[]{:S(2)}) copy-start(bf16[1,2,64,1280]{3,2,1,0:T(8,128)(2,1)} %param.9) | copy-start | bytes 983044
  4.7 3.4 %collective-permute-start = (f32[256,1]{1,0:T(8,128)S(1)}, f32[256,1]{1,0:T(8,128)S(1)}, u32[]{:S(2)}, u32[]{:S(2)}) collective-permute-start(f32[256,1]{1,0:T(8,128)S(1)} %get-tuple-element.24.sums_ref), channel_id=1, source_target_pairs={{0,1},{1,0},{2,3},{3,2},{4,5},{5,4},{6,7},{7,6},{8,9},{9,8},{10,11... | collective-permute-start | bytes 3080 | tf_op jit(solution)/shard_map/ppermute | solution.py:421
  5.5 22.5 %collective-permute-start.2 = (bf16[256,640]{1,0:T(8,128)(2,1)S(1)}, bf16[256,640]{1,0:T(8,128)(2,1)S(1)}, u32[]{:S(2)}, u32[]{:S(2)}) collective-permute-start(bf16[256,640]{1,0:T(8,128)(2,1)S(1)} %get-tuple-element.27), channel_id=1, source_target_pairs={{0,16},{16,0},{1,17},{17,1},{2,18},{18,2},{3,19},{19,3},{4,20},{20... | collective-permute-start | bytes 983048 | tf_op jit(solution)/shard_map/ppermute | solution.py:420
  6.7 0.7 %copy-start.10 = (s32[2,16,4]{1,2,0:T(4,128)S(1)}, s32[2,16,4]{1,2,0:T(4,128)}, u32[]{:S(2)}) copy-start(s32[2,16,4]{1,2,0:T(4,128)} %param.13) | copy-start | bytes 1540
  7.4 0.7 %copy-start.8 = (f32[1280]{0:T(1024)S(1)}, f32[1280]{0:T(1024)}, u32[]{:S(2)}) copy-start(f32[1280]{0:T(1024)} %param.11) | copy-start | bytes 15364
  7.5 0.7 %copy-start.9 = (f32[1280]{0:T(1024)S(1)}, f32[1280]{0:T(1024)}, u32[]{:S(2)}) copy-start(f32[1280]{0:T(1024)} %param.12) | copy-start | bytes 15364
  9.1 18.9 %copy-start.7 = (bf16[1,2,64,1280]{3,2,1,0:T(8,128)(2,1)S(1)}, bf16[1,2,64,1280]{3,2,1,0:T(8,128)(2,1)}, u32[]{:S(2)}) copy-start(bf16[1,2,64,1280]{3,2,1,0:T(8,128)(2,1)} %param.10) | copy-start | bytes 983044
  9.1 11.1 %collective-permute-start.3 = (bf16[128,640]{1,0:T(8,128)(2,1)}, bf16[128,640]{1,0:T(8,128)(2,1)S(1)}, u32[]{:S(2)}, u32[]{:S(2)}) collective-permute-start(bf16[128,640]{1,0:T(8,128)(2,1)} %get-tuple-element.28), channel_id=1, source_target_pairs={{0,2},{2,4},{4,6},{6,8},{8,10},{10,12},{12,14},{1,3},{3,5},{5,7},{... | collective-permute-start | bytes 491528 | tf_op jit(solution)/shard_map/ppermute | solution.py:431
  12.7 15.3 %collective-permute-start.1 = (bf16[256,640]{1,0:T(8,128)(2,1)S(1)}, bf16[256,640]{1,0:T(8,128)(2,1)S(1)}, u32[]{:S(2)}, u32[]{:S(2)}) collective-permute-start(bf16[256,640]{1,0:T(8,128)(2,1)S(1)} %get-tuple-element.26), channel_id=1, source_target_pairs={{0,16},{16,0},{1,17},{17,1},{2,18},{18,2},{3,19},{19,3},{4,20},{20... | collective-permute-start | bytes 983048 | tf_op jit(solution)/shard_map/ppermute | solution.py:428
  13.0 9.5 %collective-permute-start.4 = (bf16[128,640]{1,0:T(8,128)(2,1)S(1)}, bf16[128,640]{1,0:T(8,128)(2,1)S(1)}, u32[]{:S(2)}, u32[]{:S(2)}) collective-permute-start(bf16[128,640]{1,0:T(8,128)(2,1)S(1)} %get-tuple-element.29), channel_id=1, source_target_pairs={{2,0},{4,2},{6,4},{8,6},{10,8},{12,10},{14,12},{3,1},{5,3},{7,5},{... | collective-permute-start | bytes 491528 | tf_op jit(solution)/shard_map/ppermute | solution.py:432
  15.1 9.7 %collective-permute-start.5 = (bf16[128,640]{1,0:T(8,128)(2,1)S(1)}, bf16[128,640]{1,0:T(8,128)(2,1)S(1)}, u32[]{:S(2)}, u32[]{:S(2)}) collective-permute-start(bf16[128,640]{1,0:T(8,128)(2,1)S(1)} %get-tuple-element.30), channel_id=1, source_target_pairs={{0,18},{2,20},{4,22},{6,24},{8,26},{10,28},{12,30},{16,2},{18,4},{... | collective-permute-start | bytes 491528 | tf_op jit(solution)/shard_map/ppermute | solution.py:429
  20.1 7.9 %collective-permute-start.6 = (bf16[128,640]{1,0:T(8,128)(2,1)S(1)}, bf16[128,640]{1,0:T(8,128)(2,1)S(1)}, u32[]{:S(2)}, u32[]{:S(2)}) collective-permute-start(bf16[128,640]{1,0:T(8,128)(2,1)S(1)} %get-tuple-element.31), channel_id=1, source_target_pairs={{2,16},{4,18},{6,20},{8,22},{10,24},{12,26},{14,28},{18,0},{20,2},... | collective-permute-start | bytes 491528 | tf_op jit(solution)/shard_map/ppermute | solution.py:430
  34.1 20.2 %collective-permute-start.7 = (bf16[384,640]{1,0:T(8,128)(2,1)S(1)}, bf16[384,640]{1,0:T(8,128)(2,1)S(1)}, u32[]{:S(2)}, u32[]{:S(2)}) collective-permute-start(bf16[384,640]{1,0:T(8,128)(2,1)S(1)} %get-tuple-element.33), channel_id=1, source_target_pairs={{0,16},{16,0},{1,17},{17,1},{2,18},{18,2},{3,19},{19,3},{4,20},{20... | collective-permute-start | bytes 1474568 | tf_op jit(solution)/shard_map/ppermute | solution.py:476
  34.5 13.9 %collective-permute-start.8 = (bf16[128,640]{1,0:T(8,128)(2,1)S(1)}, bf16[128,640]{1,0:T(8,128)(2,1)S(1)}, u32[]{:S(2)}, u32[]{:S(2)}) collective-permute-start(bf16[128,640]{1,0:T(8,128)(2,1)S(1)} %get-tuple-element.34), channel_id=1, source_target_pairs={{0,2},{2,4},{4,6},{6,8},{8,10},{10,12},{12,14},{1,3},{3,5},{5,7},{... | collective-permute-start | bytes 491528 | tf_op jit(solution)/shard_map/ppermute | solution.py:480
  40.2 8.1 %collective-permute-start.9 = (bf16[128,640]{1,0:T(8,128)(2,1)S(1)}, bf16[128,640]{1,0:T(8,128)(2,1)S(1)}, u32[]{:S(2)}, u32[]{:S(2)}) collective-permute-start(bf16[128,640]{1,0:T(8,128)(2,1)S(1)} %get-tuple-element.35), channel_id=1, source_target_pairs={{2,0},{4,2},{6,4},{8,6},{10,8},{12,10},{14,12},{3,1},{5,3},{7,5},{... | collective-permute-start | bytes 491528 | tf_op jit(solution)/shard_map/ppermute | solution.py:479
  42.2 9.5 %collective-permute-start.10 = (bf16[128,640]{1,0:T(8,128)(2,1)S(1)}, bf16[128,640]{1,0:T(8,128)(2,1)S(1)}, u32[]{:S(2)}, u32[]{:S(2)}) collective-permute-start(bf16[128,640]{1,0:T(8,128)(2,1)S(1)} %get-tuple-element.36), channel_id=1, source_target_pairs={{0,18},{2,20},{4,22},{6,24},{8,26},{10,28},{12,30},{16,2},{18,4},{... | collective-permute-start | bytes 491528 | tf_op jit(solution)/shard_map/ppermute | solution.py:478
  46.3 8.0 %collective-permute-start.11 = (bf16[128,640]{1,0:T(8,128)(2,1)S(1)}, bf16[128,640]{1,0:T(8,128)(2,1)S(1)}, u32[]{:S(2)}, u32[]{:S(2)}) collective-permute-start(bf16[128,640]{1,0:T(8,128)(2,1)S(1)} %get-tuple-element.37), channel_id=1, source_target_pairs={{2,16},{4,18},{6,20},{8,22},{10,24},{12,26},{14,28},{18,0},{20,2},... | collective-permute-start | bytes 491528 | tf_op jit(solution)/shard_map/ppermute | solution.py:477
  55.4 4.3 %collective-permute-start.12 = (f32[256,1]{1,0:T(8,128)S(1)}, f32[256,1]{1,0:T(8,128)S(1)}, u32[]{:S(2)}, u32[]{:S(2)}) collective-permute-start(f32[256,1]{1,0:T(8,128)S(1)} %get-tuple-element.41.sums_ref), channel_id=1, source_target_pairs={{0,1},{1,0},{2,3},{3,2},{4,5},{5,4},{6,7},{7,6},{8,9},{9,8},{10,11... | collective-permute-start | bytes 3080 | tf_op jit(solution)/shard_map/ppermute | solution.py:497

commit v2 on v0

--- a/solution.py
+++ b/solution.py
@@ -1,6 +1,10 @@
+import functools
+
 import jax
 import jax.numpy as jnp
 from jax import lax
+from jax.experimental import pallas as pl
+from jax.experimental.pallas import tpu as pltpu
 from jax.sharding import PartitionSpec as P
 
 TC = 16
@@ -156,9 +160,395 @@
     return (grad_q, grad_k, value_total.astype(jnp.bfloat16))
 
 
+SWAP = [(0, 1), (1, 0)]
+F32 = jnp.float32
+BF16 = jnp.bfloat16
+VMEM_LIMIT = 48 * 1024 * 1024
+
+
+def call(body, out_shape, flops=10**6, moved=10**6, **kw):
+    return pl.pallas_call(
+        body,
+        out_shape=out_shape,
+        compiler_params=pltpu.CompilerParams(vmem_limit_bytes=VMEM_LIMIT),
+        cost_estimate=pl.CostEstimate(flops=flops, bytes_accessed=moved, transcendentals=0),
+        **kw,
+    )
+
+
+def halves(half):
+    frame_at = lax.axis_index("frame")
+    mine = pl.multiple_of(frame_at * half, HD)
+    theirs = pl.multiple_of((1 - frame_at) * half, HD)
+    return (pl.ds(mine, half), pl.ds(theirs, half))
+
+
+def sides(width):
+    odd = lax.rem(lax.axis_index("row"), 2)
+    near = pl.multiple_of((1 - odd) * width, width)
+    far = pl.multiple_of(odd * width, width)
+    return (pl.ds(near, width), pl.ds(far, width))
+
+
+def load_kernel(q_in, k_in, v_in, t_in, q_ref, k_ref, v_ref, t_ref, sums_ref, v_out_ref, sems):
+    tokens, feat_dev = q_ref.shape
+    _, theirs = halves(feat_dev // 2)
+    pairs = ((v_in, v_ref), (q_in, q_ref), (k_in, k_ref), (t_in, t_ref))
+    copies = [pltpu.make_async_copy(a, b, sems.at[i]) for i, (a, b) in enumerate(pairs)]
+    for copy in copies:
+        copy.start()
+    copies[0].wait()
+    v_out_ref[...] = v_ref[:, theirs]
+    copies[1].wait()
+    q_float = q_ref[...].astype(F32)
+    sums_ref[:tokens] = jnp.sum(q_float * q_float, -1, keepdims=True)
+    copies[2].wait()
+    k_float = k_ref[...].astype(F32)
+    sums_ref[tokens:] = jnp.sum(k_float * k_float, -1, keepdims=True)
+    copies[3].wait()
+
+
+def norm_kernel(
+    width,
+    q_ref,
+    k_ref,
+    v_ref,
+    t_ref,
+    sums_ref,
+    peer_ref,
+    gain_q_ref,
+    gain_k_ref,
+    scale_ref,
+    own_ref,
+    k_out_ref,
+    qt_out_ref,
+    near_ref,
+    far_ref,
+):
+    tokens, feat_dev = q_ref.shape
+    features = HEADS * HD
+    mine, theirs = halves(feat_dev // 2)
+    near, far = sides(width)
+    scale = lax.rsqrt((sums_ref[...] + peer_ref[...]) / features + norm_eps)
+    scale_ref[...] = scale
+    scale_q, scale_k = (scale[:tokens], scale[tokens:])
+
+    def normed(ref, part, scales, gain_ref):
+        return (ref[:, part].astype(F32) * scales * gain_ref[:, part]).astype(BF16)
+
+    k_out_ref[...] = normed(k_ref, theirs, scale_k, gain_k_ref)
+    qt_out_ref[:tokens] = normed(q_ref, theirs, scale_q, gain_q_ref)
+    qt_out_ref[tokens:] = t_ref[:, theirs]
+    own_ref[:tokens] = normed(k_ref, mine, scale_k, gain_k_ref)
+    own_ref[tokens:] = normed(q_ref, mine, scale_q, gain_q_ref)
+    for out_ref, rows in ((near_ref, near), (far_ref, far)):
+        out_ref[:width] = own_ref[rows]
+        out_ref[width:] = v_ref[rows, mine]
+
+
+def relay_kernel(width, k_ref, v_ref, near_ref, far_ref):
+    for out_ref, rows in zip((near_ref, far_ref), sides(width)):
+        out_ref[:width] = k_ref[rows]
+        out_ref[width:] = v_ref[rows]
+
+
+def attend_kernel(
+    width,
+    near_ref,
+    far_ref,
+    swap_near_ref,
+    swap_far_ref,
+    own_ref,
+    v_ref,
+    t_ref,
+    swap_k_ref,
+    swap_v_ref,
+    swap_qt_ref,
+    bias_ref,
+    own_grad_ref,
+    swap_first_ref,
+    swap_last_ref,
+    near_grad_ref,
+    far_grad_ref,
+    swap_near_grad_ref,
+    swap_far_grad_ref,
+):
+    tokens, half = swap_k_ref.shape
+    score_scale = HD ** (-0.5)
+    mine = lax.axis_index("frame") * half
+    odd = lax.rem(lax.axis_index("row"), 2)
+    bias = bias_ref[...]
+    own_rows = slice(width, width + tokens)
+    side = tokens + 2 * width
+
+    def product(a, b, a_dim, b_dim):
+        return lax.dot_general(a, b, (((a_dim,), (b_dim,)), ((), ())), preferred_element_type=F32)
+
+    for head in range(half // HD):
+        at = slice(head * HD, (head + 1) * HD)
+        mine_at = pl.ds(pl.multiple_of(mine + head * HD, HD), HD)
+        query = jnp.concatenate([own_ref[tokens:, at], swap_qt_ref[:tokens, at]], 0)
+        target = jnp.concatenate([t_ref[:, mine_at], swap_qt_ref[tokens:, at]], 0)
+        key = jnp.concatenate(
+            [
+                near_ref[:width, at],
+                own_ref[:tokens, at],
+                far_ref[:width, at],
+                swap_near_ref[:width, at],
+                swap_k_ref[:, at],
+                swap_far_ref[:width, at],
+            ],
+            0,
+        )
+        value = jnp.concatenate(
+            [
+                near_ref[width:, at],
+                v_ref[:, mine_at],
+                far_ref[width:, at],
+                swap_near_ref[width:, at],
+                swap_v_ref[:, at],
+                swap_far_ref[width:, at],
+            ],
+            0,
+        )
+        scores = product(query, key, 1, 1) * score_scale + bias
+        row_max = jnp.max(scores, -1, keepdims=True)
+        expo = jnp.exp(scores - row_max)
+        probability = expo * (1.0 / jnp.sum(expo, -1, keepdims=True))
+        prob_b = probability.astype(BF16)
+        attended = product(prob_b, value, 1, 0)
+        d_out = (attended - target.astype(F32)).astype(BF16)
+        delta_sum = jnp.sum(d_out.astype(F32) * attended, -1, keepdims=True)
+        prob_grad = product(d_out, value, 1, 1)
+        score_grad = (probability * (prob_grad - delta_sum) * score_scale).astype(BF16)
+        dq = product(score_grad, key, 1, 0)
+        own_grad_ref[:tokens, at] = dq[:tokens]
+        swap_first_ref[:tokens, at] = dq[tokens:].astype(BF16)
+        dk = product(score_grad, query, 0, 0)
+        dv = product(prob_b, d_out, 0, 0)
+        for place, grad in ((0, dk), (1, dv)):
+            own_at = slice((1 + place) * tokens, (2 + place) * tokens)
+            own_grad_ref[own_at, at] = grad[own_rows]
+            to = slice(place * width, (place + 1) * width)
+            near_grad_ref[to, at] = grad[:width].astype(BF16)
+            far_grad_ref[to, at] = grad[width + tokens : side].astype(BF16)
+            other = grad[side:]
+            swap_near_grad_ref[to, at] = other[:width].astype(BF16)
+            swap_far_grad_ref[to, at] = other[width + tokens :].astype(BF16)
+            first, last = (other[width : 2 * width], other[2 * width : 3 * width])
+            first_to = slice(tokens + place * width, tokens + (place + 1) * width)
+            swap_first_ref[first_to, at] = jnp.where(odd == 0, last, first).astype(BF16)
+            swap_last_ref[to, at] = jnp.where(odd == 0, first, last)
+
+
+def add_kernel(a_ref, b_ref, out_ref):
+    out_ref[...] = (a_ref[...] + b_ref[...].astype(F32)).astype(BF16)
+
+
+def gather_kernel(
+    width,
+    q_ref,
+    k_ref,
+    gain_q_ref,
+    gain_k_ref,
+    own_ref,
+    near_ref,
+    far_ref,
+    swap_first_ref,
+    swap_last_ref,
+    swap_near_ref,
+    gated_q_ref,
+    gated_k_ref,
+    grad_v_ref,
+    sums_ref,
+    total_ref,
+):
+    tokens, feat_dev = q_ref.shape
+    mine, theirs = halves(feat_dev // 2)
+    near, far = sides(width)
+    k_at, v_at = (slice(0, width), slice(width, 2 * width))
+
+    def total(own_base, near_terms, far_terms):
+        for rows, terms in ((near, near_terms), (far, far_terms)):
+            value = sum(terms[1:], terms[0])
+            total_ref[rows] = value if own_base is None else value + own_base[rows]
+        return total_ref[...]
+
+    def term(ref, at):
+        return ref[at].astype(F32)
+
+    own_dk = total(own_ref.at[tokens : 2 * tokens], [term(near_ref, k_at)], [term(far_ref, k_at)])
+    gated_k_mine = gain_k_ref[:, mine] * own_dk
+    own_dv = total(own_ref.at[2 * tokens :], [term(near_ref, v_at)], [term(far_ref, v_at)])
+    grad_v_ref[:, mine] = own_dv.astype(BF16)
+    gated_q_mine = gain_q_ref[:, mine] * own_ref[:tokens]
+    first_k = term(swap_first_ref, slice(tokens, tokens + width))
+    first_v = term(swap_first_ref, slice(tokens + width, tokens + 2 * width))
+    swap_dk = total(
+        None, [first_k, term(swap_near_ref, k_at)], [term(swap_last_ref, k_at)]
+    )
+    gated_k_theirs = gain_k_ref[:, theirs] * swap_dk
+    swap_dv = total(
+        None, [first_v, term(swap_near_ref, v_at)], [term(swap_last_ref, v_at)]
+    )
+    grad_v_ref[:, theirs] = swap_dv.astype(BF16)
+    gated_q_theirs = gain_q_ref[:, theirs] * term(swap_first_ref, slice(0, tokens))
+    gated_q_ref[:, mine] = gated_q_mine
+    gated_q_ref[:, theirs] = gated_q_theirs
+    gated_k_ref[:, mine] = gated_k_mine
+    gated_k_ref[:, theirs] = gated_k_theirs
+    sums_ref[:tokens] = jnp.sum(q_ref[...].astype(F32) * gated_q_ref[...], -1, keepdims=True)
+    sums_ref[tokens:] = jnp.sum(k_ref[...].astype(F32) * gated_k_ref[...], -1, keepdims=True)
+
+
+def finish_kernel(
+    q_ref, k_ref, gated_q_ref, gated_k_ref, scale_ref, sums_ref, peer_ref, grad_q_ref, grad_k_ref
+):
+    tokens = q_ref.shape[0]
+    features = HEADS * HD
+    scale = scale_ref[...]
+    slope = scale * scale * scale * (sums_ref[...] + peer_ref[...]) / features
+    for rows, pre_ref, gated_ref, out_ref in (
+        (slice(0, tokens), q_ref, gated_q_ref, grad_q_ref),
+        (slice(tokens, 2 * tokens), k_ref, gated_k_ref, grad_k_ref),
+    ):
+        out_ref[...] = (
+            scale[rows] * gated_ref[...] - pre_ref[...].astype(F32) * slope[rows]
+        ).astype(BF16)
+
+
+def window_bias(kept, rows, width, tiles):
+    frame_at = lax.axis_index("frame")
+    row_at = lax.axis_index("row")
+    odd = lax.rem(row_at, 2)
+    kept_pad = jnp.pad(kept, ((0, 0), (1, 1), (0, 0)))
+    kept_win = lax.dynamic_slice_in_dim(kept_pad, row_at * rows, rows + 2, 1)
+    kept_win = jnp.where(frame_at == 0, kept_win, kept_win[::-1])
+    turned = jnp.concatenate([kept_win[:, 3:], kept_win[:, 1:3], kept_win[:, :1]], 1)
+    kept_win = jnp.where(odd == 0, turned, kept_win)
+    key_kept = jnp.repeat(kept_win.reshape(-1), width // tiles)
+    query_at = jnp.arange(2 * rows * width)
+    key_at = jnp.arange(2 * (rows + 2) * width)
+    query_row, query_tile = (query_at // width, query_at % width // TC)
+    key_slot, key_tile = (key_at // width, key_at % width // TC)
+    key_row = key_slot % (rows + 2) - 1
+    outer = (key_row < 0) | (key_row >= rows)
+    key_row = jnp.where(outer & (odd == 0), rows - 1 - key_row, key_row)
+    near_cols = jnp.abs(query_tile[:, None] - key_tile[None, :]) <= 1
+    near_rows = jnp.abs((query_row % rows)[:, None] - key_row[None, :]) <= 1
+    same_line = (query_row // rows * (rows + 2) + query_row % rows + 1)[:, None] == key_slot[None, :]
+    same = same_line & (query_tile[:, None] == key_tile[None, :])
+    allowed = near_cols & near_rows & ((key_kept > 0)[None, :] | same)
+    return jnp.where(allowed, 0.0, -1e30).astype(F32)
+
+
+def swapped_device(q_pre, k_pre, values, target, gain_q, gain_k, kept):
+    frames, rows, width, feat_dev = q_pre.shape
+    tokens = rows * width
+    half = feat_dev // 2
+    row_blocks = lax.axis_size("row")
+    inputs = [array.reshape(tokens, feat_dev) for array in (q_pre, k_pre, values, target)]
+    gain_q = gain_q.reshape(1, feat_dev)
+    gain_k = gain_k.reshape(1, feat_dev)
+    near_pairs = [(r, r + 1) for r in range(0, row_blocks - 1, 2)]
+    far_pairs = [(r, r + 1) for r in range(1, row_blocks - 1, 2)]
+    near, far = (pairs + [(b, a) for a, b in pairs] for pairs in (near_pairs, far_pairs))
+    swap_near = [
+        (f * row_blocks + a, (1 - f) * row_blocks + b) for f in range(2) for a, b in near
+    ]
+
+    def shape(first, last, dtype=BF16):
+        return jax.ShapeDtypeStruct((first, last), dtype)
+
+    block = shape(tokens, feat_dev)
+    sum_pair = shape(2 * tokens, 1, F32)
+    tokens_half = shape(tokens, half)
+    edge = shape(2 * width, half)
+
+    q_all, k_all, v_all, t_all, sums, v_out = call(
+        load_kernel,
+        (block,) * 4 + (sum_pair, tokens_half),
+        in_specs=[pl.BlockSpec(memory_space=pltpu.HBM)] * 4,
+        scratch_shapes=[pltpu.SemaphoreType.DMA((4,))],
+    )(*inputs)
+    swap_v = lax.ppermute(v_out, "frame", SWAP)
+    peer = lax.ppermute(sums, "head", SWAP)
+    scale, own_kq, k_out, qt_out, near_out, far_out = call(
+        functools.partial(norm_kernel, width),
+        (sum_pair, shape(2 * tokens, half), tokens_half, shape(2 * tokens, half), edge, edge),
+    )(q_all, k_all, v_all, t_all, sums, peer, gain_q, gain_k)
+    swap_k = lax.ppermute(k_out, "frame", SWAP)
+    near_in = lax.ppermute(near_out, "row", near)
+    far_in = lax.ppermute(far_out, "row", far)
+    swap_qt = lax.ppermute(qt_out, "frame", SWAP)
+    relay_near, relay_far = call(functools.partial(relay_kernel, width), (edge, edge))(
+        swap_k, swap_v
+    )
+    swap_near_in = lax.ppermute(relay_near, "row", near)
+    swap_far_in = lax.ppermute(relay_far, "row", far)
+    bias = window_bias(kept, rows, width, kept.shape[-1])
+    own_grad, first_out, last_terms, near_out, far_out, swap_near_out, swap_far_out = call(
+        functools.partial(attend_kernel, width),
+        (shape(3 * tokens, half, F32), shape(2 * tokens, half), shape(2 * width, half, F32))
+        + (edge,) * 4,
+        flops=10**9,
+        moved=4 * 10**6,
+    )(
+        near_in,
+        far_in,
+        swap_near_in,
+        swap_far_in,
+        own_kq,
+        v_all,
+        t_all,
+        swap_k,
+        swap_v,
+        swap_qt,
+        bias,
+    )
+    swap_first = lax.ppermute(first_out, "frame", SWAP)
+    far_terms = lax.ppermute(swap_far_out, "row", far)
+    last_out = call(add_kernel, edge)(last_terms, far_terms)
+    swap_near_total = lax.ppermute(swap_near_out, ("frame", "row"), swap_near)
+    far_total = lax.ppermute(far_out, "row", far)
+    near_total = lax.ppermute(near_out, "row", near)
+    swap_last = lax.ppermute(last_out, "frame", SWAP)
+    gated_q, gated_k, grad_v, sum_terms = call(
+        functools.partial(gather_kernel, width),
+        (shape(tokens, feat_dev, F32),) * 2 + (block, sum_pair),
+        scratch_shapes=[pltpu.VMEM((tokens, half), F32)],
+    )(
+        q_all,
+        k_all,
+        gain_q,
+        gain_k,
+        own_grad,
+        near_total,
+        far_total,
+        swap_first,
+        swap_last,
+        swap_near_total,
+    )
+    sum_peer = lax.ppermute(sum_terms, "head", SWAP)
+    grad_q, grad_k = call(finish_kernel, (block, block))(
+        q_all, k_all, gated_q, gated_k, scale, sum_terms, sum_peer
+    )
+    return tuple(
+        array.reshape(frames, rows, width, feat_dev) for array in (grad_q, grad_k, grad_v)
+    )
+
+
+def on_device(q_pre, *rest):
+    frames, rows, _, feat_dev = q_pre.shape
+    paired = lax.axis_size("frame") == 2 and frames == 1 and rows == 2
+    if paired and feat_dev % (2 * HD) == 0:
+        return swapped_device(q_pre, *rest)
+    return per_device(q_pre, *rest)
+
+
 def solution(mesh):
     return jax.shard_map(
-        per_device,
+        on_device,
         mesh=mesh,
         in_specs=(
             P("frame", "row", None, "head"),

time: 314 us -> 57.8 us (0.18)
  the two profiles are of different devices: /device:TPU:13 before, /device:TPU:0 now
where the time goes in v2:
time: 57.8 us; the launch traced here: 57.4 us
  starting transfers between devices  23.7 us (41%)
  waiting for transfers between devices  18.7 us (32%)
  Pallas kernels  7.95 us (14%)
  local copies, waits for them, and re-layouts  5.86 us (10%)
  between operations  0.75 us (1%)
    ppermute x1, waiting for transfers between devices, swapped_device(): swap_near_in = lax.ppermute(relay_near, 'row', near)  6.82 us
    ppermute x1, starting transfers between devices, swapped_device(): near_total = lax.ppermute(near_out, 'row', near)  5.74 us
    ppermute x1, waiting for transfers between devices, swapped_device(): near_total = lax.ppermute(near_out, 'row', near)  5.59 us
    ppermute x1, starting transfers between devices, swapped_device(): swap_near_total = lax.ppermute(swap_near_out, ('frame', 'row'), swap_near)  5.27 us
    unnamed x14, local copies, waits for them, and re-layouts  5.25 us
    pallas_call x1, Pallas kernels, swapped_device(): call(functools.partial(attend_kernel, width), (shape(3 * tokens, half, F3...  4.55 us
    ppermute x1, starting transfers between devices, swapped_device(): swap_v = lax.ppermute(v_out, 'frame', SWAP)  2.56 us
    ppermute x1, waiting for transfers between devices, swapped_device(): swap_k = lax.ppermute(k_out, 'frame', SWAP)  2.35 us
  transfers between devices with their start and end apart: 15, of which 7 were waited for; matrix products, arithmetic and copies ran while one was open for 2% of the time, Pallas kernels for 1%

profile of v2, /device:TPU:0, one launch (start us, length us, event | category | flops | bytes accessed | tf_op | source)
XLA Modules:
  0.0 57.4 jit_solution(4002299137288774703)
XLA Ops:
  0.6 0.0 copy-start
  0.6 1.0 %copy-done = bf16[1,2,64,1280]{3,2,1,0:T(8,128)(2,1)S(1)} copy-done((bf16[1,2,64,1280]{3,2,1,0:T(8,128)(2,1)S(1)}, bf16[1,2,64,1280]{3,2,1,0:T(8,128)(2,1)}, u32[]{:S(2)}) %copy-start) | copy-done | bytes 327704
  1.6 0.0 copy-start.1
  1.6 1.0 %copy-done.1 = bf16[1,2,64,1280]{3,2,1,0:T(8,128)(2,1)S(1)} copy-done((bf16[1,2,64,1280]{3,2,1,0:T(8,128)(2,1)S(1)}, bf16[1,2,64,1280]{3,2,1,0:T(8,128)(2,1)}, u32[]{:S(2)}) %copy-start.1) | copy-done | bytes 327704
  2.6 0.0 copy-start.2
  2.6 1.0 %copy-done.2 = bf16[1,2,64,1280]{3,2,1,0:T(8,128)(2,1)S(1)} copy-done((bf16[1,2,64,1280]{3,2,1,0:T(8,128)(2,1)S(1)}, bf16[1,2,64,1280]{3,2,1,0:T(8,128)(2,1)}, u32[]{:S(2)}) %copy-start.2) | copy-done | bytes 327704
  3.6 0.0 copy-start.3
  3.6 1.0 %copy-done.3 = bf16[1,2,64,1280]{3,2,1,0:T(8,128)(2,1)S(1)} copy-done((bf16[1,2,64,1280]{3,2,1,0:T(8,128)(2,1)S(1)}, bf16[1,2,64,1280]{3,2,1,0:T(8,128)(2,1)}, u32[]{:S(2)}) %copy-start.3) | copy-done | bytes 327704
  4.5 0.7 %shard_map.94 = (bf16[128,1280]{1,0:T(8,128)(2,1)S(1)}, bf16[128,1280]{1,0:T(8,128)(2,1)S(1)}, bf16[128,1280]{1,0:T(8,128)(2,1)S(1)}, bf16[128,1280]{1,0:T(8,128...) custom-call(bf16[128,1280]{1,0:T(8,128)(2,1)S(1)} %bitcast.7, bf16[128,1280]{1,0:T(8,128)(2,1)S(1)} %bitcast.8, ...), custom_call_target="tpu_custom_call" | custom-call | flops 1000000 | bytes 1000000 | tf_op jit(solution)/shard_map/pallas_call | solution.py:468
  5.3 0.5 collective-permute-start
  5.8 2.6 %collective-permute-start.4 = (bf16[128,640]{1,0:T(8,128)(2,1)S(1)}, bf16[128,640]{1,0:T(8,128)(2,1)S(1)}, u32[]{:S(2)}, u32[]{:S(2)}) collective-permute-start(bf16[128,640]{1,0:T(8,128)(2,1)S(1)} %get-tuple-element.38), channel_id=1, source_target_pairs={{0,16},{16,0},{1,17},{17,1},{2,18},{18,2},{3,19},{19,3},{4,20},{20... | collective-permute-start | bytes 491528 | tf_op jit(solution)/shard_map/ppermute | solution.py:474
  8.4 0.0 copy-start.6
  8.4 0.7 %copy-done.6 = s32[2,16,4]{1,2,0:T(4,128)S(1)} copy-done((s32[2,16,4]{1,2,0:T(4,128)S(1)}, s32[2,16,4]{1,2,0:T(4,128)}, u32[]{:S(2)}) %copy-start.6) | copy-done | bytes 536
  9.0 0.1 pad_dynamic-slice_fusion
  9.1 0.1 slice.13
  9.2 0.1 fusion.15
  9.3 0.0 copy-start.4
  9.3 0.1 fusion.3
  9.4 0.0 copy-start.5
  9.4 0.6 %copy-done.4 = f32[1280]{0:T(1024)S(1)} copy-done((f32[1280]{0:T(1024)S(1)}, f32[1280]{0:T(1024)}, u32[]{:S(2)}) %copy-start.4) | copy-done | bytes 5144
  10.0 0.1 copy-done.5
  10.1 0.0 collective-permute-done.peer_ref
  10.1 0.3 shard_map.95
  10.4 0.1 collective-permute-start.3
  10.4 0.1 copy.11
  10.6 0.1 gt.15
  10.7 0.1 broadcast_in_dim.8
  10.7 0.1 gt.16
  10.8 2.0 %collective-permute-start.7 = (bf16[256,640]{1,0:T(8,128)(2,1)S(1)}, bf16[256,640]{1,0:T(8,128)(2,1)S(1)}, u32[]{:S(2)}, u32[]{:S(2)}) collective-permute-start(bf16[256,640]{1,0:T(8,128)(2,1)S(1)} %get-tuple-element.42), channel_id=1, source_target_pairs={{0,16},{16,0},{1,17},{17,1},{2,18},{18,2},{3,19},{19,3},{4,20},{20... | collective-permute-start | bytes 983048 | tf_op jit(solution)/shard_map/ppermute | solution.py:483
  12.9 1.6 %collective-permute-start.1 = (bf16[128,640]{1,0:T(8,128)(2,1)S(1)}, bf16[128,640]{1,0:T(8,128)(2,1)S(1)}, u32[]{:S(2)}, u32[]{:S(2)}) collective-permute-start(bf16[128,640]{1,0:T(8,128)(2,1)S(1)} %get-tuple-element.35), channel_id=1, source_target_pairs={{0,2},{4,6},{8,10},{12,14},{2,0},{6,4},{10,8},{14,12},{1,3},{5,7},... | collective-permute-start | bytes 491528 | tf_op jit(solution)/shard_map/ppermute | solution.py:481
  14.4 0.7 %collective-permute-start.2 = (bf16[128,640]{1,0:T(8,128)(2,1)S(1)}, bf16[128,640]{1,0:T(8,128)(2,1)S(1)}, u32[]{:S(2)}, u32[]{:S(2)}) collective-permute-start(bf16[128,640]{1,0:T(8,128)(2,1)S(1)} %get-tuple-element.36), channel_id=1, source_target_pairs={{2,4},{6,8},{10,12},{4,2},{8,6},{12,10},{3,5},{7,9},{11,13},{5,3},... | collective-permute-start | bytes 491528 | tf_op jit(solution)/shard_map/ppermute | solution.py:482
  15.1 0.0 collective-permute-done.4.v_ref.swap_v_ref
  15.1 2.4 %collective-permute-done.3.k_ref.swap_k_ref = bf16[128,640]{1,0:T(8,128)(2,1)S(1)} collective-permute-done((bf16[128,640]{1,0:T(8,128)(2,1)S(1)}, bf16[128,640]{1,0:T(8,128)(2,1)S(1)}, u32[]{:S(2)}, u32[]{:S(2)}) %collective-permute-start.3) | collective-permute-done | bytes 163872 | tf_op jit(solution)/shard_map/ppermute | solution.py:480
  17.5 2.0 %collective-permute-start.5 = (bf16[128,640]{1,0:T(8,128)(2,1)S(1)}, bf16[128,640]{1,0:T(8,128)(2,1)S(1)}, u32[]{:S(2)}, u32[]{:S(2)}) collective-permute-start(bf16[128,640]{1,0:T(8,128)(2,1)S(1)} %get-tuple-element.39), channel_id=1, source_target_pairs={{0,2},{4,6},{8,10},{12,14},{2,0},{6,4},{10,8},{14,12},{1,3},{5,7},... | collective-permute-start | bytes 491528 | tf_op jit(solution)/shard_map/ppermute | solution.py:487
  19.5 0.7 %collective-permute-start.6 = (bf16[128,640]{1,0:T(8,128)(2,1)S(1)}, bf16[128,640]{1,0:T(8,128)(2,1)S(1)}, u32[]{:S(2)}, u32[]{:S(2)}) collective-permute-start(bf16[128,640]{1,0:T(8,128)(2,1)S(1)} %get-tuple-element.40), channel_id=1, source_target_pairs={{2,4},{6,8},{10,12},{4,2},{8,6},{12,10},{3,5},{7,9},{11,13},{5,3},... | collective-permute-start | bytes 491528 | tf_op jit(solution)/shard_map/ppermute | solution.py:488
  20.2 0.4 fusion.2.bias_ref
  20.6 0.8 %collective-permute-done.1.near_ref = bf16[128,640]{1,0:T(8,128)(2,1)S(1)} collective-permute-done((bf16[128,640]{1,0:T(8,128)(2,1)S(1)}, bf16[128,640]{1,0:T(8,128)(2,1)S(1)}, u32[]{:S(2)}, u32[]{:S(2)}) %collective-permute-start.1) | collective-permute-done | bytes 163872 | tf_op jit(solution)/shard_map/ppermute | solution.py:481
  21.4 0.0 collective-permute-done.2.far_ref
  21.4 6.8 %collective-permute-done.5.swap_near_ref = bf16[128,640]{1,0:T(8,128)(2,1)S(1)} collective-permute-done((bf16[128,640]{1,0:T(8,128)(2,1)S(1)}, bf16[128,640]{1,0:T(8,128)(2,1)S(1)}, u32[]{:S(2)}, u32[]{:S(2)}) %collective-permute-start.5) | collective-permute-done | bytes 163872 | tf_op jit(solution)/shard_map/ppermute | solution.py:487
  28.2 0.0 collective-permute-done.6.swap_far_ref
  28.2 0.0 collective-permute-done.7.swap_qt_ref
  28.2 4.6 %shard_map.97 = (f32[384,640]{1,0:T(8,128)S(1)}, bf16[256,640]{1,0:T(8,128)(2,1)S(1)}, f32[128,640]{1,0:T(8,128)S(1)}, bf16[128,640]{1,0:T(8,128)(2,1)S(1)}, bf1...) custom-call(bf16[128,640]{1,0:T(8,128)(2,1)S(1)} %collective-permute-done.1.near_ref, ...), custom_call_target="tpu_custom_call" | custom-call | flops 1000000000 | bytes 4000000 | tf_op jit(solution)/shard_map/pallas_call | solution.py:490
  32.8 0.7 %collective-permute-start.11 = (bf16[128,640]{1,0:T(8,128)(2,1)S(1)}, bf16[128,640]{1,0:T(8,128)(2,1)S(1)}, u32[]{:S(2)}, u32[]{:S(2)}) collective-permute-start(bf16[128,640]{1,0:T(8,128)(2,1)S(1)} %get-tuple-element.48), channel_id=1, source_target_pairs={{2,4},{6,8},{10,12},{4,2},{8,6},{12,10},{3,5},{7,9},{11,13},{5,3},... | collective-permute-start | bytes 491528 | tf_op jit(solution)/shard_map/ppermute | solution.py:510
  33.4 0.6 %collective-permute-start.10 = (bf16[256,640]{1,0:T(8,128)(2,1)S(1)}, bf16[256,640]{1,0:T(8,128)(2,1)S(1)}, u32[]{:S(2)}, u32[]{:S(2)}) collective-permute-start(bf16[256,640]{1,0:T(8,128)(2,1)S(1)} %get-tuple-element.46), channel_id=1, source_target_pairs={{0,16},{16,0},{1,17},{17,1},{2,18},{18,2},{3,19},{19,3},{4,20},{20... | collective-permute-start | bytes 983048 | tf_op jit(solution)/shard_map/ppermute | solution.py:509
  34.0 5.7 %collective-permute-start.8 = (bf16[128,640]{1,0:T(8,128)(2,1)S(1)}, bf16[128,640]{1,0:T(8,128)(2,1)S(1)}, u32[]{:S(2)}, u32[]{:S(2)}) collective-permute-start(bf16[128,640]{1,0:T(8,128)(2,1)S(1)} %get-tuple-element.44), channel_id=1, source_target_pairs={{0,2},{4,6},{8,10},{12,14},{2,0},{6,4},{10,8},{14,12},{1,3},{5,7},... | collective-permute-start | bytes 491528 | tf_op jit(solution)/shard_map/ppermute | solution.py:514
  39.8 0.7 %collective-permute-start.9 = (bf16[128,640]{1,0:T(8,128)(2,1)S(1)}, bf16[128,640]{1,0:T(8,128)(2,1)S(1)}, u32[]{:S(2)}, u32[]{:S(2)}) collective-permute-start(bf16[128,640]{1,0:T(8,128)(2,1)S(1)} %get-tuple-element.45), channel_id=1, source_target_pairs={{2,4},{6,8},{10,12},{4,2},{8,6},{12,10},{3,5},{7,9},{11,13},{5,3},... | collective-permute-start | bytes 491528 | tf_op jit(solution)/shard_map/ppermute | solution.py:513
  40.5 5.3 %collective-permute-start.13 = (bf16[128,640]{1,0:T(8,128)(2,1)S(1)}, bf16[128,640]{1,0:T(8,128)(2,1)S(1)}, u32[]{:S(2)}, u32[]{:S(2)}) collective-permute-start(bf16[128,640]{1,0:T(8,128)(2,1)S(1)} %get-tuple-element.49), channel_id=1, source_target_pairs={{0,18},{4,22},{8,26},{12,30},{2,16},{6,20},{10,24},{14,28},{16,2},... | collective-permute-start | bytes 491528 | tf_op jit(solution)/shard_map/ppermute | solution.py:512
  45.7 0.0 collective-permute-done.11.b_ref
  45.8 0.6 %collective-permute-start.12 = (bf16[128,640]{1,0:T(8,128)(2,1)S(1)}, bf16[128,640]{1,0:T(8,128)(2,1)S(1)}, u32[]{:S(2)}, u32[]{:S(2)}) collective-permute-start(bf16[128,640]{1,0:T(8,128)(2,1)S(1)} %shard_map.98), channel_id=1, source_target_pairs={{0,16},{16,0},{1,17},{17,1},{2,18},{18,2},{3,19},{19,3},{4,20},{20... | collective-permute-start | bytes 491528 | tf_op jit(solution)/shard_map/ppermute | solution.py:515
  46.4 5.6 %collective-permute-done.8.near_ref = bf16[128,640]{1,0:T(8,128)(2,1)S(1)} collective-permute-done((bf16[128,640]{1,0:T(8,128)(2,1)S(1)}, bf16[128,640]{1,0:T(8,128)(2,1)S(1)}, u32[]{:S(2)}, u32[]{:S(2)}) %collective-permute-start.8) | collective-permute-done | bytes 163872 | tf_op jit(solution)/shard_map/ppermute | solution.py:514
  52.0 0.0 collective-permute-done.9.far_ref
  52.0 0.8 %collective-permute-done.13.swap_near_ref = bf16[128,640]{1,0:T(8,128)(2,1)S(1)} collective-permute-done((bf16[128,640]{1,0:T(8,128)(2,1)S(1)}, bf16[128,640]{1,0:T(8,128)(2,1)S(1)}, u32[]{:S(2)}, u32[]{:S(2)}) %collective-permute-start.13) | collective-permute-done | bytes 163872 | tf_op jit(solution)/shard_map/ppermute | solution.py:512
  52.8 0.9 %collective-permute-done.12.swap_last_ref = bf16[128,640]{1,0:T(8,128)(2,1)S(1)} collective-permute-done((bf16[128,640]{1,0:T(8,128)(2,1)S(1)}, bf16[128,640]{1,0:T(8,128)(2,1)S(1)}, u32[]{:S(2)}, u32[]{:S(2)}) %collective-permute-start.12) | collective-permute-done | bytes 163872 | tf_op jit(solution)/shard_map/ppermute | solution.py:515
  53.7 0.0 collective-permute-done.10.swap_first_ref
  53.7 1.3 %shard_map.99 = (f32[128,1280]{1,0:T(8,128)S(1)}, f32[128,1280]{1,0:T(8,128)S(1)}, bf16[128,1280]{1,0:T(8,128)(2,1)}, f32[256,1]{1,0:T(8,128)S(1)}) custom-call(bf16[128,1280]{1,0:T(8,128)(2,1)S(1)} %get-tuple-element.30.q_ref, bf16[128,1280]{1,0:T(8,128)(2,1)S(1)} %get-tuple-element.31.k_ref, f32[1,1280]{1,0:T(1,128)S(1)} %reshape.173.gain_q_ref, ...), custom_call_target="tpu_custom_call" | custom-call | flops 1000000 | bytes 1000000 | tf_op jit(solution)/shard_map/pallas_call | solution.py:516
  55.0 0.0 collective-permute-start.14
  55.0 1.3 %collective-permute-done.14.peer_ref = f32[256,1]{1,0:T(8,128)S(1)} collective-permute-done((f32[256,1]{1,0:T(8,128)S(1)}, f32[256,1]{1,0:T(8,128)S(1)}, u32[]{:S(2)}, u32[]{:S(2)}) %collective-permute-start.14) | collective-permute-done | bytes 1056 | tf_op jit(solution)/shard_map/ppermute | solution.py:532
  56.4 1.0 %shard_map.100 = (bf16[128,1280]{1,0:T(8,128)(2,1)}, bf16[128,1280]{1,0:T(8,128)(2,1)}) custom-call(bf16[128,1280]{1,0:T(8,128)(2,1)S(1)} %get-tuple-element.30.q_ref, bf16[128,1280]{1,0:T(8,128)(2,1)S(1)} %get-tuple-element.31.k_ref, f32[128,1280]{1,0:T(8,128)S(1)} %get-tuple-element.50.gated_q_ref, f32[128,1280]{1,0:T(8,128)S(1)} %get-tuple-element.51.gated_k_ref, ...), custom_call_target="tpu_custom_call" | custom-call | flops 1000000 | bytes 1000000 | tf_op jit(solution)/shard_map/pallas_call | solution.py:533
  (9 shorter events, 0.1 us)
Async XLA Ops:
  0.6 1.0 %copy-start = (bf16[1,2,64,1280]{3,2,1,0:T(8,128)(2,1)S(1)}, bf16[1,2,64,1280]{3,2,1,0:T(8,128)(2,1)}, u32[]{:S(2)}) copy-start(bf16[1,2,64,1280]{3,2,1,0:T(8,128)(2,1)} %param.7) | copy-start | bytes 983044
  1.6 1.0 %copy-start.1 = (bf16[1,2,64,1280]{3,2,1,0:T(8,128)(2,1)S(1)}, bf16[1,2,64,1280]{3,2,1,0:T(8,128)(2,1)}, u32[]{:S(2)}) copy-start(bf16[1,2,64,1280]{3,2,1,0:T(8,128)(2,1)} %param.8) | copy-start | bytes 983044
  2.6 1.0 %copy-start.2 = (bf16[1,2,64,1280]{3,2,1,0:T(8,128)(2,1)S(1)}, bf16[1,2,64,1280]{3,2,1,0:T(8,128)(2,1)}, u32[]{:S(2)}) copy-start(bf16[1,2,64,1280]{3,2,1,0:T(8,128)(2,1)} %param.9) | copy-start | bytes 983044
  3.6 1.0 %copy-start.3 = (bf16[1,2,64,1280]{3,2,1,0:T(8,128)(2,1)S(1)}, bf16[1,2,64,1280]{3,2,1,0:T(8,128)(2,1)}, u32[]{:S(2)}) copy-start(bf16[1,2,64,1280]{3,2,1,0:T(8,128)(2,1)} %param.10) | copy-start | bytes 983044
  5.3 4.8 %collective-permute-start = (f32[256,1]{1,0:T(8,128)S(1)}, f32[256,1]{1,0:T(8,128)S(1)}, u32[]{:S(2)}, u32[]{:S(2)}) collective-permute-start(f32[256,1]{1,0:T(8,128)S(1)} %get-tuple-element.34.sums_ref), channel_id=1, source_target_pairs={{0,1},{1,0},{2,3},{3,2},{4,5},{5,4},{6,7},{7,6},{8,9},{9,8},{10,11... | collective-permute-start | bytes 3080 | tf_op jit(solution)/shard_map/ppermute | solution.py:475
  5.8 9.3 %collective-permute-start.4 = (bf16[128,640]{1,0:T(8,128)(2,1)S(1)}, bf16[128,640]{1,0:T(8,128)(2,1)S(1)}, u32[]{:S(2)}, u32[]{:S(2)}) collective-permute-start(bf16[128,640]{1,0:T(8,128)(2,1)S(1)} %get-tuple-element.38), channel_id=1, source_target_pairs={{0,16},{16,0},{1,17},{17,1},{2,18},{18,2},{3,19},{19,3},{4,20},{20... | collective-permute-start | bytes 491528 | tf_op jit(solution)/shard_map/ppermute | solution.py:474
  8.4 0.7 %copy-start.6 = (s32[2,16,4]{1,2,0:T(4,128)S(1)}, s32[2,16,4]{1,2,0:T(4,128)}, u32[]{:S(2)}) copy-start(s32[2,16,4]{1,2,0:T(4,128)} %param.13) | copy-start | bytes 1540
  9.3 0.7 %copy-start.4 = (f32[1280]{0:T(1024)S(1)}, f32[1280]{0:T(1024)}, u32[]{:S(2)}) copy-start(f32[1280]{0:T(1024)} %param.11) | copy-start | bytes 15364
  9.4 0.7 %copy-start.5 = (f32[1280]{0:T(1024)S(1)}, f32[1280]{0:T(1024)}, u32[]{:S(2)}) copy-start(f32[1280]{0:T(1024)} %param.12) | copy-start | bytes 15364
  10.4 7.1 %collective-permute-start.3 = (bf16[128,640]{1,0:T(8,128)(2,1)S(1)}, bf16[128,640]{1,0:T(8,128)(2,1)S(1)}, u32[]{:S(2)}, u32[]{:S(2)}) collective-permute-start(bf16[128,640]{1,0:T(8,128)(2,1)S(1)} %get-tuple-element.37), channel_id=1, source_target_pairs={{0,16},{16,0},{1,17},{17,1},{2,18},{18,2},{3,19},{19,3},{4,20},{20... | collective-permute-start | bytes 491528 | tf_op jit(solution)/shard_map/ppermute | solution.py:480
  10.8 17.4 %collective-permute-start.7 = (bf16[256,640]{1,0:T(8,128)(2,1)S(1)}, bf16[256,640]{1,0:T(8,128)(2,1)S(1)}, u32[]{:S(2)}, u32[]{:S(2)}) collective-permute-start(bf16[256,640]{1,0:T(8,128)(2,1)S(1)} %get-tuple-element.42), channel_id=1, source_target_pairs={{0,16},{16,0},{1,17},{17,1},{2,18},{18,2},{3,19},{19,3},{4,20},{20... | collective-permute-start | bytes 983048 | tf_op jit(solution)/shard_map/ppermute | solution.py:483
  12.9 8.5 %collective-permute-start.1 = (bf16[128,640]{1,0:T(8,128)(2,1)S(1)}, bf16[128,640]{1,0:T(8,128)(2,1)S(1)}, u32[]{:S(2)}, u32[]{:S(2)}) collective-permute-start(bf16[128,640]{1,0:T(8,128)(2,1)S(1)} %get-tuple-element.35), channel_id=1, source_target_pairs={{0,2},{4,6},{8,10},{12,14},{2,0},{6,4},{10,8},{14,12},{1,3},{5,7},... | collective-permute-start | bytes 491528 | tf_op jit(solution)/shard_map/ppermute | solution.py:481
  14.4 6.9 %collective-permute-start.2 = (bf16[128,640]{1,0:T(8,128)(2,1)S(1)}, bf16[128,640]{1,0:T(8,128)(2,1)S(1)}, u32[]{:S(2)}, u32[]{:S(2)}) collective-permute-start(bf16[128,640]{1,0:T(8,128)(2,1)S(1)} %get-tuple-element.36), channel_id=1, source_target_pairs={{2,4},{6,8},{10,12},{4,2},{8,6},{12,10},{3,5},{7,9},{11,13},{5,3},... | collective-permute-start | bytes 491528 | tf_op jit(solution)/shard_map/ppermute | solution.py:482
  17.5 10.7 %collective-permute-start.5 = (bf16[128,640]{1,0:T(8,128)(2,1)S(1)}, bf16[128,640]{1,0:T(8,128)(2,1)S(1)}, u32[]{:S(2)}, u32[]{:S(2)}) collective-permute-start(bf16[128,640]{1,0:T(8,128)(2,1)S(1)} %get-tuple-element.39), channel_id=1, source_target_pairs={{0,2},{4,6},{8,10},{12,14},{2,0},{6,4},{10,8},{14,12},{1,3},{5,7},... | collective-permute-start | bytes 491528 | tf_op jit(solution)/shard_map/ppermute | solution.py:487
  19.5 8.7 %collective-permute-start.6 = (bf16[128,640]{1,0:T(8,128)(2,1)S(1)}, bf16[128,640]{1,0:T(8,128)(2,1)S(1)}, u32[]{:S(2)}, u32[]{:S(2)}) collective-permute-start(bf16[128,640]{1,0:T(8,128)(2,1)S(1)} %get-tuple-element.40), channel_id=1, source_target_pairs={{2,4},{6,8},{10,12},{4,2},{8,6},{12,10},{3,5},{7,9},{11,13},{5,3},... | collective-permute-start | bytes 491528 | tf_op jit(solution)/shard_map/ppermute | solution.py:488
  32.8 13.0 %collective-permute-start.11 = (bf16[128,640]{1,0:T(8,128)(2,1)S(1)}, bf16[128,640]{1,0:T(8,128)(2,1)S(1)}, u32[]{:S(2)}, u32[]{:S(2)}) collective-permute-start(bf16[128,640]{1,0:T(8,128)(2,1)S(1)} %get-tuple-element.48), channel_id=1, source_target_pairs={{2,4},{6,8},{10,12},{4,2},{8,6},{12,10},{3,5},{7,9},{11,13},{5,3},... | collective-permute-start | bytes 491528 | tf_op jit(solution)/shard_map/ppermute | solution.py:510
  33.4 20.3 %collective-permute-start.10 = (bf16[256,640]{1,0:T(8,128)(2,1)S(1)}, bf16[256,640]{1,0:T(8,128)(2,1)S(1)}, u32[]{:S(2)}, u32[]{:S(2)}) collective-permute-start(bf16[256,640]{1,0:T(8,128)(2,1)S(1)} %get-tuple-element.46), channel_id=1, source_target_pairs={{0,16},{16,0},{1,17},{17,1},{2,18},{18,2},{3,19},{19,3},{4,20},{20... | collective-permute-start | bytes 983048 | tf_op jit(solution)/shard_map/ppermute | solution.py:509
  34.0 17.9 %collective-permute-start.8 = (bf16[128,640]{1,0:T(8,128)(2,1)S(1)}, bf16[128,640]{1,0:T(8,128)(2,1)S(1)}, u32[]{:S(2)}, u32[]{:S(2)}) collective-permute-start(bf16[128,640]{1,0:T(8,128)(2,1)S(1)} %get-tuple-element.44), channel_id=1, source_target_pairs={{0,2},{4,6},{8,10},{12,14},{2,0},{6,4},{10,8},{14,12},{1,3},{5,7},... | collective-permute-start | bytes 491528 | tf_op jit(solution)/shard_map/ppermute | solution.py:514
  39.8 12.2 %collective-permute-start.9 = (bf16[128,640]{1,0:T(8,128)(2,1)S(1)}, bf16[128,640]{1,0:T(8,128)(2,1)S(1)}, u32[]{:S(2)}, u32[]{:S(2)}) collective-permute-start(bf16[128,640]{1,0:T(8,128)(2,1)S(1)} %get-tuple-element.45), channel_id=1, source_target_pairs={{2,4},{6,8},{10,12},{4,2},{8,6},{12,10},{3,5},{7,9},{11,13},{5,3},... | collective-permute-start | bytes 491528 | tf_op jit(solution)/shard_map/ppermute | solution.py:513
  40.5 12.3 %collective-permute-start.13 = (bf16[128,640]{1,0:T(8,128)(2,1)S(1)}, bf16[128,640]{1,0:T(8,128)(2,1)S(1)}, u32[]{:S(2)}, u32[]{:S(2)}) collective-permute-start(bf16[128,640]{1,0:T(8,128)(2,1)S(1)} %get-tuple-element.49), channel_id=1, source_target_pairs={{0,18},{4,22},{8,26},{12,30},{2,16},{6,20},{10,24},{14,28},{16,2},... | collective-permute-start | bytes 491528 | tf_op jit(solution)/shard_map/ppermute | solution.py:512
  45.8 8.0 %collective-permute-start.12 = (bf16[128,640]{1,0:T(8,128)(2,1)S(1)}, bf16[128,640]{1,0:T(8,128)(2,1)S(1)}, u32[]{:S(2)}, u32[]{:S(2)}) collective-permute-start(bf16[128,640]{1,0:T(8,128)(2,1)S(1)} %shard_map.98), channel_id=1, source_target_pairs={{0,16},{16,0},{1,17},{17,1},{2,18},{18,2},{3,19},{19,3},{4,20},{20... | collective-permute-start | bytes 491528 | tf_op jit(solution)/shard_map/ppermute | solution.py:515
  55.0 1.3 %collective-permute-start.14 = (f32[256,1]{1,0:T(8,128)S(1)}, f32[256,1]{1,0:T(8,128)S(1)}, u32[]{:S(2)}, u32[]{:S(2)}) collective-permute-start(f32[256,1]{1,0:T(8,128)S(1)} %get-tuple-element.53.sums_ref), channel_id=1, source_target_pairs={{0,1},{1,0},{2,3},{3,2},{4,5},{5,4},{6,7},{7,6},{8,9},{9,8},{10,11... | collective-permute-start | bytes 3080 | tf_op jit(solution)/shard_map/ppermute | solution.py:532

commit v3 on v2

--- a/solution.py
+++ b/solution.py
@@ -190,22 +190,46 @@
     return (pl.ds(near, width), pl.ds(far, width))
 
 
-def load_kernel(q_in, k_in, v_in, t_in, q_ref, k_ref, v_ref, t_ref, sums_ref, v_out_ref, sems):
+def load_kernel(
+    q_in,
+    k_in,
+    v_in,
+    t_in,
+    gain_q_in,
+    gain_k_in,
+    q_ref,
+    k_ref,
+    v_ref,
+    t_ref,
+    gain_q_ref,
+    gain_k_ref,
+    sums_ref,
+    v_out_ref,
+    sems,
+):
     tokens, feat_dev = q_ref.shape
     _, theirs = halves(feat_dev // 2)
-    pairs = ((v_in, v_ref), (q_in, q_ref), (k_in, k_ref), (t_in, t_ref))
+    pairs = (
+        (q_in, q_ref),
+        (k_in, k_ref),
+        (v_in, v_ref),
+        (t_in, t_ref),
+        (gain_q_in, gain_q_ref.at[0]),
+        (gain_k_in, gain_k_ref.at[0]),
+    )
     copies = [pltpu.make_async_copy(a, b, sems.at[i]) for i, (a, b) in enumerate(pairs)]
     for copy in copies:
         copy.start()
     copies[0].wait()
-    v_out_ref[...] = v_ref[:, theirs]
-    copies[1].wait()
     q_float = q_ref[...].astype(F32)
     sums_ref[:tokens] = jnp.sum(q_float * q_float, -1, keepdims=True)
-    copies[2].wait()
+    copies[1].wait()
     k_float = k_ref[...].astype(F32)
     sums_ref[tokens:] = jnp.sum(k_float * k_float, -1, keepdims=True)
-    copies[3].wait()
+    copies[2].wait()
+    v_out_ref[...] = v_ref[:, theirs]
+    for copy in copies[3:]:
+        copy.wait()
 
 
 def norm_kernel(
@@ -246,40 +270,54 @@
         out_ref[width:] = v_ref[rows, mine]
 
 
-def relay_kernel(width, k_ref, v_ref, near_ref, far_ref):
+def relay_kernel(width, k_ref, v_ref, earlier_ref, near_ref, far_ref):
     for out_ref, rows in zip((near_ref, far_ref), sides(width)):
         out_ref[:width] = k_ref[rows]
         out_ref[width:] = v_ref[rows]
 
 
-def attend_kernel(
-    width,
-    near_ref,
-    far_ref,
-    swap_near_ref,
-    swap_far_ref,
-    own_ref,
-    v_ref,
-    t_ref,
-    swap_k_ref,
-    swap_v_ref,
-    swap_qt_ref,
-    bias_ref,
-    own_grad_ref,
-    swap_first_ref,
-    swap_last_ref,
-    near_grad_ref,
-    far_grad_ref,
-    swap_near_grad_ref,
-    swap_far_grad_ref,
-):
+def mask_kernel(width, kept_ref, near_ref, far_ref):
+    rows = 2
+    count = kept_ref.shape[2]
+    tiles = width // TC
+    frame_at = lax.axis_index("frame")
+    first_row = lax.axis_index("row") * rows
+    odd = lax.rem(lax.axis_index("row"), 2)
+    shape = near_ref.shape
+    key_at = lax.broadcasted_iota(jnp.int32, shape, 1)
+    query_at = lax.broadcasted_iota(jnp.int32, shape, 0)
+    key_tile = lax.rem(key_at, width) // TC
+    query_tile = lax.rem(query_at, width) // TC
+    near_cols = jnp.abs(query_tile - key_tile) <= 1
+    same = (query_tile == key_tile) & (key_at // width == 3 * (query_at // width) + 1)
+    lane = lax.broadcasted_iota(jnp.int32, (1, shape[1]), 1) // TC
+    for out_ref, row in ((near_ref, 1 - odd), (far_ref, odd)):
+        places = (3 * row - 1, row, 1 - row)
+        key_kept = jnp.zeros((1, shape[1]), jnp.int32)
+        for part in range(2):
+            frame = frame_at if part == 0 else 1 - frame_at
+            for slot, place in enumerate(places):
+                at = first_row + place
+                inside = (at >= 0) & (at < count)
+                at = jnp.clip(at, 0, count - 1)
+                for tile in range(tiles):
+                    value = jnp.where(inside, kept_ref[frame, tile, at], 0)
+                    here = (part * 3 + slot) * tiles + tile
+                    key_kept = jnp.where(lane == here, value, key_kept)
+        allowed = near_cols & (same | (key_kept > 0))
+        out_ref[...] = jnp.where(allowed, 0.0, -1e30)
+
+
+def attend(width, row, halo_ref, swap_halo_ref, own_ref, v_ref, t_ref, swap_k_ref, swap_v_ref,
+           swap_qt_ref, bias_ref, store):
     tokens, half = swap_k_ref.shape
     score_scale = HD ** (-0.5)
     mine = lax.axis_index("frame") * half
-    odd = lax.rem(lax.axis_index("row"), 2)
     bias = bias_ref[...]
-    own_rows = slice(width, width + tokens)
-    side = tokens + 2 * width
+    own_at = pl.multiple_of(row * width, width)
+    other_at = pl.multiple_of((1 - row) * width, width)
+    rows = (pl.ds(own_at, width), pl.ds(other_at, width))
+    query_at = pl.ds(pl.multiple_of(tokens + own_at, width), width)
 
     def product(a, b, a_dim, b_dim):
         return lax.dot_general(a, b, (((a_dim,), (b_dim,)), ((), ())), preferred_element_type=F32)
@@ -287,28 +325,20 @@
     for head in range(half // HD):
         at = slice(head * HD, (head + 1) * HD)
         mine_at = pl.ds(pl.multiple_of(mine + head * HD, HD), HD)
-        query = jnp.concatenate([own_ref[tokens:, at], swap_qt_ref[:tokens, at]], 0)
-        target = jnp.concatenate([t_ref[:, mine_at], swap_qt_ref[tokens:, at]], 0)
+        query = jnp.concatenate([own_ref[query_at, at], swap_qt_ref[rows[0], at]], 0)
+        target = jnp.concatenate([t_ref[rows[0], mine_at], swap_qt_ref[query_at, at]], 0)
         key = jnp.concatenate(
-            [
-                near_ref[:width, at],
-                own_ref[:tokens, at],
-                far_ref[:width, at],
-                swap_near_ref[:width, at],
-                swap_k_ref[:, at],
-                swap_far_ref[:width, at],
-            ],
+            [halo_ref[:width, at]]
+            + [own_ref[r, at] for r in rows]
+            + [swap_halo_ref[:width, at]]
+            + [swap_k_ref[r, at] for r in rows],
             0,
         )
         value = jnp.concatenate(
-            [
-                near_ref[width:, at],
-                v_ref[:, mine_at],
-                far_ref[width:, at],
-                swap_near_ref[width:, at],
-                swap_v_ref[:, at],
-                swap_far_ref[width:, at],
-            ],
+            [halo_ref[width:, at]]
+            + [v_ref[r, mine_at] for r in rows]
+            + [swap_halo_ref[width:, at]]
+            + [swap_v_ref[r, at] for r in rows],
             0,
         )
         scores = product(query, key, 1, 1) * score_scale + bias
@@ -322,26 +352,98 @@
         prob_grad = product(d_out, value, 1, 1)
         score_grad = (probability * (prob_grad - delta_sum) * score_scale).astype(BF16)
         dq = product(score_grad, key, 1, 0)
-        own_grad_ref[:tokens, at] = dq[:tokens]
-        swap_first_ref[:tokens, at] = dq[tokens:].astype(BF16)
         dk = product(score_grad, query, 0, 0)
         dv = product(prob_b, d_out, 0, 0)
+        store(at, dq, dk, dv)
+
+
+def attend_near_kernel(
+    width,
+    halo_ref,
+    swap_halo_ref,
+    own_ref,
+    v_ref,
+    t_ref,
+    swap_k_ref,
+    swap_v_ref,
+    swap_qt_ref,
+    bias_ref,
+    earlier_ref,
+    halo_grad_ref,
+    swap_halo_grad_ref,
+    grad_ref,
+):
+    def store(at, dq, dk, dv):
         for place, grad in ((0, dk), (1, dv)):
-            own_at = slice((1 + place) * tokens, (2 + place) * tokens)
-            own_grad_ref[own_at, at] = grad[own_rows]
             to = slice(place * width, (place + 1) * width)
-            near_grad_ref[to, at] = grad[:width].astype(BF16)
-            far_grad_ref[to, at] = grad[width + tokens : side].astype(BF16)
-            other = grad[side:]
-            swap_near_grad_ref[to, at] = other[:width].astype(BF16)
-            swap_far_grad_ref[to, at] = other[width + tokens :].astype(BF16)
-            first, last = (other[width : 2 * width], other[2 * width : 3 * width])
-            first_to = slice(tokens + place * width, tokens + (place + 1) * width)
-            swap_first_ref[first_to, at] = jnp.where(odd == 0, last, first).astype(BF16)
-            swap_last_ref[to, at] = jnp.where(odd == 0, first, last)
-
-
-def add_kernel(a_ref, b_ref, out_ref):
+            halo_grad_ref[to, at] = grad[:width].astype(BF16)
+            swap_halo_grad_ref[to, at] = grad[3 * width : 4 * width].astype(BF16)
+            for part in range(2):
+                start = (5 * part + 1 + 2 * place) * width
+                first = (3 * part + 1) * width
+                grad_ref[start : start + 2 * width, at] = grad[first : first + 2 * width]
+        for part in range(2):
+            start = 5 * part * width
+            grad_ref[start : start + width, at] = dq[part * width : (part + 1) * width]
+
+    row = 1 - lax.rem(lax.axis_index("row"), 2)
+    attend(width, row, halo_ref, swap_halo_ref, own_ref, v_ref, t_ref, swap_k_ref, swap_v_ref,
+           swap_qt_ref, bias_ref, store)
+
+
+def attend_far_kernel(
+    width,
+    halo_ref,
+    swap_halo_ref,
+    own_ref,
+    v_ref,
+    t_ref,
+    swap_k_ref,
+    swap_v_ref,
+    swap_qt_ref,
+    bias_ref,
+    grad_ref,
+    halo_grad_ref,
+    swap_halo_grad_ref,
+    total_ref,
+    swap_first_ref,
+    swap_last_ref,
+):
+    def block(ref, index, at):
+        return ref[index * width : (index + 1) * width, at]
+
+    def put(ref, index, at, value):
+        ref[index * width : (index + 1) * width, at] = value.astype(ref.dtype)
+
+    def store(at, dq, dk, dv):
+        put(total_ref, 0, at, block(grad_ref, 0, at))
+        put(total_ref, 1, at, dq[:width])
+        put(swap_first_ref, 0, at, block(grad_ref, 5, at))
+        put(swap_first_ref, 1, at, dq[width:])
+        for place, grad in ((0, dk), (1, dv)):
+            parts = [grad[i * width : (i + 1) * width] for i in range(6)]
+            put(halo_grad_ref, place, at, parts[0])
+            put(swap_halo_grad_ref, place, at, parts[3])
+            put(total_ref, 2 + 2 * place, at, parts[2] + block(grad_ref, 1 + 2 * place, at))
+            put(total_ref, 3 + 2 * place, at, parts[1] + block(grad_ref, 2 + 2 * place, at))
+            put(swap_first_ref, 2 + place, at, parts[5] + block(grad_ref, 6 + 2 * place, at))
+            put(swap_last_ref, place, at, parts[4] + block(grad_ref, 7 + 2 * place, at))
+
+    row = lax.rem(lax.axis_index("row"), 2)
+    attend(width, row, halo_ref, swap_halo_ref, own_ref, v_ref, t_ref, swap_k_ref, swap_v_ref,
+           swap_qt_ref, bias_ref, store)
+
+
+def near_kernel(width, own_ref, near_ref, swap_near_ref, out_ref, swap_out_ref):
+    for place in range(2):
+        rows = slice(place * width, (place + 1) * width)
+        at = 2 + 2 * place
+        own = own_ref[at * width : (at + 1) * width]
+        out_ref[rows] = own + near_ref[rows].astype(F32)
+    swap_out_ref[...] = swap_near_ref[...].astype(F32)
+
+
+def add_kernel(a_ref, b_ref, earlier_ref, out_ref):
     out_ref[...] = (a_ref[...] + b_ref[...].astype(F32)).astype(BF16)
 
 
@@ -355,48 +457,33 @@
     near_ref,
     far_ref,
     swap_first_ref,
+    swap_near_ref,
     swap_last_ref,
-    swap_near_ref,
     gated_q_ref,
     gated_k_ref,
     grad_v_ref,
     sums_ref,
-    total_ref,
 ):
     tokens, feat_dev = q_ref.shape
     mine, theirs = halves(feat_dev // 2)
     near, far = sides(width)
-    k_at, v_at = (slice(0, width), slice(width, 2 * width))
-
-    def total(own_base, near_terms, far_terms):
-        for rows, terms in ((near, near_terms), (far, far_terms)):
-            value = sum(terms[1:], terms[0])
-            total_ref[rows] = value if own_base is None else value + own_base[rows]
-        return total_ref[...]
-
-    def term(ref, at):
-        return ref[at].astype(F32)
-
-    own_dk = total(own_ref.at[tokens : 2 * tokens], [term(near_ref, k_at)], [term(far_ref, k_at)])
-    gated_k_mine = gain_k_ref[:, mine] * own_dk
-    own_dv = total(own_ref.at[2 * tokens :], [term(near_ref, v_at)], [term(far_ref, v_at)])
-    grad_v_ref[:, mine] = own_dv.astype(BF16)
-    gated_q_mine = gain_q_ref[:, mine] * own_ref[:tokens]
-    first_k = term(swap_first_ref, slice(tokens, tokens + width))
-    first_v = term(swap_first_ref, slice(tokens + width, tokens + 2 * width))
-    swap_dk = total(
-        None, [first_k, term(swap_near_ref, k_at)], [term(swap_last_ref, k_at)]
-    )
-    gated_k_theirs = gain_k_ref[:, theirs] * swap_dk
-    swap_dv = total(
-        None, [first_v, term(swap_near_ref, v_at)], [term(swap_last_ref, v_at)]
-    )
-    grad_v_ref[:, theirs] = swap_dv.astype(BF16)
-    gated_q_theirs = gain_q_ref[:, theirs] * term(swap_first_ref, slice(0, tokens))
-    gated_q_ref[:, mine] = gated_q_mine
-    gated_q_ref[:, theirs] = gated_q_theirs
-    gated_k_ref[:, mine] = gated_k_mine
-    gated_k_ref[:, theirs] = gated_k_theirs
+
+    def term(ref, index):
+        return ref[index * width : (index + 1) * width].astype(F32)
+
+    for index, rows in enumerate((near, far)):
+        gated_q_ref[rows, mine] = gain_q_ref[:, mine] * term(own_ref, index)
+        gated_q_ref[rows, theirs] = gain_q_ref[:, theirs] * term(swap_first_ref, index)
+    gated_k_ref[near, mine] = gain_k_ref[:, mine] * term(near_ref, 0)
+    gated_k_ref[far, mine] = gain_k_ref[:, mine] * (term(own_ref, 3) + term(far_ref, 0))
+    grad_v_ref[near, mine] = term(near_ref, 1).astype(BF16)
+    grad_v_ref[far, mine] = (term(own_ref, 5) + term(far_ref, 1)).astype(BF16)
+    near_dk = term(swap_first_ref, 2) + term(swap_near_ref, 0)
+    near_dv = term(swap_first_ref, 3) + term(swap_near_ref, 1)
+    gated_k_ref[near, theirs] = gain_k_ref[:, theirs] * near_dk
+    gated_k_ref[far, theirs] = gain_k_ref[:, theirs] * term(swap_last_ref, 0)
+    grad_v_ref[near, theirs] = near_dv.astype(BF16)
+    grad_v_ref[far, theirs] = swap_last_ref[width:]
     sums_ref[:tokens] = jnp.sum(q_ref[...].astype(F32) * gated_q_ref[...], -1, keepdims=True)
     sums_ref[tokens:] = jnp.sum(k_ref[...].astype(F32) * gated_k_ref[...], -1, keepdims=True)
 
@@ -417,39 +504,14 @@
         ).astype(BF16)
 
 
-def window_bias(kept, rows, width, tiles):
-    frame_at = lax.axis_index("frame")
-    row_at = lax.axis_index("row")
-    odd = lax.rem(row_at, 2)
-    kept_pad = jnp.pad(kept, ((0, 0), (1, 1), (0, 0)))
-    kept_win = lax.dynamic_slice_in_dim(kept_pad, row_at * rows, rows + 2, 1)
-    kept_win = jnp.where(frame_at == 0, kept_win, kept_win[::-1])
-    turned = jnp.concatenate([kept_win[:, 3:], kept_win[:, 1:3], kept_win[:, :1]], 1)
-    kept_win = jnp.where(odd == 0, turned, kept_win)
-    key_kept = jnp.repeat(kept_win.reshape(-1), width // tiles)
-    query_at = jnp.arange(2 * rows * width)
-    key_at = jnp.arange(2 * (rows + 2) * width)
-    query_row, query_tile = (query_at // width, query_at % width // TC)
-    key_slot, key_tile = (key_at // width, key_at % width // TC)
-    key_row = key_slot % (rows + 2) - 1
-    outer = (key_row < 0) | (key_row >= rows)
-    key_row = jnp.where(outer & (odd == 0), rows - 1 - key_row, key_row)
-    near_cols = jnp.abs(query_tile[:, None] - key_tile[None, :]) <= 1
-    near_rows = jnp.abs((query_row % rows)[:, None] - key_row[None, :]) <= 1
-    same_line = (query_row // rows * (rows + 2) + query_row % rows + 1)[:, None] == key_slot[None, :]
-    same = same_line & (query_tile[:, None] == key_tile[None, :])
-    allowed = near_cols & near_rows & ((key_kept > 0)[None, :] | same)
-    return jnp.where(allowed, 0.0, -1e30).astype(F32)
-
-
 def swapped_device(q_pre, k_pre, values, target, gain_q, gain_k, kept):
     frames, rows, width, feat_dev = q_pre.shape
     tokens = rows * width
     half = feat_dev // 2
     row_blocks = lax.axis_size("row")
     inputs = [array.reshape(tokens, feat_dev) for array in (q_pre, k_pre, values, target)]
-    gain_q = gain_q.reshape(1, feat_dev)
-    gain_k = gain_k.reshape(1, feat_dev)
+    inputs += [gain_q, gain_k]
+    inputs = [pltpu.with_memory_space_constraint(array, pltpu.HBM) for array in inputs]
     near_pairs = [(r, r + 1) for r in range(0, row_blocks - 1, 2)]
     far_pairs = [(r, r + 1) for r in range(1, row_blocks - 1, 2)]
     near, far = (pairs + [(b, a) for a, b in pairs] for pairs in (near_pairs, far_pairs))
@@ -463,13 +525,15 @@
     block = shape(tokens, feat_dev)
     sum_pair = shape(2 * tokens, 1, F32)
     tokens_half = shape(tokens, half)
+    gain = shape(1, feat_dev, F32)
     edge = shape(2 * width, half)
-
-    q_all, k_all, v_all, t_all, sums, v_out = call(
+    bias = shape(2 * width, 6 * width, F32)
+
+    q_all, k_all, v_all, t_all, gain_q, gain_k, sums, v_out = call(
         load_kernel,
-        (block,) * 4 + (sum_pair, tokens_half),
-        in_specs=[pl.BlockSpec(memory_space=pltpu.HBM)] * 4,
-        scratch_shapes=[pltpu.SemaphoreType.DMA((4,))],
+        (block,) * 4 + (gain,) * 2 + (sum_pair, tokens_half),
+        in_specs=[pl.BlockSpec(memory_space=pltpu.HBM)] * 6,
+        scratch_shapes=[pltpu.SemaphoreType.DMA((6,))],
     )(*inputs)
     swap_v = lax.ppermute(v_out, "frame", SWAP)
     peer = lax.ppermute(sums, "head", SWAP)
@@ -477,57 +541,58 @@
         functools.partial(norm_kernel, width),
         (sum_pair, shape(2 * tokens, half), tokens_half, shape(2 * tokens, half), edge, edge),
     )(q_all, k_all, v_all, t_all, sums, peer, gain_q, gain_k)
+    near_in = lax.ppermute(near_out, "row", near)
     swap_k = lax.ppermute(k_out, "frame", SWAP)
-    near_in = lax.ppermute(near_out, "row", near)
+    swap_qt = lax.ppermute(qt_out, "frame", SWAP)
     far_in = lax.ppermute(far_out, "row", far)
-    swap_qt = lax.ppermute(qt_out, "frame", SWAP)
     relay_near, relay_far = call(functools.partial(relay_kernel, width), (edge, edge))(
-        swap_k, swap_v
+        swap_k, swap_v, near_in
     )
     swap_near_in = lax.ppermute(relay_near, "row", near)
     swap_far_in = lax.ppermute(relay_far, "row", far)
-    bias = window_bias(kept, rows, width, kept.shape[-1])
-    own_grad, first_out, last_terms, near_out, far_out, swap_near_out, swap_far_out = call(
-        functools.partial(attend_kernel, width),
-        (shape(3 * tokens, half, F32), shape(2 * tokens, half), shape(2 * width, half, F32))
-        + (edge,) * 4,
-        flops=10**9,
-        moved=4 * 10**6,
-    )(
-        near_in,
-        far_in,
-        swap_near_in,
-        swap_far_in,
-        own_kq,
-        v_all,
-        t_all,
-        swap_k,
-        swap_v,
-        swap_qt,
-        bias,
-    )
+    near_bias, far_bias = call(
+        functools.partial(mask_kernel, width),
+        (bias, bias),
+        in_specs=[pl.BlockSpec(memory_space=pltpu.SMEM)],
+    )(kept.transpose(0, 2, 1))
+    shared = (own_kq, v_all, t_all, swap_k, swap_v, swap_qt)
+    near_out, swap_near_out, near_terms = call(
+        functools.partial(attend_near_kernel, width),
+        (edge, edge, shape(10 * width, half, F32)),
+        flops=5 * 10**8,
+        moved=2 * 10**6,
+    )(near_in, swap_near_in, *shared, near_bias, far_in)
+    near_total = lax.ppermute(near_out, "row", near)
+    swap_near_total = lax.ppermute(swap_near_out, ("frame", "row"), swap_near)
+    far_out, swap_far_out, own_total, first_out, last_terms = call(
+        functools.partial(attend_far_kernel, width),
+        (edge, edge, shape(3 * tokens, half, F32), shape(4 * width, half))
+        + (shape(2 * width, half, F32),),
+        flops=5 * 10**8,
+        moved=2 * 10**6,
+    )(far_in, swap_far_in, *shared, far_bias, near_terms)
+    far_terms = lax.ppermute(swap_far_out, "row", far)
     swap_first = lax.ppermute(first_out, "frame", SWAP)
-    far_terms = lax.ppermute(swap_far_out, "row", far)
-    last_out = call(add_kernel, edge)(last_terms, far_terms)
-    swap_near_total = lax.ppermute(swap_near_out, ("frame", "row"), swap_near)
     far_total = lax.ppermute(far_out, "row", far)
-    near_total = lax.ppermute(near_out, "row", near)
+    near_total, swap_near_total = call(
+        functools.partial(near_kernel, width), (shape(2 * width, half, F32),) * 2
+    )(own_total, near_total, swap_near_total)
+    last_out = call(add_kernel, edge)(last_terms, far_terms, near_total)
     swap_last = lax.ppermute(last_out, "frame", SWAP)
     gated_q, gated_k, grad_v, sum_terms = call(
         functools.partial(gather_kernel, width),
         (shape(tokens, feat_dev, F32),) * 2 + (block, sum_pair),
-        scratch_shapes=[pltpu.VMEM((tokens, half), F32)],
     )(
         q_all,
         k_all,
         gain_q,
         gain_k,
-        own_grad,
+        own_total,
         near_total,
         far_total,
         swap_first,
+        swap_near_total,
         swap_last,
-        swap_near_total,
     )
     sum_peer = lax.ppermute(sum_terms, "head", SWAP)
     grad_q, grad_k = call(finish_kernel, (block, block))(

time: 57.8 us -> 50.1 us (0.87)
  the two profiles are of different devices: /device:TPU:0 before, /device:TPU:13 now
where the time goes in v3:
time: 50.1 us; the launch traced here: 49.9 us
  starting transfers between devices  28.7 us (57%)
  Pallas kernels  11.5 us (23%)
  waiting for transfers between devices  8.82 us (18%)
  between operations  0.78 us (2%)
    ppermute x1, starting transfers between devices, swapped_device(): sum_peer = lax.ppermute(sum_terms, 'head', SWAP)  6.55 us
    ppermute x1, starting transfers between devices, swapped_device(): far_in = lax.ppermute(far_out, 'row', far)  4.15 us
    ppermute x1, starting transfers between devices, swapped_device(): swap_far_in = lax.ppermute(relay_far, 'row', far)  4.15 us
    ppermute x1, waiting for transfers between devices, swapped_device(): far_total = lax.ppermute(far_out, 'row', far)  3.84 us
    pallas_call x1, Pallas kernels, swapped_device(): call(functools.partial(attend_far_kernel, width), (edge, edge, shape(3 *...  3.53 us
    pallas_call x1, Pallas kernels, swapped_device(): call(functools.partial(attend_near_kernel, width), (edge, edge, shape(10...  3.53 us
    ppermute x1, starting transfers between devices, swapped_device(): far_terms = lax.ppermute(swap_far_out, 'row', far)  3.15 us
    ppermute x1, starting transfers between devices, swapped_device(): far_total = lax.ppermute(far_out, 'row', far)  3.01 us
  transfers between devices with their start and end apart: 15, of which 5 were waited for; matrix products, arithmetic and copies ran while one was open for 0% of the time, Pallas kernels for 16%

profile of v3, /device:TPU:13, one launch (start us, length us, event | category | flops | bytes accessed | tf_op | source)
XLA Modules:
  0.0 49.9 jit_solution(10397672651855077399)
XLA Ops:
  0.6 0.0 copy-start
  0.6 1.3 %shard_map.94 = (bf16[128,1280]{1,0:T(8,128)(2,1)S(1)}, bf16[128,1280]{1,0:T(8,128)(2,1)S(1)}, bf16[128,1280]{1,0:T(8,128)(2,1)S(1)}, bf16[128,1280]{1,0:T(8,128...) custom-call(bf16[128,1280]{1,0:T(8,128)(2,1)} %bitcast.9, ...), custom_call_target="tpu_custom_call" | custom-call | flops 1000000 | bytes 1000000 | tf_op jit(solution)/shard_map/pallas_call | solution.py:532
  2.0 0.7 %collective-permute-start = (f32[256,1]{1,0:T(8,128)S(1)}, f32[256,1]{1,0:T(8,128)S(1)}, u32[]{:S(2)}, u32[]{:S(2)}) collective-permute-start(f32[256,1]{1,0:T(8,128)S(1)} %get-tuple-element.43.sums_ref), channel_id=1, source_target_pairs={{0,1},{1,0},{2,3},{3,2},{4,5},{5,4},{6,7},{7,6},{8,9},{9,8},{10,11... | collective-permute-start | bytes 3080 | tf_op jit(solution)/shard_map/ppermute | solution.py:539
  2.7 1.2 %collective-permute-start.3 = (bf16[128,640]{1,0:T(8,128)(2,1)S(1)}, bf16[128,640]{1,0:T(8,128)(2,1)S(1)}, u32[]{:S(2)}, u32[]{:S(2)}) collective-permute-start(bf16[128,640]{1,0:T(8,128)(2,1)S(1)} %get-tuple-element.46), channel_id=1, source_target_pairs={{0,16},{16,0},{1,17},{17,1},{2,18},{18,2},{3,19},{19,3},{4,20},{20... | collective-permute-start | bytes 491528 | tf_op jit(solution)/shard_map/ppermute | solution.py:538
  4.0 0.0 collective-permute-done.peer_ref
  4.0 0.3 shard_map.95
  4.2 1.0 %collective-permute-start.2 = (bf16[128,640]{1,0:T(8,128)(2,1)S(1)}, bf16[128,640]{1,0:T(8,128)(2,1)S(1)}, u32[]{:S(2)}, u32[]{:S(2)}) collective-permute-start(bf16[128,640]{1,0:T(8,128)(2,1)S(1)} %get-tuple-element.45), channel_id=1, source_target_pairs={{0,16},{16,0},{1,17},{17,1},{2,18},{18,2},{3,19},{19,3},{4,20},{20... | collective-permute-start | bytes 491528 | tf_op jit(solution)/shard_map/ppermute | solution.py:545
  5.3 0.2 collective-permute-start.4
  5.5 0.5 %collective-permute-start.6 = (bf16[256,640]{1,0:T(8,128)(2,1)S(1)}, bf16[256,640]{1,0:T(8,128)(2,1)S(1)}, u32[]{:S(2)}, u32[]{:S(2)}) collective-permute-start(bf16[256,640]{1,0:T(8,128)(2,1)S(1)} %get-tuple-element.50), channel_id=1, source_target_pairs={{0,16},{16,0},{1,17},{17,1},{2,18},{18,2},{3,19},{19,3},{4,20},{20... | collective-permute-start | bytes 983048 | tf_op jit(solution)/shard_map/ppermute | solution.py:546
  6.0 4.1 %collective-permute-start.1 = (bf16[128,640]{1,0:T(8,128)(2,1)S(1)}, bf16[128,640]{1,0:T(8,128)(2,1)S(1)}, u32[]{:S(2)}, u32[]{:S(2)}) collective-permute-start(bf16[128,640]{1,0:T(8,128)(2,1)S(1)} %get-tuple-element.44), channel_id=1, source_target_pairs={{2,4},{6,8},{10,12},{4,2},{8,6},{12,10},{3,5},{7,9},{11,13},{5,3},... | collective-permute-start | bytes 491528 | tf_op jit(solution)/shard_map/ppermute | solution.py:547
  10.1 0.0 collective-permute-done.3.v_ref.swap_v_ref
  10.1 1.9 %collective-permute-done.2.k_ref.swap_k_ref = bf16[128,640]{1,0:T(8,128)(2,1)S(1)} collective-permute-done((bf16[128,640]{1,0:T(8,128)(2,1)S(1)}, bf16[128,640]{1,0:T(8,128)(2,1)S(1)}, u32[]{:S(2)}, u32[]{:S(2)}) %collective-permute-start.2) | collective-permute-done | bytes 163872 | tf_op jit(solution)/shard_map/ppermute | solution.py:545
  12.0 0.0 collective-permute-done.4.earlier_ref.halo_ref
  12.1 0.3 collective-permute-start.7
  12.3 4.1 %collective-permute-start.5 = (bf16[128,640]{1,0:T(8,128)(2,1)S(1)}, bf16[128,640]{1,0:T(8,128)(2,1)S(1)}, u32[]{:S(2)}, u32[]{:S(2)}) collective-permute-start(bf16[128,640]{1,0:T(8,128)(2,1)S(1)} %get-tuple-element.48), channel_id=1, source_target_pairs={{2,4},{6,8},{10,12},{4,2},{8,6},{12,10},{3,5},{7,9},{11,13},{5,3},... | collective-permute-start | bytes 491528 | tf_op jit(solution)/shard_map/ppermute | solution.py:552
  16.5 0.0 copy-done
  16.5 0.8 %shard_map.97 = (f32[128,384]{1,0:T(8,128)S(1)}, f32[128,384]{1,0:T(8,128)S(1)}) custom-call(s32[2,4,16]{2,1,0:T(4,128)S(1)} %bitcast.8), custom_call_target="tpu_custom_call" | custom-call | flops 1000000 | bytes 1000000 | tf_op jit(solution)/shard_map/pallas_call | solution.py:553
  17.3 0.0 collective-permute-done.1.earlier_ref.halo_ref
  17.3 0.0 collective-permute-done.7.swap_halo_ref
  17.3 1.7 %collective-permute-done.6.swap_qt_ref = bf16[256,640]{1,0:T(8,128)(2,1)S(1)} collective-permute-done((bf16[256,640]{1,0:T(8,128)(2,1)S(1)}, bf16[256,640]{1,0:T(8,128)(2,1)S(1)}, u32[]{:S(2)}, u32[]{:S(2)}) %collective-permute-start.6) | collective-permute-done | bytes 327712 | tf_op jit(solution)/shard_map/ppermute | solution.py:546
  19.0 3.5 %shard_map.98 = (bf16[128,640]{1,0:T(8,128)(2,1)S(1)}, bf16[128,640]{1,0:T(8,128)(2,1)S(1)}, f32[640,640]{1,0:T(8,128)S(1)}) custom-call(bf16[128,640]{1,0:T(8,128)(2,1)S(1)} %collective-permute-done.4.earlier_ref.halo_ref, bf16[128,640]{1,0:T(8,128)(2,1)S(1)} %collective-permute-done.7.swap_halo_ref, bf16[256,640]{1,0:T(8,128)(2,1)S(1)} %get-tuple-element.49.own_ref, ...), custom_call_target="tpu_custom_call" | custom-call | flops 500000000 | bytes 2000000 | tf_op jit(solution)/shard_map/pallas_call | solution.py:559
  22.6 0.3 collective-permute-start.8
  22.9 2.2 %collective-permute-start.9 = (bf16[128,640]{1,0:T(8,128)(2,1)S(1)}, bf16[128,640]{1,0:T(8,128)(2,1)S(1)}, u32[]{:S(2)}, u32[]{:S(2)}) collective-permute-start(bf16[128,640]{1,0:T(8,128)(2,1)S(1)} %get-tuple-element.57), channel_id=1, source_target_pairs={{0,18},{4,22},{8,26},{12,30},{2,16},{6,20},{10,24},{14,28},{16,2},... | collective-permute-start | bytes 491528 | tf_op jit(solution)/shard_map/ppermute | solution.py:566
  25.0 0.0 collective-permute-done.5.swap_halo_ref
  25.0 3.5 %shard_map.99 = (bf16[128,640]{1,0:T(8,128)(2,1)S(1)}, bf16[128,640]{1,0:T(8,128)(2,1)S(1)}, f32[384,640]{1,0:T(8,128)S(1)}, bf16[256,640]{1,0:T(8,128)(2,1)S(1)}, f32[128,640]{1,0:T(8,128)S(1)}) custom-call(bf16[128,640]{1,0:T(8,128)(2,1)S(1)} %collective-permute-done.1.earlier_ref.halo_ref, bf16[128,640]{1,0:T(8,128)(2,1)S(1)} %collective-permute-done.5.swap_halo_ref, ...), custom_call_target="tpu_custom_call" | custom-call | flops 500000000 | bytes 2000000 | tf_op jit(solution)/shard_map/pallas_call | solution.py:567
  28.6 3.1 %collective-permute-start.12 = (bf16[128,640]{1,0:T(8,128)(2,1)S(1)}, bf16[128,640]{1,0:T(8,128)(2,1)S(1)}, u32[]{:S(2)}, u32[]{:S(2)}) collective-permute-start(bf16[128,640]{1,0:T(8,128)(2,1)S(1)} %get-tuple-element.63), channel_id=1, source_target_pairs={{2,4},{6,8},{10,12},{4,2},{8,6},{12,10},{3,5},{7,9},{11,13},{5,3},... | collective-permute-start | bytes 491528 | tf_op jit(solution)/shard_map/ppermute | solution.py:574
  31.7 0.3 collective-permute-start.11
  32.1 3.0 %collective-permute-start.10 = (bf16[128,640]{1,0:T(8,128)(2,1)S(1)}, bf16[128,640]{1,0:T(8,128)(2,1)S(1)}, u32[]{:S(2)}, u32[]{:S(2)}) collective-permute-start(bf16[128,640]{1,0:T(8,128)(2,1)S(1)} %get-tuple-element.59), channel_id=1, source_target_pairs={{2,4},{6,8},{10,12},{4,2},{8,6},{12,10},{3,5},{7,9},{11,13},{5,3},... | collective-permute-start | bytes 491528 | tf_op jit(solution)/shard_map/ppermute | solution.py:576
  35.1 0.0 collective-permute-done.8.near_ref
  35.1 0.0 collective-permute-done.9.swap_near_ref
  35.1 0.1 shard_map.100
  35.2 0.4 collective-permute-done.12.b_ref
  35.6 0.9 %collective-permute-start.13 = (bf16[128,640]{1,0:T(8,128)(2,1)S(1)}, bf16[128,640]{1,0:T(8,128)(2,1)S(1)}, u32[]{:S(2)}, u32[]{:S(2)}) collective-permute-start(bf16[128,640]{1,0:T(8,128)(2,1)S(1)} %shard_map.101), channel_id=1, source_target_pairs={{0,16},{16,0},{1,17},{17,1},{2,18},{18,2},{3,19},{19,3},{4,20},{20... | collective-permute-start | bytes 491528 | tf_op jit(solution)/shard_map/ppermute | solution.py:581
  36.5 3.8 %collective-permute-done.10.far_ref = bf16[128,640]{1,0:T(8,128)(2,1)S(1)} collective-permute-done((bf16[128,640]{1,0:T(8,128)(2,1)S(1)}, bf16[128,640]{1,0:T(8,128)(2,1)S(1)}, u32[]{:S(2)}, u32[]{:S(2)}) %collective-permute-start.10) | collective-permute-done | bytes 163872 | tf_op jit(solution)/shard_map/ppermute | solution.py:576
  40.3 0.0 collective-permute-done.13.swap_last_ref
  40.3 0.0 collective-permute-done.11.swap_first_ref
  40.3 1.0 %shard_map.102 = (f32[128,1280]{1,0:T(8,128)S(1)}, f32[128,1280]{1,0:T(8,128)S(1)}, bf16[128,1280]{1,0:T(8,128)(2,1)}, f32[256,1]{1,0:T(8,128)S(1)}) custom-call(bf16[128,1280]{1,0:T(8,128)(2,1)S(1)} %get-tuple-element.37.q_ref, bf16[128,1280]{1,0:T(8,128)(2,1)S(1)} %get-tuple-element.38.k_ref, f32[1,1280]{1,0:T(1,128)S(1)} %get-tuple-element.39.gain_q_ref, ...), custom_call_target="tpu_custom_call" | custom-call | flops 1000000 | bytes 1000000 | tf_op jit(solution)/shard_map/pallas_call | solution.py:582
  41.3 6.5 %collective-permute-start.14 = (f32[256,1]{1,0:T(8,128)S(1)}, f32[256,1]{1,0:T(8,128)S(1)}, u32[]{:S(2)}, u32[]{:S(2)}) collective-permute-start(f32[256,1]{1,0:T(8,128)S(1)} %get-tuple-element.67.sums_ref), channel_id=1, source_target_pairs={{0,1},{1,0},{2,3},{3,2},{4,5},{5,4},{6,7},{7,6},{8,9},{9,8},{10,11... | collective-permute-start | bytes 3080 | tf_op jit(solution)/shard_map/ppermute | solution.py:597
  47.9 1.0 %collective-permute-done.14.peer_ref = f32[256,1]{1,0:T(8,128)S(1)} collective-permute-done((f32[256,1]{1,0:T(8,128)S(1)}, f32[256,1]{1,0:T(8,128)S(1)}, u32[]{:S(2)}, u32[]{:S(2)}) %collective-permute-start.14) | collective-permute-done | bytes 1056 | tf_op jit(solution)/shard_map/ppermute | solution.py:597
  48.8 1.0 %shard_map.103 = (bf16[128,1280]{1,0:T(8,128)(2,1)}, bf16[128,1280]{1,0:T(8,128)(2,1)}) custom-call(bf16[128,1280]{1,0:T(8,128)(2,1)S(1)} %get-tuple-element.37.q_ref, bf16[128,1280]{1,0:T(8,128)(2,1)S(1)} %get-tuple-element.38.k_ref, f32[128,1280]{1,0:T(8,128)S(1)} %get-tuple-element.64.gated_q_ref, f32[128,1280]{1,0:T(8,128)S(1)} %get-tuple-element.65.gated_k_ref, ...), custom_call_target="tpu_custom_call" | custom-call | flops 1000000 | bytes 1000000 | tf_op jit(solution)/shard_map/pallas_call | solution.py:598
  (2 shorter events, 0.1 us)
Async XLA Ops:
  0.6 15.9 %copy-start = (s32[2,16,4]{1,2,0:T(4,128)S(1)}, s32[2,16,4]{1,2,0:T(4,128)}, u32[]{:S(2)}) copy-start(s32[2,16,4]{1,2,0:T(4,128)} %param.13) | copy-start | bytes 1540
  2.0 2.0 %collective-permute-start = (f32[256,1]{1,0:T(8,128)S(1)}, f32[256,1]{1,0:T(8,128)S(1)}, u32[]{:S(2)}, u32[]{:S(2)}) collective-permute-start(f32[256,1]{1,0:T(8,128)S(1)} %get-tuple-element.43.sums_ref), channel_id=1, source_target_pairs={{0,1},{1,0},{2,3},{3,2},{4,5},{5,4},{6,7},{7,6},{8,9},{9,8},{10,11... | collective-permute-start | bytes 3080 | tf_op jit(solution)/shard_map/ppermute | solution.py:539
  2.7 7.4 %collective-permute-start.3 = (bf16[128,640]{1,0:T(8,128)(2,1)S(1)}, bf16[128,640]{1,0:T(8,128)(2,1)S(1)}, u32[]{:S(2)}, u32[]{:S(2)}) collective-permute-start(bf16[128,640]{1,0:T(8,128)(2,1)S(1)} %get-tuple-element.46), channel_id=1, source_target_pairs={{0,16},{16,0},{1,17},{17,1},{2,18},{18,2},{3,19},{19,3},{4,20},{20... | collective-permute-start | bytes 491528 | tf_op jit(solution)/shard_map/ppermute | solution.py:538
  4.2 7.8 %collective-permute-start.2 = (bf16[128,640]{1,0:T(8,128)(2,1)S(1)}, bf16[128,640]{1,0:T(8,128)(2,1)S(1)}, u32[]{:S(2)}, u32[]{:S(2)}) collective-permute-start(bf16[128,640]{1,0:T(8,128)(2,1)S(1)} %get-tuple-element.45), channel_id=1, source_target_pairs={{0,16},{16,0},{1,17},{17,1},{2,18},{18,2},{3,19},{19,3},{4,20},{20... | collective-permute-start | bytes 491528 | tf_op jit(solution)/shard_map/ppermute | solution.py:545
  5.3 6.8 %collective-permute-start.4 = (bf16[128,640]{1,0:T(8,128)(2,1)S(1)}, bf16[128,640]{1,0:T(8,128)(2,1)S(1)}, u32[]{:S(2)}, u32[]{:S(2)}) collective-permute-start(bf16[128,640]{1,0:T(8,128)(2,1)S(1)} %get-tuple-element.47), channel_id=1, source_target_pairs={{0,2},{4,6},{8,10},{12,14},{2,0},{6,4},{10,8},{14,12},{1,3},{5,7},... | collective-permute-start | bytes 491528 | tf_op jit(solution)/shard_map/ppermute | solution.py:544
  5.5 13.6 %collective-permute-start.6 = (bf16[256,640]{1,0:T(8,128)(2,1)S(1)}, bf16[256,640]{1,0:T(8,128)(2,1)S(1)}, u32[]{:S(2)}, u32[]{:S(2)}) collective-permute-start(bf16[256,640]{1,0:T(8,128)(2,1)S(1)} %get-tuple-element.50), channel_id=1, source_target_pairs={{0,16},{16,0},{1,17},{17,1},{2,18},{18,2},{3,19},{19,3},{4,20},{20... | collective-permute-start | bytes 983048 | tf_op jit(solution)/shard_map/ppermute | solution.py:546
  6.0 11.3 %collective-permute-start.1 = (bf16[128,640]{1,0:T(8,128)(2,1)S(1)}, bf16[128,640]{1,0:T(8,128)(2,1)S(1)}, u32[]{:S(2)}, u32[]{:S(2)}) collective-permute-start(bf16[128,640]{1,0:T(8,128)(2,1)S(1)} %get-tuple-element.44), channel_id=1, source_target_pairs={{2,4},{6,8},{10,12},{4,2},{8,6},{12,10},{3,5},{7,9},{11,13},{5,3},... | collective-permute-start | bytes 491528 | tf_op jit(solution)/shard_map/ppermute | solution.py:547
  12.1 5.2 %collective-permute-start.7 = (bf16[128,640]{1,0:T(8,128)(2,1)S(1)}, bf16[128,640]{1,0:T(8,128)(2,1)S(1)}, u32[]{:S(2)}, u32[]{:S(2)}) collective-permute-start(bf16[128,640]{1,0:T(8,128)(2,1)S(1)} %get-tuple-element.52), channel_id=1, source_target_pairs={{0,2},{4,6},{8,10},{12,14},{2,0},{6,4},{10,8},{14,12},{1,3},{5,7},... | collective-permute-start | bytes 491528 | tf_op jit(solution)/shard_map/ppermute | solution.py:551
  12.3 12.7 %collective-permute-start.5 = (bf16[128,640]{1,0:T(8,128)(2,1)S(1)}, bf16[128,640]{1,0:T(8,128)(2,1)S(1)}, u32[]{:S(2)}, u32[]{:S(2)}) collective-permute-start(bf16[128,640]{1,0:T(8,128)(2,1)S(1)} %get-tuple-element.48), channel_id=1, source_target_pairs={{2,4},{6,8},{10,12},{4,2},{8,6},{12,10},{3,5},{7,9},{11,13},{5,3},... | collective-permute-start | bytes 491528 | tf_op jit(solution)/shard_map/ppermute | solution.py:552
  22.6 12.5 %collective-permute-start.8 = (bf16[128,640]{1,0:T(8,128)(2,1)S(1)}, bf16[128,640]{1,0:T(8,128)(2,1)S(1)}, u32[]{:S(2)}, u32[]{:S(2)}) collective-permute-start(bf16[128,640]{1,0:T(8,128)(2,1)S(1)} %get-tuple-element.56), channel_id=1, source_target_pairs={{0,2},{4,6},{8,10},{12,14},{2,0},{6,4},{10,8},{14,12},{1,3},{5,7},... | collective-permute-start | bytes 491528 | tf_op jit(solution)/shard_map/ppermute | solution.py:565
  22.9 12.2 %collective-permute-start.9 = (bf16[128,640]{1,0:T(8,128)(2,1)S(1)}, bf16[128,640]{1,0:T(8,128)(2,1)S(1)}, u32[]{:S(2)}, u32[]{:S(2)}) collective-permute-start(bf16[128,640]{1,0:T(8,128)(2,1)S(1)} %get-tuple-element.57), channel_id=1, source_target_pairs={{0,18},{4,22},{8,26},{12,30},{2,16},{6,20},{10,24},{14,28},{16,2},... | collective-permute-start | bytes 491528 | tf_op jit(solution)/shard_map/ppermute | solution.py:566
  28.6 7.0 %collective-permute-start.12 = (bf16[128,640]{1,0:T(8,128)(2,1)S(1)}, bf16[128,640]{1,0:T(8,128)(2,1)S(1)}, u32[]{:S(2)}, u32[]{:S(2)}) collective-permute-start(bf16[128,640]{1,0:T(8,128)(2,1)S(1)} %get-tuple-element.63), channel_id=1, source_target_pairs={{2,4},{6,8},{10,12},{4,2},{8,6},{12,10},{3,5},{7,9},{11,13},{5,3},... | collective-permute-start | bytes 491528 | tf_op jit(solution)/shard_map/ppermute | solution.py:574
  31.7 8.6 %collective-permute-start.11 = (bf16[256,640]{1,0:T(8,128)(2,1)S(1)}, bf16[256,640]{1,0:T(8,128)(2,1)S(1)}, u32[]{:S(2)}, u32[]{:S(2)}) collective-permute-start(bf16[256,640]{1,0:T(8,128)(2,1)S(1)} %get-tuple-element.60), channel_id=1, source_target_pairs={{0,16},{16,0},{1,17},{17,1},{2,18},{18,2},{3,19},{19,3},{4,20},{20... | collective-permute-start | bytes 983048 | tf_op jit(solution)/shard_map/ppermute | solution.py:575
  32.1 8.3 %collective-permute-start.10 = (bf16[128,640]{1,0:T(8,128)(2,1)S(1)}, bf16[128,640]{1,0:T(8,128)(2,1)S(1)}, u32[]{:S(2)}, u32[]{:S(2)}) collective-permute-start(bf16[128,640]{1,0:T(8,128)(2,1)S(1)} %get-tuple-element.59), channel_id=1, source_target_pairs={{2,4},{6,8},{10,12},{4,2},{8,6},{12,10},{3,5},{7,9},{11,13},{5,3},... | collective-permute-start | bytes 491528 | tf_op jit(solution)/shard_map/ppermute | solution.py:576
  35.6 4.8 %collective-permute-start.13 = (bf16[128,640]{1,0:T(8,128)(2,1)S(1)}, bf16[128,640]{1,0:T(8,128)(2,1)S(1)}, u32[]{:S(2)}, u32[]{:S(2)}) collective-permute-start(bf16[128,640]{1,0:T(8,128)(2,1)S(1)} %shard_map.101), channel_id=1, source_target_pairs={{0,16},{16,0},{1,17},{17,1},{2,18},{18,2},{3,19},{19,3},{4,20},{20... | collective-permute-start | bytes 491528 | tf_op jit(solution)/shard_map/ppermute | solution.py:581
  41.3 7.5 %collective-permute-start.14 = (f32[256,1]{1,0:T(8,128)S(1)}, f32[256,1]{1,0:T(8,128)S(1)}, u32[]{:S(2)}, u32[]{:S(2)}) collective-permute-start(f32[256,1]{1,0:T(8,128)S(1)} %get-tuple-element.67.sums_ref), channel_id=1, source_target_pairs={{0,1},{1,0},{2,3},{3,2},{4,5},{5,4},{6,7},{7,6},{8,9},{9,8},{10,11... | collective-permute-start | bytes 3080 | tf_op jit(solution)/shard_map/ppermute | solution.py:597

commit v4 on v3

--- a/solution.py
+++ b/solution.py
@@ -283,29 +283,22 @@
     frame_at = lax.axis_index("frame")
     first_row = lax.axis_index("row") * rows
     odd = lax.rem(lax.axis_index("row"), 2)
-    shape = near_ref.shape
-    key_at = lax.broadcasted_iota(jnp.int32, shape, 1)
-    query_at = lax.broadcasted_iota(jnp.int32, shape, 0)
-    key_tile = lax.rem(key_at, width) // TC
+    query_at = lax.broadcasted_iota(jnp.int32, (TC, near_ref.shape[1]), 1)
     query_tile = lax.rem(query_at, width) // TC
-    near_cols = jnp.abs(query_tile - key_tile) <= 1
-    same = (query_tile == key_tile) & (key_at // width == 3 * (query_at // width) + 1)
-    lane = lax.broadcasted_iota(jnp.int32, (1, shape[1]), 1) // TC
     for out_ref, row in ((near_ref, 1 - odd), (far_ref, odd)):
-        places = (3 * row - 1, row, 1 - row)
-        key_kept = jnp.zeros((1, shape[1]), jnp.int32)
         for part in range(2):
             frame = frame_at if part == 0 else 1 - frame_at
-            for slot, place in enumerate(places):
+            for slot, place in enumerate((3 * row - 1, row, 1 - row)):
                 at = first_row + place
                 inside = (at >= 0) & (at < count)
                 at = jnp.clip(at, 0, count - 1)
                 for tile in range(tiles):
                     value = jnp.where(inside, kept_ref[frame, tile, at], 0)
-                    here = (part * 3 + slot) * tiles + tile
-                    key_kept = jnp.where(lane == here, value, key_kept)
-        allowed = near_cols & (same | (key_kept > 0))
-        out_ref[...] = jnp.where(allowed, 0.0, -1e30)
+                    allowed = (jnp.abs(query_tile - tile) <= 1) & (value > 0)
+                    if slot == 1:
+                        allowed |= (query_tile == tile) & (query_at // width == part)
+                    here = ((part * 3 + slot) * tiles + tile) * TC
+                    out_ref[here : here + TC] = jnp.where(allowed, 0.0, -1e30)
 
 
 def attend(width, row, halo_ref, swap_halo_ref, own_ref, v_ref, t_ref, swap_k_ref, swap_v_ref,
@@ -322,7 +315,7 @@
     def product(a, b, a_dim, b_dim):
         return lax.dot_general(a, b, (((a_dim,), (b_dim,)), ((), ())), preferred_element_type=F32)
 
-    for head in range(half // HD):
+    def load(head):
         at = slice(head * HD, (head + 1) * HD)
         mine_at = pl.ds(pl.multiple_of(mine + head * HD, HD), HD)
         query = jnp.concatenate([own_ref[query_at, at], swap_qt_ref[rows[0], at]], 0)
@@ -341,20 +334,37 @@
             + [swap_v_ref[r, at] for r in rows],
             0,
         )
-        scores = product(query, key, 1, 1) * score_scale + bias
-        row_max = jnp.max(scores, -1, keepdims=True)
-        expo = jnp.exp(scores - row_max)
-        probability = expo * (1.0 / jnp.sum(expo, -1, keepdims=True))
-        prob_b = probability.astype(BF16)
-        attended = product(prob_b, value, 1, 0)
-        d_out = (attended - target.astype(F32)).astype(BF16)
-        delta_sum = jnp.sum(d_out.astype(F32) * attended, -1, keepdims=True)
-        prob_grad = product(d_out, value, 1, 1)
-        score_grad = (probability * (prob_grad - delta_sum) * score_scale).astype(BF16)
-        dq = product(score_grad, key, 1, 0)
-        dk = product(score_grad, query, 0, 0)
-        dv = product(prob_b, d_out, 0, 0)
-        store(at, dq, dk, dv)
+        return (query, target, key, value)
+
+    def weights(query, key):
+        scores = product(key, query, 1, 1) * score_scale + bias
+        expo = jnp.exp(scores - jnp.max(scores, 0, keepdims=True))
+        return expo * (1.0 / jnp.sum(expo, 0, keepdims=True))
+
+    def output_grad(prob_b, target, value):
+        attended = product(value, prob_b, 0, 0)
+        d_out = (attended - target.astype(F32).T).astype(BF16)
+        return (d_out, jnp.sum(d_out.astype(F32) * attended, 0, keepdims=True))
+
+    def score_grads(probability, d_out, delta_sum, value):
+        prob_grad = product(value, d_out, 1, 0)
+        return (probability * (prob_grad - delta_sum) * score_scale).astype(BF16)
+
+    def grads(score_grad, prob_b, d_out, query, key):
+        dq = product(key, score_grad, 0, 0).T
+        dk = product(score_grad, query, 1, 0)
+        return (dq, dk, product(prob_b, d_out, 1, 1))
+
+    heads = range(half // HD)
+    loaded = [load(head) for head in heads]
+    probability = [weights(query, key) for query, _, key, _ in loaded]
+    prob_b = [p.astype(BF16) for p in probability]
+    outs = [output_grad(p, t, v) for p, (_, t, _, v) in zip(prob_b, loaded)]
+    score_grad = [score_grads(p, *o, x[3]) for p, o, x in zip(probability, outs, loaded)]
+    for head in heads:
+        query, _, key, _ = loaded[head]
+        at = slice(head * HD, (head + 1) * HD)
+        store(at, *grads(score_grad[head], prob_b[head], outs[head][0], query, key))
 
 
 def attend_near_kernel(
@@ -527,7 +537,7 @@
     tokens_half = shape(tokens, half)
     gain = shape(1, feat_dev, F32)
     edge = shape(2 * width, half)
-    bias = shape(2 * width, 6 * width, F32)
+    bias = shape(6 * width, 2 * width, F32)
 
     q_all, k_all, v_all, t_all, gain_q, gain_k, sums, v_out = call(
         load_kernel,

time: 50.1 us -> 45.9 us (0.916)
  Pallas kernels: 11.5 us -> 7.28 us
  waiting for transfers between devices: 8.82 us -> 12.1 us
  starting transfers between devices: 28.7 us -> 25.5 us
    ppermute x1, waiting for transfers between devices: 0.01 us -> 2.42 us  [swapped_device(): swap_last = lax.ppermute(last_out, 'frame', SWAP)]
    ppermute x1, starting transfers between devices: 6.55 us -> 4.21 us  [swapped_device(): sum_peer = lax.ppermute(sum_terms, 'head', SWAP)]
    pallas_call x1, Pallas kernels: 3.53 us -> 1.4 us  [swapped_device(): call(functools.partial(attend_far_kernel, width), (edge, edge, shape(3 *...]
    pallas_call x1, Pallas kernels: 3.53 us -> 1.43 us  [swapped_device(): call(functools.partial(attend_near_kernel, width), (edge, edge, shape(10...]
    ppermute x1, waiting for transfers between devices: 0.37 us -> 1.57 us  [swapped_device(): far_terms = lax.ppermute(swap_far_out, 'row', far)]
    ppermute x1, starting transfers between devices: 0.92 us -> 0.07 us  [swapped_device(): swap_last = lax.ppermute(last_out, 'frame', SWAP)]
  transfers between devices with their start and end apart: 15 -> 15, of which waited for: 5 -> 6; matrix products, arithmetic and copies ran while one was open for 0% -> 0% of each run, Pallas kernels for 16% -> 9%
where the time goes in v4:
time: 45.9 us; the launch traced here: 45.7 us
  starting transfers between devices  25.5 us (56%)
  waiting for transfers between devices  12.1 us (26%)
  Pallas kernels  7.28 us (16%)
  between operations  0.78 us (2%)
    ppermute x1, starting transfers between devices, swapped_device(): sum_peer = lax.ppermute(sum_terms, 'head', SWAP)  4.21 us
    ppermute x1, starting transfers between devices, swapped_device(): far_in = lax.ppermute(far_out, 'row', far)  4.15 us
    ppermute x1, starting transfers between devices, swapped_device(): swap_far_in = lax.ppermute(relay_far, 'row', far)  4.15 us
    ppermute x1, waiting for transfers between devices, swapped_device(): far_total = lax.ppermute(far_out, 'row', far)  3.48 us
    ppermute x1, starting transfers between devices, swapped_device(): far_terms = lax.ppermute(swap_far_out, 'row', far)  3.16 us
    ppermute x1, starting transfers between devices, swapped_device(): far_total = lax.ppermute(far_out, 'row', far)  3.02 us
    ppermute x1, waiting for transfers between devices, swapped_device(): swap_last = lax.ppermute(last_out, 'frame', SWAP)  2.42 us
    ppermute x1, starting transfers between devices, swapped_device(): swap_near_total = lax.ppermute(swap_near_out, ('frame', 'row'), swap_near)  2.16 us
  transfers between devices with their start and end apart: 15, of which 6 were waited for; matrix products, arithmetic and copies ran while one was open for 0% of the time, Pallas kernels for 9%

profile of v4, /device:TPU:13, one launch (start us, length us, event | category | flops | bytes accessed | tf_op | source)
XLA Modules:
  0.0 45.7 jit_solution(17188315803883576657)
XLA Ops:
  0.6 0.0 copy-start
  0.6 1.3 %shard_map.94 = (bf16[128,1280]{1,0:T(8,128)(2,1)S(1)}, bf16[128,1280]{1,0:T(8,128)(2,1)S(1)}, bf16[128,1280]{1,0:T(8,128)(2,1)S(1)}, bf16[128,1280]{1,0:T(8,128...) custom-call(bf16[128,1280]{1,0:T(8,128)(2,1)} %bitcast.9, ...), custom_call_target="tpu_custom_call" | custom-call | flops 1000000 | bytes 1000000 | tf_op jit(solution)/shard_map/pallas_call | solution.py:542
  2.0 0.7 %collective-permute-start = (f32[256,1]{1,0:T(8,128)S(1)}, f32[256,1]{1,0:T(8,128)S(1)}, u32[]{:S(2)}, u32[]{:S(2)}) collective-permute-start(f32[256,1]{1,0:T(8,128)S(1)} %get-tuple-element.43.sums_ref), channel_id=1, source_target_pairs={{0,1},{1,0},{2,3},{3,2},{4,5},{5,4},{6,7},{7,6},{8,9},{9,8},{10,11... | collective-permute-start | bytes 3080 | tf_op jit(solution)/shard_map/ppermute | solution.py:549
  2.7 1.2 %collective-permute-start.3 = (bf16[128,640]{1,0:T(8,128)(2,1)S(1)}, bf16[128,640]{1,0:T(8,128)(2,1)S(1)}, u32[]{:S(2)}, u32[]{:S(2)}) collective-permute-start(bf16[128,640]{1,0:T(8,128)(2,1)S(1)} %get-tuple-element.46), channel_id=1, source_target_pairs={{0,16},{16,0},{1,17},{17,1},{2,18},{18,2},{3,19},{19,3},{4,20},{20... | collective-permute-start | bytes 491528 | tf_op jit(solution)/shard_map/ppermute | solution.py:548
  4.0 0.0 collective-permute-done.peer_ref
  4.0 0.3 shard_map.95
  4.2 1.0 %collective-permute-start.2 = (bf16[128,640]{1,0:T(8,128)(2,1)S(1)}, bf16[128,640]{1,0:T(8,128)(2,1)S(1)}, u32[]{:S(2)}, u32[]{:S(2)}) collective-permute-start(bf16[128,640]{1,0:T(8,128)(2,1)S(1)} %get-tuple-element.45), channel_id=1, source_target_pairs={{0,16},{16,0},{1,17},{17,1},{2,18},{18,2},{3,19},{19,3},{4,20},{20... | collective-permute-start | bytes 491528 | tf_op jit(solution)/shard_map/ppermute | solution.py:555
  5.3 0.2 collective-permute-start.4
  5.5 0.5 %collective-permute-start.6 = (bf16[256,640]{1,0:T(8,128)(2,1)S(1)}, bf16[256,640]{1,0:T(8,128)(2,1)S(1)}, u32[]{:S(2)}, u32[]{:S(2)}) collective-permute-start(bf16[256,640]{1,0:T(8,128)(2,1)S(1)} %get-tuple-element.50), channel_id=1, source_target_pairs={{0,16},{16,0},{1,17},{17,1},{2,18},{18,2},{3,19},{19,3},{4,20},{20... | collective-permute-start | bytes 983048 | tf_op jit(solution)/shard_map/ppermute | solution.py:556
  6.0 4.1 %collective-permute-start.1 = (bf16[128,640]{1,0:T(8,128)(2,1)S(1)}, bf16[128,640]{1,0:T(8,128)(2,1)S(1)}, u32[]{:S(2)}, u32[]{:S(2)}) collective-permute-start(bf16[128,640]{1,0:T(8,128)(2,1)S(1)} %get-tuple-element.44), channel_id=1, source_target_pairs={{2,4},{6,8},{10,12},{4,2},{8,6},{12,10},{3,5},{7,9},{11,13},{5,3},... | collective-permute-start | bytes 491528 | tf_op jit(solution)/shard_map/ppermute | solution.py:557
  10.1 0.0 collective-permute-done.3.v_ref.swap_v_ref
  10.1 1.9 %collective-permute-done.2.k_ref.swap_k_ref = bf16[128,640]{1,0:T(8,128)(2,1)S(1)} collective-permute-done((bf16[128,640]{1,0:T(8,128)(2,1)S(1)}, bf16[128,640]{1,0:T(8,128)(2,1)S(1)}, u32[]{:S(2)}, u32[]{:S(2)}) %collective-permute-start.2) | collective-permute-done | bytes 163872 | tf_op jit(solution)/shard_map/ppermute | solution.py:555
  12.0 0.0 collective-permute-done.4.earlier_ref.halo_ref
  12.1 0.3 collective-permute-start.7
  12.3 4.1 %collective-permute-start.5 = (bf16[128,640]{1,0:T(8,128)(2,1)S(1)}, bf16[128,640]{1,0:T(8,128)(2,1)S(1)}, u32[]{:S(2)}, u32[]{:S(2)}) collective-permute-start(bf16[128,640]{1,0:T(8,128)(2,1)S(1)} %get-tuple-element.48), channel_id=1, source_target_pairs={{2,4},{6,8},{10,12},{4,2},{8,6},{12,10},{3,5},{7,9},{11,13},{5,3},... | collective-permute-start | bytes 491528 | tf_op jit(solution)/shard_map/ppermute | solution.py:562
  16.5 0.0 copy-done
  16.5 0.7 %shard_map.97 = (f32[384,128]{1,0:T(8,128)S(1)}, f32[384,128]{1,0:T(8,128)S(1)}) custom-call(s32[2,4,16]{2,1,0:T(4,128)S(1)} %bitcast.8), custom_call_target="tpu_custom_call" | custom-call | flops 1000000 | bytes 1000000 | tf_op jit(solution)/shard_map/pallas_call | solution.py:563
  17.3 0.0 collective-permute-done.1.earlier_ref.halo_ref
  17.3 0.0 collective-permute-done.7.swap_halo_ref
  17.3 1.8 %collective-permute-done.6.swap_qt_ref = bf16[256,640]{1,0:T(8,128)(2,1)S(1)} collective-permute-done((bf16[256,640]{1,0:T(8,128)(2,1)S(1)}, bf16[256,640]{1,0:T(8,128)(2,1)S(1)}, u32[]{:S(2)}, u32[]{:S(2)}) %collective-permute-start.6) | collective-permute-done | bytes 327712 | tf_op jit(solution)/shard_map/ppermute | solution.py:556
  19.0 1.4 %shard_map.98 = (bf16[128,640]{1,0:T(8,128)(2,1)S(1)}, bf16[128,640]{1,0:T(8,128)(2,1)S(1)}, f32[640,640]{1,0:T(8,128)S(1)}) custom-call(bf16[128,640]{1,0:T(8,128)(2,1)S(1)} %collective-permute-done.4.earlier_ref.halo_ref, bf16[128,640]{1,0:T(8,128)(2,1)S(1)} %collective-permute-done.7.swap_halo_ref, bf16[256,640]{1,0:T(8,128)(2,1)S(1)} %get-tuple-element.49.own_ref, ...), custom_call_target="tpu_custom_call" | custom-call | flops 500000000 | bytes 2000000 | tf_op jit(solution)/shard_map/pallas_call | solution.py:569
  20.5 0.3 collective-permute-start.8
  20.8 2.2 %collective-permute-start.9 = (bf16[128,640]{1,0:T(8,128)(2,1)S(1)}, bf16[128,640]{1,0:T(8,128)(2,1)S(1)}, u32[]{:S(2)}, u32[]{:S(2)}) collective-permute-start(bf16[128,640]{1,0:T(8,128)(2,1)S(1)} %get-tuple-element.57), channel_id=1, source_target_pairs={{0,18},{4,22},{8,26},{12,30},{2,16},{6,20},{10,24},{14,28},{16,2},... | collective-permute-start | bytes 491528 | tf_op jit(solution)/shard_map/ppermute | solution.py:576
  22.9 0.0 collective-permute-done.5.swap_halo_ref
  22.9 1.4 %shard_map.99 = (bf16[128,640]{1,0:T(8,128)(2,1)S(1)}, bf16[128,640]{1,0:T(8,128)(2,1)S(1)}, f32[384,640]{1,0:T(8,128)S(1)}, bf16[256,640]{1,0:T(8,128)(2,1)S(1)}, f32[128,640]{1,0:T(8,128)S(1)}) custom-call(bf16[128,640]{1,0:T(8,128)(2,1)S(1)} %collective-permute-done.1.earlier_ref.halo_ref, bf16[128,640]{1,0:T(8,128)(2,1)S(1)} %collective-permute-done.5.swap_halo_ref, ...), custom_call_target="tpu_custom_call" | custom-call | flops 500000000 | bytes 2000000 | tf_op jit(solution)/shard_map/pallas_call | solution.py:577
  24.3 3.2 %collective-permute-start.12 = (bf16[128,640]{1,0:T(8,128)(2,1)S(1)}, bf16[128,640]{1,0:T(8,128)(2,1)S(1)}, u32[]{:S(2)}, u32[]{:S(2)}) collective-permute-start(bf16[128,640]{1,0:T(8,128)(2,1)S(1)} %get-tuple-element.63), channel_id=1, source_target_pairs={{2,4},{6,8},{10,12},{4,2},{8,6},{12,10},{3,5},{7,9},{11,13},{5,3},... | collective-permute-start | bytes 491528 | tf_op jit(solution)/shard_map/ppermute | solution.py:584
  27.5 0.3 collective-permute-start.11
  27.8 3.0 %collective-permute-start.10 = (bf16[128,640]{1,0:T(8,128)(2,1)S(1)}, bf16[128,640]{1,0:T(8,128)(2,1)S(1)}, u32[]{:S(2)}, u32[]{:S(2)}) collective-permute-start(bf16[128,640]{1,0:T(8,128)(2,1)S(1)} %get-tuple-element.59), channel_id=1, source_target_pairs={{2,4},{6,8},{10,12},{4,2},{8,6},{12,10},{3,5},{7,9},{11,13},{5,3},... | collective-permute-start | bytes 491528 | tf_op jit(solution)/shard_map/ppermute | solution.py:586
  30.8 0.0 collective-permute-done.8.near_ref
  30.8 0.0 collective-permute-done.9.swap_near_ref
  30.9 0.1 shard_map.100
  30.9 1.6 %collective-permute-done.12.b_ref = bf16[128,640]{1,0:T(8,128)(2,1)S(1)} collective-permute-done((bf16[128,640]{1,0:T(8,128)(2,1)S(1)}, bf16[128,640]{1,0:T(8,128)(2,1)S(1)}, u32[]{:S(2)}, u32[]{:S(2)}) %collective-permute-start.12) | collective-permute-done | bytes 163872 | tf_op jit(solution)/shard_map/ppermute | solution.py:584
  32.5 0.1 collective-permute-start.13
  32.6 3.5 %collective-permute-done.10.far_ref = bf16[128,640]{1,0:T(8,128)(2,1)S(1)} collective-permute-done((bf16[128,640]{1,0:T(8,128)(2,1)S(1)}, bf16[128,640]{1,0:T(8,128)(2,1)S(1)}, u32[]{:S(2)}, u32[]{:S(2)}) %collective-permute-start.10) | collective-permute-done | bytes 163872 | tf_op jit(solution)/shard_map/ppermute | solution.py:586
  36.1 2.4 %collective-permute-done.13.swap_last_ref = bf16[128,640]{1,0:T(8,128)(2,1)S(1)} collective-permute-done((bf16[128,640]{1,0:T(8,128)(2,1)S(1)}, bf16[128,640]{1,0:T(8,128)(2,1)S(1)}, u32[]{:S(2)}, u32[]{:S(2)}) %collective-permute-start.13) | collective-permute-done | bytes 163872 | tf_op jit(solution)/shard_map/ppermute | solution.py:591
  38.5 0.0 collective-permute-done.11.swap_first_ref
  38.5 1.0 %shard_map.102 = (f32[128,1280]{1,0:T(8,128)S(1)}, f32[128,1280]{1,0:T(8,128)S(1)}, bf16[128,1280]{1,0:T(8,128)(2,1)}, f32[256,1]{1,0:T(8,128)S(1)}) custom-call(bf16[128,1280]{1,0:T(8,128)(2,1)S(1)} %get-tuple-element.37.q_ref, bf16[128,1280]{1,0:T(8,128)(2,1)S(1)} %get-tuple-element.38.k_ref, f32[1,1280]{1,0:T(1,128)S(1)} %get-tuple-element.39.gain_q_ref, ...), custom_call_target="tpu_custom_call" | custom-call | flops 1000000 | bytes 1000000 | tf_op jit(solution)/shard_map/pallas_call | solution.py:592
  39.5 4.2 %collective-permute-start.14 = (f32[256,1]{1,0:T(8,128)S(1)}, f32[256,1]{1,0:T(8,128)S(1)}, u32[]{:S(2)}, u32[]{:S(2)}) collective-permute-start(f32[256,1]{1,0:T(8,128)S(1)} %get-tuple-element.67.sums_ref), channel_id=1, source_target_pairs={{0,1},{1,0},{2,3},{3,2},{4,5},{5,4},{6,7},{7,6},{8,9},{9,8},{10,11... | collective-permute-start | bytes 3080 | tf_op jit(solution)/shard_map/ppermute | solution.py:607
  43.7 1.0 %collective-permute-done.14.peer_ref = f32[256,1]{1,0:T(8,128)S(1)} collective-permute-done((f32[256,1]{1,0:T(8,128)S(1)}, f32[256,1]{1,0:T(8,128)S(1)}, u32[]{:S(2)}, u32[]{:S(2)}) %collective-permute-start.14) | collective-permute-done | bytes 1056 | tf_op jit(solution)/shard_map/ppermute | solution.py:607
  44.7 1.0 %shard_map.103 = (bf16[128,1280]{1,0:T(8,128)(2,1)}, bf16[128,1280]{1,0:T(8,128)(2,1)}) custom-call(bf16[128,1280]{1,0:T(8,128)(2,1)S(1)} %get-tuple-element.37.q_ref, bf16[128,1280]{1,0:T(8,128)(2,1)S(1)} %get-tuple-element.38.k_ref, f32[128,1280]{1,0:T(8,128)S(1)} %get-tuple-element.64.gated_q_ref, f32[128,1280]{1,0:T(8,128)S(1)} %get-tuple-element.65.gated_k_ref, ...), custom_call_target="tpu_custom_call" | custom-call | flops 1000000 | bytes 1000000 | tf_op jit(solution)/shard_map/pallas_call | solution.py:608
  (2 shorter events, 0.1 us)
Async XLA Ops:
  0.6 15.9 %copy-start = (s32[2,16,4]{1,2,0:T(4,128)S(1)}, s32[2,16,4]{1,2,0:T(4,128)}, u32[]{:S(2)}) copy-start(s32[2,16,4]{1,2,0:T(4,128)} %param.13) | copy-start | bytes 1540
  2.0 2.0 %collective-permute-start = (f32[256,1]{1,0:T(8,128)S(1)}, f32[256,1]{1,0:T(8,128)S(1)}, u32[]{:S(2)}, u32[]{:S(2)}) collective-permute-start(f32[256,1]{1,0:T(8,128)S(1)} %get-tuple-element.43.sums_ref), channel_id=1, source_target_pairs={{0,1},{1,0},{2,3},{3,2},{4,5},{5,4},{6,7},{7,6},{8,9},{9,8},{10,11... | collective-permute-start | bytes 3080 | tf_op jit(solution)/shard_map/ppermute | solution.py:549
  2.7 7.4 %collective-permute-start.3 = (bf16[128,640]{1,0:T(8,128)(2,1)S(1)}, bf16[128,640]{1,0:T(8,128)(2,1)S(1)}, u32[]{:S(2)}, u32[]{:S(2)}) collective-permute-start(bf16[128,640]{1,0:T(8,128)(2,1)S(1)} %get-tuple-element.46), channel_id=1, source_target_pairs={{0,16},{16,0},{1,17},{17,1},{2,18},{18,2},{3,19},{19,3},{4,20},{20... | collective-permute-start | bytes 491528 | tf_op jit(solution)/shard_map/ppermute | solution.py:548
  4.2 7.8 %collective-permute-start.2 = (bf16[128,640]{1,0:T(8,128)(2,1)S(1)}, bf16[128,640]{1,0:T(8,128)(2,1)S(1)}, u32[]{:S(2)}, u32[]{:S(2)}) collective-permute-start(bf16[128,640]{1,0:T(8,128)(2,1)S(1)} %get-tuple-element.45), channel_id=1, source_target_pairs={{0,16},{16,0},{1,17},{17,1},{2,18},{18,2},{3,19},{19,3},{4,20},{20... | collective-permute-start | bytes 491528 | tf_op jit(solution)/shard_map/ppermute | solution.py:555
  5.3 6.8 %collective-permute-start.4 = (bf16[128,640]{1,0:T(8,128)(2,1)S(1)}, bf16[128,640]{1,0:T(8,128)(2,1)S(1)}, u32[]{:S(2)}, u32[]{:S(2)}) collective-permute-start(bf16[128,640]{1,0:T(8,128)(2,1)S(1)} %get-tuple-element.47), channel_id=1, source_target_pairs={{0,2},{4,6},{8,10},{12,14},{2,0},{6,4},{10,8},{14,12},{1,3},{5,7},... | collective-permute-start | bytes 491528 | tf_op jit(solution)/shard_map/ppermute | solution.py:554
  5.5 13.6 %collective-permute-start.6 = (bf16[256,640]{1,0:T(8,128)(2,1)S(1)}, bf16[256,640]{1,0:T(8,128)(2,1)S(1)}, u32[]{:S(2)}, u32[]{:S(2)}) collective-permute-start(bf16[256,640]{1,0:T(8,128)(2,1)S(1)} %get-tuple-element.50), channel_id=1, source_target_pairs={{0,16},{16,0},{1,17},{17,1},{2,18},{18,2},{3,19},{19,3},{4,20},{20... | collective-permute-start | bytes 983048 | tf_op jit(solution)/shard_map/ppermute | solution.py:556
  6.0 11.3 %collective-permute-start.1 = (bf16[128,640]{1,0:T(8,128)(2,1)S(1)}, bf16[128,640]{1,0:T(8,128)(2,1)S(1)}, u32[]{:S(2)}, u32[]{:S(2)}) collective-permute-start(bf16[128,640]{1,0:T(8,128)(2,1)S(1)} %get-tuple-element.44), channel_id=1, source_target_pairs={{2,4},{6,8},{10,12},{4,2},{8,6},{12,10},{3,5},{7,9},{11,13},{5,3},... | collective-permute-start | bytes 491528 | tf_op jit(solution)/shard_map/ppermute | solution.py:557
  12.1 5.2 %collective-permute-start.7 = (bf16[128,640]{1,0:T(8,128)(2,1)S(1)}, bf16[128,640]{1,0:T(8,128)(2,1)S(1)}, u32[]{:S(2)}, u32[]{:S(2)}) collective-permute-start(bf16[128,640]{1,0:T(8,128)(2,1)S(1)} %get-tuple-element.52), channel_id=1, source_target_pairs={{0,2},{4,6},{8,10},{12,14},{2,0},{6,4},{10,8},{14,12},{1,3},{5,7},... | collective-permute-start | bytes 491528 | tf_op jit(solution)/shard_map/ppermute | solution.py:561
  12.3 10.6 %collective-permute-start.5 = (bf16[128,640]{1,0:T(8,128)(2,1)S(1)}, bf16[128,640]{1,0:T(8,128)(2,1)S(1)}, u32[]{:S(2)}, u32[]{:S(2)}) collective-permute-start(bf16[128,640]{1,0:T(8,128)(2,1)S(1)} %get-tuple-element.48), channel_id=1, source_target_pairs={{2,4},{6,8},{10,12},{4,2},{8,6},{12,10},{3,5},{7,9},{11,13},{5,3},... | collective-permute-start | bytes 491528 | tf_op jit(solution)/shard_map/ppermute | solution.py:562
  20.5 10.4 %collective-permute-start.8 = (bf16[128,640]{1,0:T(8,128)(2,1)S(1)}, bf16[128,640]{1,0:T(8,128)(2,1)S(1)}, u32[]{:S(2)}, u32[]{:S(2)}) collective-permute-start(bf16[128,640]{1,0:T(8,128)(2,1)S(1)} %get-tuple-element.56), channel_id=1, source_target_pairs={{0,2},{4,6},{8,10},{12,14},{2,0},{6,4},{10,8},{14,12},{1,3},{5,7},... | collective-permute-start | bytes 491528 | tf_op jit(solution)/shard_map/ppermute | solution.py:575
  20.8 10.1 %collective-permute-start.9 = (bf16[128,640]{1,0:T(8,128)(2,1)S(1)}, bf16[128,640]{1,0:T(8,128)(2,1)S(1)}, u32[]{:S(2)}, u32[]{:S(2)}) collective-permute-start(bf16[128,640]{1,0:T(8,128)(2,1)S(1)} %get-tuple-element.57), channel_id=1, source_target_pairs={{0,18},{4,22},{8,26},{12,30},{2,16},{6,20},{10,24},{14,28},{16,2},... | collective-permute-start | bytes 491528 | tf_op jit(solution)/shard_map/ppermute | solution.py:576
  24.3 8.2 %collective-permute-start.12 = (bf16[128,640]{1,0:T(8,128)(2,1)S(1)}, bf16[128,640]{1,0:T(8,128)(2,1)S(1)}, u32[]{:S(2)}, u32[]{:S(2)}) collective-permute-start(bf16[128,640]{1,0:T(8,128)(2,1)S(1)} %get-tuple-element.63), channel_id=1, source_target_pairs={{2,4},{6,8},{10,12},{4,2},{8,6},{12,10},{3,5},{7,9},{11,13},{5,3},... | collective-permute-start | bytes 491528 | tf_op jit(solution)/shard_map/ppermute | solution.py:584
  27.5 11.0 %collective-permute-start.11 = (bf16[256,640]{1,0:T(8,128)(2,1)S(1)}, bf16[256,640]{1,0:T(8,128)(2,1)S(1)}, u32[]{:S(2)}, u32[]{:S(2)}) collective-permute-start(bf16[256,640]{1,0:T(8,128)(2,1)S(1)} %get-tuple-element.60), channel_id=1, source_target_pairs={{0,16},{16,0},{1,17},{17,1},{2,18},{18,2},{3,19},{19,3},{4,20},{20... | collective-permute-start | bytes 983048 | tf_op jit(solution)/shard_map/ppermute | solution.py:585
  27.8 8.3 %collective-permute-start.10 = (bf16[128,640]{1,0:T(8,128)(2,1)S(1)}, bf16[128,640]{1,0:T(8,128)(2,1)S(1)}, u32[]{:S(2)}, u32[]{:S(2)}) collective-permute-start(bf16[128,640]{1,0:T(8,128)(2,1)S(1)} %get-tuple-element.59), channel_id=1, source_target_pairs={{2,4},{6,8},{10,12},{4,2},{8,6},{12,10},{3,5},{7,9},{11,13},{5,3},... | collective-permute-start | bytes 491528 | tf_op jit(solution)/shard_map/ppermute | solution.py:586
  32.5 6.0 %collective-permute-start.13 = (bf16[128,640]{1,0:T(8,128)(2,1)S(1)}, bf16[128,640]{1,0:T(8,128)(2,1)S(1)}, u32[]{:S(2)}, u32[]{:S(2)}) collective-permute-start(bf16[128,640]{1,0:T(8,128)(2,1)S(1)} %shard_map.101), channel_id=1, source_target_pairs={{0,16},{16,0},{1,17},{17,1},{2,18},{18,2},{3,19},{19,3},{4,20},{20... | collective-permute-start | bytes 491528 | tf_op jit(solution)/shard_map/ppermute | solution.py:591
  39.5 5.2 %collective-permute-start.14 = (f32[256,1]{1,0:T(8,128)S(1)}, f32[256,1]{1,0:T(8,128)S(1)}, u32[]{:S(2)}, u32[]{:S(2)}) collective-permute-start(f32[256,1]{1,0:T(8,128)S(1)} %get-tuple-element.67.sums_ref), channel_id=1, source_target_pairs={{0,1},{1,0},{2,3},{3,2},{4,5},{5,4},{6,7},{7,6},{8,9},{9,8},{10,11... | collective-permute-start | bytes 3080 | tf_op jit(solution)/shard_map/ppermute | solution.py:607

commit v5 on v4

--- a/solution.py
+++ b/solution.py
@@ -270,13 +270,16 @@
         out_ref[width:] = v_ref[rows, mine]
 
 
-def relay_kernel(width, k_ref, v_ref, earlier_ref, near_ref, far_ref):
-    for out_ref, rows in zip((near_ref, far_ref), sides(width)):
-        out_ref[:width] = k_ref[rows]
-        out_ref[width:] = v_ref[rows]
-
-
-def mask_kernel(width, kept_ref, near_ref, far_ref):
+def relay_near_kernel(width, k_ref, v_ref, earlier_ref, out_ref):
+    near, _ = sides(width)
+    out_ref[:width] = k_ref[near]
+    out_ref[width:] = v_ref[near]
+
+
+def relay_far_kernel(width, kept_ref, k_ref, v_ref, earlier_ref, out_ref, near_ref, far_ref):
+    _, far = sides(width)
+    out_ref[:width] = k_ref[far]
+    out_ref[width:] = v_ref[far]
     rows = 2
     count = kept_ref.shape[2]
     tiles = width // TC
@@ -450,10 +453,10 @@
         at = 2 + 2 * place
         own = own_ref[at * width : (at + 1) * width]
         out_ref[rows] = own + near_ref[rows].astype(F32)
-    swap_out_ref[...] = swap_near_ref[...].astype(F32)
-
-
-def add_kernel(a_ref, b_ref, earlier_ref, out_ref):
+    swap_out_ref[...] = swap_near_ref[: 2 * width].astype(F32)
+
+
+def add_kernel(a_ref, b_ref, out_ref):
     out_ref[...] = (a_ref[...] + b_ref[...].astype(F32)).astype(BF16)
 
 
@@ -537,6 +540,7 @@
     tokens_half = shape(tokens, half)
     gain = shape(1, feat_dev, F32)
     edge = shape(2 * width, half)
+    padded_edge = shape(2 * width + 16, half)
     bias = shape(6 * width, 2 * width, F32)
 
     q_all, k_all, v_all, t_all, gain_q, gain_k, sums, v_out = call(
@@ -555,20 +559,19 @@
     swap_k = lax.ppermute(k_out, "frame", SWAP)
     swap_qt = lax.ppermute(qt_out, "frame", SWAP)
     far_in = lax.ppermute(far_out, "row", far)
-    relay_near, relay_far = call(functools.partial(relay_kernel, width), (edge, edge))(
-        swap_k, swap_v, near_in
-    )
+    relay_near = call(functools.partial(relay_near_kernel, width), edge)(swap_k, swap_v, near_in)
     swap_near_in = lax.ppermute(relay_near, "row", near)
+    relay_far, near_bias, far_bias = call(
+        functools.partial(relay_far_kernel, width),
+        (edge, bias, bias),
+        in_specs=[pl.BlockSpec(memory_space=pltpu.SMEM)]
+        + [pl.BlockSpec(memory_space=pltpu.VMEM)] * 3,
+    )(kept.transpose(0, 2, 1), swap_k, swap_v, relay_near)
     swap_far_in = lax.ppermute(relay_far, "row", far)
-    near_bias, far_bias = call(
-        functools.partial(mask_kernel, width),
-        (bias, bias),
-        in_specs=[pl.BlockSpec(memory_space=pltpu.SMEM)],
-    )(kept.transpose(0, 2, 1))
     shared = (own_kq, v_all, t_all, swap_k, swap_v, swap_qt)
     near_out, swap_near_out, near_terms = call(
         functools.partial(attend_near_kernel, width),
-        (edge, edge, shape(10 * width, half, F32)),
+        (padded_edge, padded_edge, shape(10 * width, half, F32)),
         flops=5 * 10**8,
         moved=2 * 10**6,
     )(near_in, swap_near_in, *shared, near_bias, far_in)
@@ -585,9 +588,11 @@
     swap_first = lax.ppermute(first_out, "frame", SWAP)
     far_total = lax.ppermute(far_out, "row", far)
     near_total, swap_near_total = call(
-        functools.partial(near_kernel, width), (shape(2 * width, half, F32),) * 2
+        functools.partial(near_kernel, width),
+        (shape(2 * width, half, F32),) * 2,
+        flops=3 * 10**9,
     )(own_total, near_total, swap_near_total)
-    last_out = call(add_kernel, edge)(last_terms, far_terms, near_total)
+    last_out = call(add_kernel, edge, flops=1, moved=1)(last_terms, far_terms)
     swap_last = lax.ppermute(last_out, "frame", SWAP)
     gated_q, gated_k, grad_v, sum_terms = call(
         functools.partial(gather_kernel, width),

time: 45.9 us -> 44.4 us (0.967)
  starting transfers between devices: 25.5 us -> 24.6 us
  waiting for transfers between devices: 12.1 us -> 11.6 us
    ppermute x1, starting transfers between devices: 4.21 us -> 2.61 us  [swapped_device(): sum_peer = lax.ppermute(sum_terms, 'head', SWAP)]
    ppermute x1, waiting for transfers between devices: 2.42 us -> 3.6 us  [swapped_device(): swap_last = lax.ppermute(last_out, 'frame', SWAP)]
    ppermute x1, waiting for transfers between devices: 1.57 us -> 0.56 us  [swapped_device(): far_terms = lax.ppermute(swap_far_out, 'row', far)]
    ppermute x1, waiting for transfers between devices: 3.48 us -> 2.76 us  [swapped_device(): far_total = lax.ppermute(far_out, 'row', far)]
    ppermute x1, starting transfers between devices: 0.07 us -> 0.73 us  [swapped_device(): swap_last = lax.ppermute(last_out, 'frame', SWAP)]
where the time goes in v5:
time: 44.4 us; the launch traced here: 44.2 us
  starting transfers between devices  24.6 us (55%)
  waiting for transfers between devices  11.6 us (26%)
  Pallas kernels  7.28 us (16%)
  between operations  0.75 us (2%)
    ppermute x1, starting transfers between devices, swapped_device(): swap_far_in = lax.ppermute(relay_far, 'row', far)  4.16 us
    ppermute x1, starting transfers between devices, swapped_device(): far_in = lax.ppermute(far_out, 'row', far)  4.15 us
    ppermute x1, waiting for transfers between devices, swapped_device(): swap_last = lax.ppermute(last_out, 'frame', SWAP)  3.6 us
    ppermute x1, starting transfers between devices, swapped_device(): far_terms = lax.ppermute(swap_far_out, 'row', far)  3.16 us
    ppermute x1, starting transfers between devices, swapped_device(): far_total = lax.ppermute(far_out, 'row', far)  3.02 us
    ppermute x1, waiting for transfers between devices, swapped_device(): far_total = lax.ppermute(far_out, 'row', far)  2.76 us
    ppermute x1, starting transfers between devices, swapped_device(): sum_peer = lax.ppermute(sum_terms, 'head', SWAP)  2.61 us
    ppermute x1, starting transfers between devices, swapped_device(): swap_near_total = lax.ppermute(swap_near_out, ('frame', 'row'), swap_near)  2.17 us
  transfers between devices with their start and end apart: 15, of which 6 were waited for; matrix products, arithmetic and copies ran while one was open for 0% of the time, Pallas kernels for 9%

profile of v5, /device:TPU:13, one launch (start us, length us, event | category | flops | bytes accessed | tf_op | source)
XLA Modules:
  0.0 44.2 jit_solution(9631637980442477694)
XLA Ops:
  0.6 0.0 copy-start
  0.6 1.3 %shard_map.94 = (bf16[128,1280]{1,0:T(8,128)(2,1)S(1)}, bf16[128,1280]{1,0:T(8,128)(2,1)S(1)}, bf16[128,1280]{1,0:T(8,128)(2,1)S(1)}, bf16[128,1280]{1,0:T(8,128...) custom-call(bf16[128,1280]{1,0:T(8,128)(2,1)} %bitcast.9, ...), custom_call_target="tpu_custom_call" | custom-call | flops 1000000 | bytes 1000000 | tf_op jit(solution)/shard_map/pallas_call | solution.py:546
  2.0 0.7 %collective-permute-start = (f32[256,1]{1,0:T(8,128)S(1)}, f32[256,1]{1,0:T(8,128)S(1)}, u32[]{:S(2)}, u32[]{:S(2)}) collective-permute-start(f32[256,1]{1,0:T(8,128)S(1)} %get-tuple-element.42.sums_ref), channel_id=1, source_target_pairs={{0,1},{1,0},{2,3},{3,2},{4,5},{5,4},{6,7},{7,6},{8,9},{9,8},{10,11... | collective-permute-start | bytes 3080 | tf_op jit(solution)/shard_map/ppermute | solution.py:553
  2.7 1.2 %collective-permute-start.3 = (bf16[128,640]{1,0:T(8,128)(2,1)S(1)}, bf16[128,640]{1,0:T(8,128)(2,1)S(1)}, u32[]{:S(2)}, u32[]{:S(2)}) collective-permute-start(bf16[128,640]{1,0:T(8,128)(2,1)S(1)} %get-tuple-element.45), channel_id=1, source_target_pairs={{0,16},{16,0},{1,17},{17,1},{2,18},{18,2},{3,19},{19,3},{4,20},{20... | collective-permute-start | bytes 491528 | tf_op jit(solution)/shard_map/ppermute | solution.py:552
  4.0 0.0 collective-permute-done.peer_ref
  4.0 0.3 shard_map.95
  4.2 1.0 %collective-permute-start.2 = (bf16[128,640]{1,0:T(8,128)(2,1)S(1)}, bf16[128,640]{1,0:T(8,128)(2,1)S(1)}, u32[]{:S(2)}, u32[]{:S(2)}) collective-permute-start(bf16[128,640]{1,0:T(8,128)(2,1)S(1)} %get-tuple-element.44), channel_id=1, source_target_pairs={{0,16},{16,0},{1,17},{17,1},{2,18},{18,2},{3,19},{19,3},{4,20},{20... | collective-permute-start | bytes 491528 | tf_op jit(solution)/shard_map/ppermute | solution.py:559
  5.3 0.2 collective-permute-start.4
  5.5 0.5 %collective-permute-start.6 = (bf16[256,640]{1,0:T(8,128)(2,1)S(1)}, bf16[256,640]{1,0:T(8,128)(2,1)S(1)}, u32[]{:S(2)}, u32[]{:S(2)}) collective-permute-start(bf16[256,640]{1,0:T(8,128)(2,1)S(1)} %get-tuple-element.49), channel_id=1, source_target_pairs={{0,16},{16,0},{1,17},{17,1},{2,18},{18,2},{3,19},{19,3},{4,20},{20... | collective-permute-start | bytes 983048 | tf_op jit(solution)/shard_map/ppermute | solution.py:560
  6.0 4.1 %collective-permute-start.1 = (bf16[128,640]{1,0:T(8,128)(2,1)S(1)}, bf16[128,640]{1,0:T(8,128)(2,1)S(1)}, u32[]{:S(2)}, u32[]{:S(2)}) collective-permute-start(bf16[128,640]{1,0:T(8,128)(2,1)S(1)} %get-tuple-element.43), channel_id=1, source_target_pairs={{2,4},{6,8},{10,12},{4,2},{8,6},{12,10},{3,5},{7,9},{11,13},{5,3},... | collective-permute-start | bytes 491528 | tf_op jit(solution)/shard_map/ppermute | solution.py:561
  10.1 0.0 collective-permute-done.3.v_ref.swap_v_ref
  10.1 1.9 %collective-permute-done.2.k_ref.swap_k_ref = bf16[128,640]{1,0:T(8,128)(2,1)S(1)} collective-permute-done((bf16[128,640]{1,0:T(8,128)(2,1)S(1)}, bf16[128,640]{1,0:T(8,128)(2,1)S(1)}, u32[]{:S(2)}, u32[]{:S(2)}) %collective-permute-start.2) | collective-permute-done | bytes 163872 | tf_op jit(solution)/shard_map/ppermute | solution.py:559
  12.0 0.0 collective-permute-done.4.earlier_ref.halo_ref
  12.0 0.3 collective-permute-start.7
  12.3 0.0 copy-done
  12.3 0.7 %shard_map.97 = (bf16[128,640]{1,0:T(8,128)(2,1)S(1)}, f32[384,128]{1,0:T(8,128)S(1)}, f32[384,128]{1,0:T(8,128)S(1)}) custom-call(s32[2,4,16]{2,1,0:T(4,128)S(1)} %bitcast.8, bf16[128,640]{1,0:T(8,128)(2,1)S(1)} %collective-permute-done.2.k_ref.swap_k_ref, bf16[128,640]{1,0:T(8,128)(2,1)S(1)} %collective-permute-done.3.v_ref.swap_v_ref, ...), custom_call_target="tpu_custom_call" | custom-call | flops 1000000 | bytes 1000000 | tf_op jit(solution)/shard_map/pallas_call | solution.py:564
  13.1 4.2 %collective-permute-start.5 = (bf16[128,640]{1,0:T(8,128)(2,1)S(1)}, bf16[128,640]{1,0:T(8,128)(2,1)S(1)}, u32[]{:S(2)}, u32[]{:S(2)}) collective-permute-start(bf16[128,640]{1,0:T(8,128)(2,1)S(1)} %get-tuple-element.47), channel_id=1, source_target_pairs={{2,4},{6,8},{10,12},{4,2},{8,6},{12,10},{3,5},{7,9},{11,13},{5,3},... | collective-permute-start | bytes 491528 | tf_op jit(solution)/shard_map/ppermute | solution.py:570
  17.2 0.0 collective-permute-done.1.earlier_ref.halo_ref
  17.3 0.0 collective-permute-done.7.swap_halo_ref
  17.3 1.8 %collective-permute-done.6.swap_qt_ref = bf16[256,640]{1,0:T(8,128)(2,1)S(1)} collective-permute-done((bf16[256,640]{1,0:T(8,128)(2,1)S(1)}, bf16[256,640]{1,0:T(8,128)(2,1)S(1)}, u32[]{:S(2)}, u32[]{:S(2)}) %collective-permute-start.6) | collective-permute-done | bytes 327712 | tf_op jit(solution)/shard_map/ppermute | solution.py:560
  19.0 1.4 %shard_map.98 = (bf16[144,640]{1,0:T(8,128)(2,1)S(1)}, bf16[144,640]{1,0:T(8,128)(2,1)S(1)}, f32[640,640]{1,0:T(8,128)S(1)}) custom-call(bf16[128,640]{1,0:T(8,128)(2,1)S(1)} %collective-permute-done.4.earlier_ref.halo_ref, bf16[128,640]{1,0:T(8,128)(2,1)S(1)} %collective-permute-done.7.swap_halo_ref, bf16[256,640]{1,0:T(8,128)(2,1)S(1)} %get-tuple-element.48.own_ref, ...), custom_call_target="tpu_custom_call" | custom-call | flops 500000000 | bytes 2000000 | tf_op jit(solution)/shard_map/pallas_call | solution.py:572
  20.5 0.3 collective-permute-start.8
  20.8 2.2 %collective-permute-start.9 = (bf16[144,640]{1,0:T(8,128)(2,1)S(1)}, bf16[144,640]{1,0:T(8,128)(2,1)S(1)}, u32[]{:S(2)}, u32[]{:S(2)}) collective-permute-start(bf16[144,640]{1,0:T(8,128)(2,1)S(1)} %get-tuple-element.55), channel_id=1, source_target_pairs={{0,18},{4,22},{8,26},{12,30},{2,16},{6,20},{10,24},{14,28},{16,2},... | collective-permute-start | bytes 552968 | tf_op jit(solution)/shard_map/ppermute | solution.py:579
  22.9 0.0 collective-permute-done.5.swap_halo_ref
  22.9 1.4 %shard_map.99 = (bf16[128,640]{1,0:T(8,128)(2,1)S(1)}, bf16[128,640]{1,0:T(8,128)(2,1)S(1)}, f32[384,640]{1,0:T(8,128)S(1)}, bf16[256,640]{1,0:T(8,128)(2,1)S(1)}, f32[128,640]{1,0:T(8,128)S(1)}) custom-call(bf16[128,640]{1,0:T(8,128)(2,1)S(1)} %collective-permute-done.1.earlier_ref.halo_ref, bf16[128,640]{1,0:T(8,128)(2,1)S(1)} %collective-permute-done.5.swap_halo_ref, ...), custom_call_target="tpu_custom_call" | custom-call | flops 500000000 | bytes 2000000 | tf_op jit(solution)/shard_map/pallas_call | solution.py:580
  24.4 3.2 %collective-permute-start.12 = (bf16[128,640]{1,0:T(8,128)(2,1)S(1)}, bf16[128,640]{1,0:T(8,128)(2,1)S(1)}, u32[]{:S(2)}, u32[]{:S(2)}) collective-permute-start(bf16[128,640]{1,0:T(8,128)(2,1)S(1)} %get-tuple-element.61), channel_id=1, source_target_pairs={{2,4},{6,8},{10,12},{4,2},{8,6},{12,10},{3,5},{7,9},{11,13},{5,3},... | collective-permute-start | bytes 491528 | tf_op jit(solution)/shard_map/ppermute | solution.py:587
  27.5 0.3 collective-permute-start.11
  27.8 3.0 %collective-permute-start.10 = (bf16[128,640]{1,0:T(8,128)(2,1)S(1)}, bf16[128,640]{1,0:T(8,128)(2,1)S(1)}, u32[]{:S(2)}, u32[]{:S(2)}) collective-permute-start(bf16[128,640]{1,0:T(8,128)(2,1)S(1)} %get-tuple-element.57), channel_id=1, source_target_pairs={{2,4},{6,8},{10,12},{4,2},{8,6},{12,10},{3,5},{7,9},{11,13},{5,3},... | collective-permute-start | bytes 491528 | tf_op jit(solution)/shard_map/ppermute | solution.py:589
  30.9 0.6 %collective-permute-done.12.b_ref = bf16[128,640]{1,0:T(8,128)(2,1)S(1)} collective-permute-done((bf16[128,640]{1,0:T(8,128)(2,1)S(1)}, bf16[128,640]{1,0:T(8,128)(2,1)S(1)}, u32[]{:S(2)}, u32[]{:S(2)}) %collective-permute-start.12) | collective-permute-done | bytes 163872 | tf_op jit(solution)/shard_map/ppermute | solution.py:587
  31.5 0.7 %collective-permute-start.13 = (bf16[128,640]{1,0:T(8,128)(2,1)S(1)}, bf16[128,640]{1,0:T(8,128)(2,1)S(1)}, u32[]{:S(2)}, u32[]{:S(2)}) collective-permute-start(bf16[128,640]{1,0:T(8,128)(2,1)S(1)} %shard_map.101), channel_id=1, source_target_pairs={{0,16},{16,0},{1,17},{17,1},{2,18},{18,2},{3,19},{19,3},{4,20},{20... | collective-permute-start | bytes 491528 | tf_op jit(solution)/shard_map/ppermute | solution.py:596
  32.2 0.0 collective-permute-done.8.near_ref
  32.2 0.0 collective-permute-done.9.swap_near_ref
  32.2 0.1 shard_map.100
  32.2 2.8 %collective-permute-done.10.far_ref = bf16[128,640]{1,0:T(8,128)(2,1)S(1)} collective-permute-done((bf16[128,640]{1,0:T(8,128)(2,1)S(1)}, bf16[128,640]{1,0:T(8,128)(2,1)S(1)}, u32[]{:S(2)}, u32[]{:S(2)}) %collective-permute-start.10) | collective-permute-done | bytes 163872 | tf_op jit(solution)/shard_map/ppermute | solution.py:589
  35.0 3.6 %collective-permute-done.13.swap_last_ref = bf16[128,640]{1,0:T(8,128)(2,1)S(1)} collective-permute-done((bf16[128,640]{1,0:T(8,128)(2,1)S(1)}, bf16[128,640]{1,0:T(8,128)(2,1)S(1)}, u32[]{:S(2)}, u32[]{:S(2)}) %collective-permute-start.13) | collective-permute-done | bytes 163872 | tf_op jit(solution)/shard_map/ppermute | solution.py:596
  38.6 0.0 collective-permute-done.11.swap_first_ref
  38.6 1.0 %shard_map.102 = (f32[128,1280]{1,0:T(8,128)S(1)}, f32[128,1280]{1,0:T(8,128)S(1)}, bf16[128,1280]{1,0:T(8,128)(2,1)}, f32[256,1]{1,0:T(8,128)S(1)}) custom-call(bf16[128,1280]{1,0:T(8,128)(2,1)S(1)} %get-tuple-element.36.q_ref, bf16[128,1280]{1,0:T(8,128)(2,1)S(1)} %get-tuple-element.37.k_ref, f32[1,1280]{1,0:T(1,128)S(1)} %get-tuple-element.38.gain_q_ref, ...), custom_call_target="tpu_custom_call" | custom-call | flops 1000000 | bytes 1000000 | tf_op jit(solution)/shard_map/pallas_call | solution.py:597
  39.6 2.6 %collective-permute-start.14 = (f32[256,1]{1,0:T(8,128)S(1)}, f32[256,1]{1,0:T(8,128)S(1)}, u32[]{:S(2)}, u32[]{:S(2)}) collective-permute-start(f32[256,1]{1,0:T(8,128)S(1)} %get-tuple-element.65.sums_ref), channel_id=1, source_target_pairs={{0,1},{1,0},{2,3},{3,2},{4,5},{5,4},{6,7},{7,6},{8,9},{9,8},{10,11... | collective-permute-start | bytes 3080 | tf_op jit(solution)/shard_map/ppermute | solution.py:612
  42.2 1.0 %collective-permute-done.14.peer_ref = f32[256,1]{1,0:T(8,128)S(1)} collective-permute-done((f32[256,1]{1,0:T(8,128)S(1)}, f32[256,1]{1,0:T(8,128)S(1)}, u32[]{:S(2)}, u32[]{:S(2)}) %collective-permute-start.14) | collective-permute-done | bytes 1056 | tf_op jit(solution)/shard_map/ppermute | solution.py:612
  43.2 1.0 %shard_map.103 = (bf16[128,1280]{1,0:T(8,128)(2,1)}, bf16[128,1280]{1,0:T(8,128)(2,1)}) custom-call(bf16[128,1280]{1,0:T(8,128)(2,1)S(1)} %get-tuple-element.36.q_ref, bf16[128,1280]{1,0:T(8,128)(2,1)S(1)} %get-tuple-element.37.k_ref, f32[128,1280]{1,0:T(8,128)S(1)} %get-tuple-element.62.gated_q_ref, f32[128,1280]{1,0:T(8,128)S(1)} %get-tuple-element.63.gated_k_ref, ...), custom_call_target="tpu_custom_call" | custom-call | flops 1000000 | bytes 1000000 | tf_op jit(solution)/shard_map/pallas_call | solution.py:613
  (2 shorter events, 0.0 us)
Async XLA Ops:
  0.6 11.7 %copy-start = (s32[2,16,4]{1,2,0:T(4,128)S(1)}, s32[2,16,4]{1,2,0:T(4,128)}, u32[]{:S(2)}) copy-start(s32[2,16,4]{1,2,0:T(4,128)} %param.13) | copy-start | bytes 1540
  2.0 2.0 %collective-permute-start = (f32[256,1]{1,0:T(8,128)S(1)}, f32[256,1]{1,0:T(8,128)S(1)}, u32[]{:S(2)}, u32[]{:S(2)}) collective-permute-start(f32[256,1]{1,0:T(8,128)S(1)} %get-tuple-element.42.sums_ref), channel_id=1, source_target_pairs={{0,1},{1,0},{2,3},{3,2},{4,5},{5,4},{6,7},{7,6},{8,9},{9,8},{10,11... | collective-permute-start | bytes 3080 | tf_op jit(solution)/shard_map/ppermute | solution.py:553
  2.7 7.4 %collective-permute-start.3 = (bf16[128,640]{1,0:T(8,128)(2,1)S(1)}, bf16[128,640]{1,0:T(8,128)(2,1)S(1)}, u32[]{:S(2)}, u32[]{:S(2)}) collective-permute-start(bf16[128,640]{1,0:T(8,128)(2,1)S(1)} %get-tuple-element.45), channel_id=1, source_target_pairs={{0,16},{16,0},{1,17},{17,1},{2,18},{18,2},{3,19},{19,3},{4,20},{20... | collective-permute-start | bytes 491528 | tf_op jit(solution)/shard_map/ppermute | solution.py:552
  4.2 7.8 %collective-permute-start.2 = (bf16[128,640]{1,0:T(8,128)(2,1)S(1)}, bf16[128,640]{1,0:T(8,128)(2,1)S(1)}, u32[]{:S(2)}, u32[]{:S(2)}) collective-permute-start(bf16[128,640]{1,0:T(8,128)(2,1)S(1)} %get-tuple-element.44), channel_id=1, source_target_pairs={{0,16},{16,0},{1,17},{17,1},{2,18},{18,2},{3,19},{19,3},{4,20},{20... | collective-permute-start | bytes 491528 | tf_op jit(solution)/shard_map/ppermute | solution.py:559
  5.3 6.8 %collective-permute-start.4 = (bf16[128,640]{1,0:T(8,128)(2,1)S(1)}, bf16[128,640]{1,0:T(8,128)(2,1)S(1)}, u32[]{:S(2)}, u32[]{:S(2)}) collective-permute-start(bf16[128,640]{1,0:T(8,128)(2,1)S(1)} %get-tuple-element.46), channel_id=1, source_target_pairs={{0,2},{4,6},{8,10},{12,14},{2,0},{6,4},{10,8},{14,12},{1,3},{5,7},... | collective-permute-start | bytes 491528 | tf_op jit(solution)/shard_map/ppermute | solution.py:558
  5.5 13.6 %collective-permute-start.6 = (bf16[256,640]{1,0:T(8,128)(2,1)S(1)}, bf16[256,640]{1,0:T(8,128)(2,1)S(1)}, u32[]{:S(2)}, u32[]{:S(2)}) collective-permute-start(bf16[256,640]{1,0:T(8,128)(2,1)S(1)} %get-tuple-element.49), channel_id=1, source_target_pairs={{0,16},{16,0},{1,17},{17,1},{2,18},{18,2},{3,19},{19,3},{4,20},{20... | collective-permute-start | bytes 983048 | tf_op jit(solution)/shard_map/ppermute | solution.py:560
  6.0 11.3 %collective-permute-start.1 = (bf16[128,640]{1,0:T(8,128)(2,1)S(1)}, bf16[128,640]{1,0:T(8,128)(2,1)S(1)}, u32[]{:S(2)}, u32[]{:S(2)}) collective-permute-start(bf16[128,640]{1,0:T(8,128)(2,1)S(1)} %get-tuple-element.43), channel_id=1, source_target_pairs={{2,4},{6,8},{10,12},{4,2},{8,6},{12,10},{3,5},{7,9},{11,13},{5,3},... | collective-permute-start | bytes 491528 | tf_op jit(solution)/shard_map/ppermute | solution.py:561
  12.0 5.2 %collective-permute-start.7 = (bf16[128,640]{1,0:T(8,128)(2,1)S(1)}, bf16[128,640]{1,0:T(8,128)(2,1)S(1)}, u32[]{:S(2)}, u32[]{:S(2)}) collective-permute-start(bf16[128,640]{1,0:T(8,128)(2,1)S(1)} %shard_map.96.earlier_ref), channel_id=1, source_target_pairs={{0,2},{4,6},{8,10},{12,14},{2,0},{6,4},{10,8},{14,12},{1,3},{5,7},... | collective-permute-start | bytes 491528 | tf_op jit(solution)/shard_map/ppermute | solution.py:563
  13.1 9.8 %collective-permute-start.5 = (bf16[128,640]{1,0:T(8,128)(2,1)S(1)}, bf16[128,640]{1,0:T(8,128)(2,1)S(1)}, u32[]{:S(2)}, u32[]{:S(2)}) collective-permute-start(bf16[128,640]{1,0:T(8,128)(2,1)S(1)} %get-tuple-element.47), channel_id=1, source_target_pairs={{2,4},{6,8},{10,12},{4,2},{8,6},{12,10},{3,5},{7,9},{11,13},{5,3},... | collective-permute-start | bytes 491528 | tf_op jit(solution)/shard_map/ppermute | solution.py:570
  20.5 11.7 %collective-permute-start.8 = (bf16[144,640]{1,0:T(8,128)(2,1)S(1)}, bf16[144,640]{1,0:T(8,128)(2,1)S(1)}, u32[]{:S(2)}, u32[]{:S(2)}) collective-permute-start(bf16[144,640]{1,0:T(8,128)(2,1)S(1)} %get-tuple-element.54), channel_id=1, source_target_pairs={{0,2},{4,6},{8,10},{12,14},{2,0},{6,4},{10,8},{14,12},{1,3},{5,7},... | collective-permute-start | bytes 552968 | tf_op jit(solution)/shard_map/ppermute | solution.py:578
  20.8 11.4 %collective-permute-start.9 = (bf16[144,640]{1,0:T(8,128)(2,1)S(1)}, bf16[144,640]{1,0:T(8,128)(2,1)S(1)}, u32[]{:S(2)}, u32[]{:S(2)}) collective-permute-start(bf16[144,640]{1,0:T(8,128)(2,1)S(1)} %get-tuple-element.55), channel_id=1, source_target_pairs={{0,18},{4,22},{8,26},{12,30},{2,16},{6,20},{10,24},{14,28},{16,2},... | collective-permute-start | bytes 552968 | tf_op jit(solution)/shard_map/ppermute | solution.py:579
  24.4 7.1 %collective-permute-start.12 = (bf16[128,640]{1,0:T(8,128)(2,1)S(1)}, bf16[128,640]{1,0:T(8,128)(2,1)S(1)}, u32[]{:S(2)}, u32[]{:S(2)}) collective-permute-start(bf16[128,640]{1,0:T(8,128)(2,1)S(1)} %get-tuple-element.61), channel_id=1, source_target_pairs={{2,4},{6,8},{10,12},{4,2},{8,6},{12,10},{3,5},{7,9},{11,13},{5,3},... | collective-permute-start | bytes 491528 | tf_op jit(solution)/shard_map/ppermute | solution.py:587
  27.5 11.1 %collective-permute-start.11 = (bf16[256,640]{1,0:T(8,128)(2,1)S(1)}, bf16[256,640]{1,0:T(8,128)(2,1)S(1)}, u32[]{:S(2)}, u32[]{:S(2)}) collective-permute-start(bf16[256,640]{1,0:T(8,128)(2,1)S(1)} %get-tuple-element.58), channel_id=1, source_target_pairs={{0,16},{16,0},{1,17},{17,1},{2,18},{18,2},{3,19},{19,3},{4,20},{20... | collective-permute-start | bytes 983048 | tf_op jit(solution)/shard_map/ppermute | solution.py:588
  27.8 7.2 %collective-permute-start.10 = (bf16[128,640]{1,0:T(8,128)(2,1)S(1)}, bf16[128,640]{1,0:T(8,128)(2,1)S(1)}, u32[]{:S(2)}, u32[]{:S(2)}) collective-permute-start(bf16[128,640]{1,0:T(8,128)(2,1)S(1)} %get-tuple-element.57), channel_id=1, source_target_pairs={{2,4},{6,8},{10,12},{4,2},{8,6},{12,10},{3,5},{7,9},{11,13},{5,3},... | collective-permute-start | bytes 491528 | tf_op jit(solution)/shard_map/ppermute | solution.py:589
  31.5 7.1 %collective-permute-start.13 = (bf16[128,640]{1,0:T(8,128)(2,1)S(1)}, bf16[128,640]{1,0:T(8,128)(2,1)S(1)}, u32[]{:S(2)}, u32[]{:S(2)}) collective-permute-start(bf16[128,640]{1,0:T(8,128)(2,1)S(1)} %shard_map.101), channel_id=1, source_target_pairs={{0,16},{16,0},{1,17},{17,1},{2,18},{18,2},{3,19},{19,3},{4,20},{20... | collective-permute-start | bytes 491528 | tf_op jit(solution)/shard_map/ppermute | solution.py:596
  39.6 3.6 %collective-permute-start.14 = (f32[256,1]{1,0:T(8,128)S(1)}, f32[256,1]{1,0:T(8,128)S(1)}, u32[]{:S(2)}, u32[]{:S(2)}) collective-permute-start(f32[256,1]{1,0:T(8,128)S(1)} %get-tuple-element.65.sums_ref), channel_id=1, source_target_pairs={{0,1},{1,0},{2,3},{3,2},{4,5},{5,4},{6,7},{7,6},{8,9},{9,8},{10,11... | collective-permute-start | bytes 3080 | tf_op jit(solution)/shard_map/ppermute | solution.py:612

commit v6 on v5

--- a/solution.py
+++ b/solution.py
@@ -474,7 +474,6 @@
     swap_last_ref,
     gated_q_ref,
     gated_k_ref,
-    grad_v_ref,
     sums_ref,
 ):
     tokens, feat_dev = q_ref.shape
@@ -489,32 +488,71 @@
         gated_q_ref[rows, theirs] = gain_q_ref[:, theirs] * term(swap_first_ref, index)
     gated_k_ref[near, mine] = gain_k_ref[:, mine] * term(near_ref, 0)
     gated_k_ref[far, mine] = gain_k_ref[:, mine] * (term(own_ref, 3) + term(far_ref, 0))
-    grad_v_ref[near, mine] = term(near_ref, 1).astype(BF16)
-    grad_v_ref[far, mine] = (term(own_ref, 5) + term(far_ref, 1)).astype(BF16)
     near_dk = term(swap_first_ref, 2) + term(swap_near_ref, 0)
-    near_dv = term(swap_first_ref, 3) + term(swap_near_ref, 1)
     gated_k_ref[near, theirs] = gain_k_ref[:, theirs] * near_dk
     gated_k_ref[far, theirs] = gain_k_ref[:, theirs] * term(swap_last_ref, 0)
-    grad_v_ref[near, theirs] = near_dv.astype(BF16)
-    grad_v_ref[far, theirs] = swap_last_ref[width:]
     sums_ref[:tokens] = jnp.sum(q_ref[...].astype(F32) * gated_q_ref[...], -1, keepdims=True)
     sums_ref[tokens:] = jnp.sum(k_ref[...].astype(F32) * gated_k_ref[...], -1, keepdims=True)
 
 
+def value_kernel(
+    width,
+    own_ref,
+    near_ref,
+    far_ref,
+    swap_first_ref,
+    swap_near_ref,
+    swap_last_ref,
+    earlier_ref,
+    out_ref,
+):
+    mine, theirs = halves(out_ref.shape[1] // 2)
+    near, far = sides(width)
+
+    def term(ref, index):
+        return ref[index * width : (index + 1) * width].astype(F32)
+
+    out_ref[near, mine] = term(near_ref, 1).astype(BF16)
+    out_ref[far, mine] = (term(own_ref, 5) + term(far_ref, 1)).astype(BF16)
+    near_dv = term(swap_first_ref, 3) + term(swap_near_ref, 1)
+    out_ref[near, theirs] = near_dv.astype(BF16)
+    out_ref[far, theirs] = swap_last_ref[width:]
+
+
 def finish_kernel(
-    q_ref, k_ref, gated_q_ref, gated_k_ref, scale_ref, sums_ref, peer_ref, grad_q_ref, grad_k_ref
+    q_ref,
+    k_ref,
+    gated_q_ref,
+    gated_k_ref,
+    scale_ref,
+    sums_ref,
+    peer_ref,
+    grad_q_out,
+    grad_k_out,
+    grad_q_ref,
+    grad_k_ref,
+    sems,
 ):
     tokens = q_ref.shape[0]
     features = HEADS * HD
-    scale = scale_ref[...]
-    slope = scale * scale * scale * (sums_ref[...] + peer_ref[...]) / features
-    for rows, pre_ref, gated_ref, out_ref in (
-        (slice(0, tokens), q_ref, gated_q_ref, grad_q_ref),
-        (slice(tokens, 2 * tokens), k_ref, gated_k_ref, grad_k_ref),
+    half = tokens // 2
+    copies = []
+    for base, pre_ref, gated_ref, out_ref, out in (
+        (0, q_ref, gated_q_ref, grad_q_ref, grad_q_out),
+        (tokens, k_ref, gated_k_ref, grad_k_ref, grad_k_out),
     ):
-        out_ref[...] = (
-            scale[rows] * gated_ref[...] - pre_ref[...].astype(F32) * slope[rows]
-        ).astype(BF16)
+        for start in (0, half):
+            rows, at = (slice(start, start + half), slice(base + start, base + start + half))
+            scale = scale_ref[at]
+            slope = scale * scale * scale * (sums_ref[at] + peer_ref[at]) / features
+            out_ref[rows] = (
+                scale * gated_ref[rows] - pre_ref[rows].astype(F32) * slope
+            ).astype(BF16)
+            copy = pltpu.make_async_copy(out_ref.at[rows], out.at[rows], sems.at[len(copies)])
+            copy.start()
+            copies.append(copy)
+    for copy in copies:
+        copy.wait()
 
 
 def swapped_device(q_pre, k_pre, values, target, gain_q, gain_k, kept):
@@ -594,23 +632,19 @@
     )(own_total, near_total, swap_near_total)
     last_out = call(add_kernel, edge, flops=1, moved=1)(last_terms, far_terms)
     swap_last = lax.ppermute(last_out, "frame", SWAP)
-    gated_q, gated_k, grad_v, sum_terms = call(
+    terms = (own_total, near_total, far_total, swap_first, swap_near_total, swap_last)
+    gated_q, gated_k, sum_terms = call(
         functools.partial(gather_kernel, width),
-        (shape(tokens, feat_dev, F32),) * 2 + (block, sum_pair),
+        (shape(tokens, feat_dev, F32),) * 2 + (sum_pair,),
+    )(q_all, k_all, gain_q, gain_k, *terms)
+    sum_peer = lax.ppermute(sum_terms, "head", SWAP)
+    grad_v = call(functools.partial(value_kernel, width), block)(*terms, sum_terms)
+    grad_q, grad_k = call(
+        finish_kernel,
+        (block, block),
+        out_specs=[pl.BlockSpec(memory_space=pltpu.HBM)] * 2,
+        scratch_shapes=[pltpu.VMEM((tokens, feat_dev), BF16)] * 2 + [pltpu.SemaphoreType.DMA((4,))],
     )(
-        q_all,
-        k_all,
-        gain_q,
-        gain_k,
-        own_total,
-        near_total,
-        far_total,
-        swap_first,
-        swap_near_total,
-        swap_last,
-    )
-    sum_peer = lax.ppermute(sum_terms, "head", SWAP)
-    grad_q, grad_k = call(finish_kernel, (block, block))(
         q_all, k_all, gated_q, gated_k, scale, sum_terms, sum_peer
     )
     return tuple(

time: 44.4 us -> 43.7 us (0.984)
  waiting for transfers between devices: 11.6 us -> 10.8 us
    ppermute x1, waiting for transfers between devices: 0.99 us -> 0.21 us  [swapped_device(): sum_peer = lax.ppermute(sum_terms, 'head', SWAP)]
    pallas_call x1 -> x2, Pallas kernels: 1.04 us -> 1.76 us  [the longest x1 0.98 us: swapped_device(): call(finish_kernel, (block, block), out_specs=[pl.BlockSpec(memory_space=...]
    pallas_call x1, Pallas kernels: 0.98 us -> 0.32 us  [swapped_device(): call(functools.partial(gather_kernel, width), (shape(tokens, feat_dev, F3...]
  transfers between devices with their start and end apart: 15 -> 15, of which waited for: 6 -> 6; matrix products, arithmetic and copies ran while one was open for 0% -> 0% of each run, Pallas kernels for 9% -> 11%
where the time goes in v6:
time: 43.7 us; the launch traced here: 43.5 us
  starting transfers between devices  24.7 us (57%)
  waiting for transfers between devices  10.8 us (25%)
  Pallas kernels  7.33 us (17%)
  between operations  0.75 us (2%)
    ppermute x1, starting transfers between devices, swapped_device(): swap_far_in = lax.ppermute(relay_far, 'row', far)  4.16 us
    ppermute x1, starting transfers between devices, swapped_device(): far_in = lax.ppermute(far_out, 'row', far)  4.15 us
    ppermute x1, waiting for transfers between devices, swapped_device(): swap_last = lax.ppermute(last_out, 'frame', SWAP)  3.6 us
    ppermute x1, starting transfers between devices, swapped_device(): far_terms = lax.ppermute(swap_far_out, 'row', far)  3.15 us
    ppermute x1, starting transfers between devices, swapped_device(): far_total = lax.ppermute(far_out, 'row', far)  3.02 us
    ppermute x1, waiting for transfers between devices, swapped_device(): far_total = lax.ppermute(far_out, 'row', far)  2.75 us
    ppermute x1, starting transfers between devices, swapped_device(): sum_peer = lax.ppermute(sum_terms, 'head', SWAP)  2.65 us
    ppermute x1, starting transfers between devices, swapped_device(): swap_near_total = lax.ppermute(swap_near_out, ('frame', 'row'), swap_near)  2.17 us
  transfers between devices with their start and end apart: 15, of which 6 were waited for; matrix products, arithmetic and copies ran while one was open for 0% of the time, Pallas kernels for 11%

profile of v6, /device:TPU:13, one launch (start us, length us, event | category | flops | bytes accessed | tf_op | source)
XLA Modules:
  0.0 43.5 jit_solution(12400928639486933354)
XLA Ops:
  0.6 0.0 copy-start
  0.6 1.3 %shard_map.94 = (bf16[128,1280]{1,0:T(8,128)(2,1)S(1)}, bf16[128,1280]{1,0:T(8,128)(2,1)S(1)}, bf16[128,1280]{1,0:T(8,128)(2,1)S(1)}, bf16[128,1280]{1,0:T(8,128...) custom-call(bf16[128,1280]{1,0:T(8,128)(2,1)} %bitcast.9, ...), custom_call_target="tpu_custom_call" | custom-call | flops 1000000 | bytes 1000000 | tf_op jit(solution)/shard_map/pallas_call | solution.py:584
  2.0 0.7 %collective-permute-start = (f32[256,1]{1,0:T(8,128)S(1)}, f32[256,1]{1,0:T(8,128)S(1)}, u32[]{:S(2)}, u32[]{:S(2)}) collective-permute-start(f32[256,1]{1,0:T(8,128)S(1)} %get-tuple-element.41.sums_ref), channel_id=1, source_target_pairs={{0,1},{1,0},{2,3},{3,2},{4,5},{5,4},{6,7},{7,6},{8,9},{9,8},{10,11... | collective-permute-start | bytes 3080 | tf_op jit(solution)/shard_map/ppermute | solution.py:591
  2.7 1.2 %collective-permute-start.3 = (bf16[128,640]{1,0:T(8,128)(2,1)S(1)}, bf16[128,640]{1,0:T(8,128)(2,1)S(1)}, u32[]{:S(2)}, u32[]{:S(2)}) collective-permute-start(bf16[128,640]{1,0:T(8,128)(2,1)S(1)} %get-tuple-element.44), channel_id=1, source_target_pairs={{0,16},{16,0},{1,17},{17,1},{2,18},{18,2},{3,19},{19,3},{4,20},{20... | collective-permute-start | bytes 491528 | tf_op jit(solution)/shard_map/ppermute | solution.py:590
  4.0 0.0 collective-permute-done.peer_ref
  4.0 0.3 shard_map.95
  4.2 1.0 %collective-permute-start.2 = (bf16[128,640]{1,0:T(8,128)(2,1)S(1)}, bf16[128,640]{1,0:T(8,128)(2,1)S(1)}, u32[]{:S(2)}, u32[]{:S(2)}) collective-permute-start(bf16[128,640]{1,0:T(8,128)(2,1)S(1)} %get-tuple-element.43), channel_id=1, source_target_pairs={{0,16},{16,0},{1,17},{17,1},{2,18},{18,2},{3,19},{19,3},{4,20},{20... | collective-permute-start | bytes 491528 | tf_op jit(solution)/shard_map/ppermute | solution.py:597
  5.3 0.2 collective-permute-start.4
  5.5 0.5 %collective-permute-start.6 = (bf16[256,640]{1,0:T(8,128)(2,1)S(1)}, bf16[256,640]{1,0:T(8,128)(2,1)S(1)}, u32[]{:S(2)}, u32[]{:S(2)}) collective-permute-start(bf16[256,640]{1,0:T(8,128)(2,1)S(1)} %get-tuple-element.48), channel_id=1, source_target_pairs={{0,16},{16,0},{1,17},{17,1},{2,18},{18,2},{3,19},{19,3},{4,20},{20... | collective-permute-start | bytes 983048 | tf_op jit(solution)/shard_map/ppermute | solution.py:598
  6.0 4.1 %collective-permute-start.1 = (bf16[128,640]{1,0:T(8,128)(2,1)S(1)}, bf16[128,640]{1,0:T(8,128)(2,1)S(1)}, u32[]{:S(2)}, u32[]{:S(2)}) collective-permute-start(bf16[128,640]{1,0:T(8,128)(2,1)S(1)} %get-tuple-element.42), channel_id=1, source_target_pairs={{2,4},{6,8},{10,12},{4,2},{8,6},{12,10},{3,5},{7,9},{11,13},{5,3},... | collective-permute-start | bytes 491528 | tf_op jit(solution)/shard_map/ppermute | solution.py:599
  10.1 0.0 collective-permute-done.3.v_ref.swap_v_ref
  10.1 1.9 %collective-permute-done.2.k_ref.swap_k_ref = bf16[128,640]{1,0:T(8,128)(2,1)S(1)} collective-permute-done((bf16[128,640]{1,0:T(8,128)(2,1)S(1)}, bf16[128,640]{1,0:T(8,128)(2,1)S(1)}, u32[]{:S(2)}, u32[]{:S(2)}) %collective-permute-start.2) | collective-permute-done | bytes 163872 | tf_op jit(solution)/shard_map/ppermute | solution.py:597
  12.0 0.0 collective-permute-done.4.earlier_ref.halo_ref
  12.0 0.3 collective-permute-start.7
  12.3 0.0 copy-done
  12.3 0.7 %shard_map.97 = (bf16[128,640]{1,0:T(8,128)(2,1)S(1)}, f32[384,128]{1,0:T(8,128)S(1)}, f32[384,128]{1,0:T(8,128)S(1)}) custom-call(s32[2,4,16]{2,1,0:T(4,128)S(1)} %bitcast.8, bf16[128,640]{1,0:T(8,128)(2,1)S(1)} %collective-permute-done.2.k_ref.swap_k_ref, bf16[128,640]{1,0:T(8,128)(2,1)S(1)} %collective-permute-done.3.v_ref.swap_v_ref, ...), custom_call_target="tpu_custom_call" | custom-call | flops 1000000 | bytes 1000000 | tf_op jit(solution)/shard_map/pallas_call | solution.py:602
  13.1 4.2 %collective-permute-start.5 = (bf16[128,640]{1,0:T(8,128)(2,1)S(1)}, bf16[128,640]{1,0:T(8,128)(2,1)S(1)}, u32[]{:S(2)}, u32[]{:S(2)}) collective-permute-start(bf16[128,640]{1,0:T(8,128)(2,1)S(1)} %get-tuple-element.46), channel_id=1, source_target_pairs={{2,4},{6,8},{10,12},{4,2},{8,6},{12,10},{3,5},{7,9},{11,13},{5,3},... | collective-permute-start | bytes 491528 | tf_op jit(solution)/shard_map/ppermute | solution.py:608
  17.2 0.0 collective-permute-done.1.earlier_ref.halo_ref
  17.3 0.0 collective-permute-done.7.swap_halo_ref
  17.3 1.8 %collective-permute-done.6.swap_qt_ref = bf16[256,640]{1,0:T(8,128)(2,1)S(1)} collective-permute-done((bf16[256,640]{1,0:T(8,128)(2,1)S(1)}, bf16[256,640]{1,0:T(8,128)(2,1)S(1)}, u32[]{:S(2)}, u32[]{:S(2)}) %collective-permute-start.6) | collective-permute-done | bytes 327712 | tf_op jit(solution)/shard_map/ppermute | solution.py:598
  19.0 1.4 %shard_map.98 = (bf16[144,640]{1,0:T(8,128)(2,1)S(1)}, bf16[144,640]{1,0:T(8,128)(2,1)S(1)}, f32[640,640]{1,0:T(8,128)S(1)}) custom-call(bf16[128,640]{1,0:T(8,128)(2,1)S(1)} %collective-permute-done.4.earlier_ref.halo_ref, bf16[128,640]{1,0:T(8,128)(2,1)S(1)} %collective-permute-done.7.swap_halo_ref, bf16[256,640]{1,0:T(8,128)(2,1)S(1)} %get-tuple-element.47.own_ref, ...), custom_call_target="tpu_custom_call" | custom-call | flops 500000000 | bytes 2000000 | tf_op jit(solution)/shard_map/pallas_call | solution.py:610
  20.5 0.3 collective-permute-start.8
  20.8 2.2 %collective-permute-start.9 = (bf16[144,640]{1,0:T(8,128)(2,1)S(1)}, bf16[144,640]{1,0:T(8,128)(2,1)S(1)}, u32[]{:S(2)}, u32[]{:S(2)}) collective-permute-start(bf16[144,640]{1,0:T(8,128)(2,1)S(1)} %get-tuple-element.54), channel_id=1, source_target_pairs={{0,18},{4,22},{8,26},{12,30},{2,16},{6,20},{10,24},{14,28},{16,2},... | collective-permute-start | bytes 552968 | tf_op jit(solution)/shard_map/ppermute | solution.py:617
  22.9 0.0 collective-permute-done.5.swap_halo_ref
  22.9 1.4 %shard_map.99 = (bf16[128,640]{1,0:T(8,128)(2,1)S(1)}, bf16[128,640]{1,0:T(8,128)(2,1)S(1)}, f32[384,640]{1,0:T(8,128)S(1)}, bf16[256,640]{1,0:T(8,128)(2,1)S(1)}, f32[128,640]{1,0:T(8,128)S(1)}) custom-call(bf16[128,640]{1,0:T(8,128)(2,1)S(1)} %collective-permute-done.1.earlier_ref.halo_ref, bf16[128,640]{1,0:T(8,128)(2,1)S(1)} %collective-permute-done.5.swap_halo_ref, ...), custom_call_target="tpu_custom_call" | custom-call | flops 500000000 | bytes 2000000 | tf_op jit(solution)/shard_map/pallas_call | solution.py:618
  24.3 3.1 %collective-permute-start.12 = (bf16[128,640]{1,0:T(8,128)(2,1)S(1)}, bf16[128,640]{1,0:T(8,128)(2,1)S(1)}, u32[]{:S(2)}, u32[]{:S(2)}) collective-permute-start(bf16[128,640]{1,0:T(8,128)(2,1)S(1)} %get-tuple-element.60), channel_id=1, source_target_pairs={{2,4},{6,8},{10,12},{4,2},{8,6},{12,10},{3,5},{7,9},{11,13},{5,3},... | collective-permute-start | bytes 491528 | tf_op jit(solution)/shard_map/ppermute | solution.py:625
  27.5 0.3 collective-permute-start.11
  27.8 3.0 %collective-permute-start.10 = (bf16[128,640]{1,0:T(8,128)(2,1)S(1)}, bf16[128,640]{1,0:T(8,128)(2,1)S(1)}, u32[]{:S(2)}, u32[]{:S(2)}) collective-permute-start(bf16[128,640]{1,0:T(8,128)(2,1)S(1)} %get-tuple-element.56), channel_id=1, source_target_pairs={{2,4},{6,8},{10,12},{4,2},{8,6},{12,10},{3,5},{7,9},{11,13},{5,3},... | collective-permute-start | bytes 491528 | tf_op jit(solution)/shard_map/ppermute | solution.py:627
  30.8 0.6 %collective-permute-done.12.b_ref = bf16[128,640]{1,0:T(8,128)(2,1)S(1)} collective-permute-done((bf16[128,640]{1,0:T(8,128)(2,1)S(1)}, bf16[128,640]{1,0:T(8,128)(2,1)S(1)}, u32[]{:S(2)}, u32[]{:S(2)}) %collective-permute-start.12) | collective-permute-done | bytes 163872 | tf_op jit(solution)/shard_map/ppermute | solution.py:625
  31.4 0.7 %collective-permute-start.13 = (bf16[128,640]{1,0:T(8,128)(2,1)S(1)}, bf16[128,640]{1,0:T(8,128)(2,1)S(1)}, u32[]{:S(2)}, u32[]{:S(2)}) collective-permute-start(bf16[128,640]{1,0:T(8,128)(2,1)S(1)} %shard_map.101), channel_id=1, source_target_pairs={{0,16},{16,0},{1,17},{17,1},{2,18},{18,2},{3,19},{19,3},{4,20},{20... | collective-permute-start | bytes 491528 | tf_op jit(solution)/shard_map/ppermute | solution.py:634
  32.2 0.0 collective-permute-done.8.near_ref
  32.2 0.0 collective-permute-done.9.swap_near_ref
  32.2 0.1 shard_map.100
  32.2 2.8 %collective-permute-done.10.far_ref = bf16[128,640]{1,0:T(8,128)(2,1)S(1)} collective-permute-done((bf16[128,640]{1,0:T(8,128)(2,1)S(1)}, bf16[128,640]{1,0:T(8,128)(2,1)S(1)}, u32[]{:S(2)}, u32[]{:S(2)}) %collective-permute-start.10) | collective-permute-done | bytes 163872 | tf_op jit(solution)/shard_map/ppermute | solution.py:627
  35.0 3.6 %collective-permute-done.13.swap_last_ref = bf16[128,640]{1,0:T(8,128)(2,1)S(1)} collective-permute-done((bf16[128,640]{1,0:T(8,128)(2,1)S(1)}, bf16[128,640]{1,0:T(8,128)(2,1)S(1)}, u32[]{:S(2)}, u32[]{:S(2)}) %collective-permute-start.13) | collective-permute-done | bytes 163872 | tf_op jit(solution)/shard_map/ppermute | solution.py:634
  38.6 0.0 collective-permute-done.11.swap_first_ref
  38.6 0.3 shard_map.102
  38.9 2.7 %collective-permute-start.14 = (f32[256,1]{1,0:T(8,128)S(1)}, f32[256,1]{1,0:T(8,128)S(1)}, u32[]{:S(2)}, u32[]{:S(2)}) collective-permute-start(f32[256,1]{1,0:T(8,128)S(1)} %get-tuple-element.64.sums_ref.earlier_ref), channel_id=1, source_target_pairs={{0,1},{1,0},{2,3},{3,2},{4,5},{5,4},{6,7},{7,6},{8,9},{9,8},{10,11... | collective-permute-start | bytes 3080 | tf_op jit(solution)/shard_map/ppermute | solution.py:640
  41.6 0.8 %shard_map.104 = bf16[128,1280]{1,0:T(8,128)(2,1)} custom-call(f32[384,640]{1,0:T(8,128)S(1)} %get-tuple-element.52.own_ref, f32[128,640]{1,0:T(8,128)S(1)} %get-tuple-element.55.near_ref, bf16[128,640]{1,0:T(8,128)(2,1)S(1)} %collective-permute-done.10.far_ref, bf16[256,640]{1,0:T(8,128)(2,1)S(1)} %collective-permute-done.11.swap_first_ref, ...), custom_call_target="tpu_custom_call" | custom-call | flops 1000000 | bytes 1000000 | tf_op jit(solution)/shard_map/pallas_call | solution.py:641
  42.3 0.2 collective-permute-done.14.peer_ref
  42.6 1.0 %shard_map.103 = (bf16[128,1280]{1,0:T(8,128)(2,1)}, bf16[128,1280]{1,0:T(8,128)(2,1)}) custom-call(bf16[128,1280]{1,0:T(8,128)(2,1)S(1)} %get-tuple-element.35.q_ref, bf16[128,1280]{1,0:T(8,128)(2,1)S(1)} %get-tuple-element.36.k_ref, f32[128,1280]{1,0:T(8,128)S(1)} %get-tuple-element.61.gated_q_ref, f32[128,1280]{1,0:T(8,128)S(1)} %get-tuple-element.62.gated_k_ref, ...), custom_call_target="tpu_custom_call" | custom-call | flops 1000000 | bytes 1000000 | tf_op jit(solution)/shard_map/pallas_call | solution.py:642
  (2 shorter events, 0.0 us)
Async XLA Ops:
  0.6 11.7 %copy-start = (s32[2,16,4]{1,2,0:T(4,128)S(1)}, s32[2,16,4]{1,2,0:T(4,128)}, u32[]{:S(2)}) copy-start(s32[2,16,4]{1,2,0:T(4,128)} %param.13) | copy-start | bytes 1540
  2.0 2.0 %collective-permute-start = (f32[256,1]{1,0:T(8,128)S(1)}, f32[256,1]{1,0:T(8,128)S(1)}, u32[]{:S(2)}, u32[]{:S(2)}) collective-permute-start(f32[256,1]{1,0:T(8,128)S(1)} %get-tuple-element.41.sums_ref), channel_id=1, source_target_pairs={{0,1},{1,0},{2,3},{3,2},{4,5},{5,4},{6,7},{7,6},{8,9},{9,8},{10,11... | collective-permute-start | bytes 3080 | tf_op jit(solution)/shard_map/ppermute | solution.py:591
  2.7 7.4 %collective-permute-start.3 = (bf16[128,640]{1,0:T(8,128)(2,1)S(1)}, bf16[128,640]{1,0:T(8,128)(2,1)S(1)}, u32[]{:S(2)}, u32[]{:S(2)}) collective-permute-start(bf16[128,640]{1,0:T(8,128)(2,1)S(1)} %get-tuple-element.44), channel_id=1, source_target_pairs={{0,16},{16,0},{1,17},{17,1},{2,18},{18,2},{3,19},{19,3},{4,20},{20... | collective-permute-start | bytes 491528 | tf_op jit(solution)/shard_map/ppermute | solution.py:590
  4.2 7.8 %collective-permute-start.2 = (bf16[128,640]{1,0:T(8,128)(2,1)S(1)}, bf16[128,640]{1,0:T(8,128)(2,1)S(1)}, u32[]{:S(2)}, u32[]{:S(2)}) collective-permute-start(bf16[128,640]{1,0:T(8,128)(2,1)S(1)} %get-tuple-element.43), channel_id=1, source_target_pairs={{0,16},{16,0},{1,17},{17,1},{2,18},{18,2},{3,19},{19,3},{4,20},{20... | collective-permute-start | bytes 491528 | tf_op jit(solution)/shard_map/ppermute | solution.py:597
  5.3 6.8 %collective-permute-start.4 = (bf16[128,640]{1,0:T(8,128)(2,1)S(1)}, bf16[128,640]{1,0:T(8,128)(2,1)S(1)}, u32[]{:S(2)}, u32[]{:S(2)}) collective-permute-start(bf16[128,640]{1,0:T(8,128)(2,1)S(1)} %get-tuple-element.45), channel_id=1, source_target_pairs={{0,2},{4,6},{8,10},{12,14},{2,0},{6,4},{10,8},{14,12},{1,3},{5,7},... | collective-permute-start | bytes 491528 | tf_op jit(solution)/shard_map/ppermute | solution.py:596
  5.5 13.6 %collective-permute-start.6 = (bf16[256,640]{1,0:T(8,128)(2,1)S(1)}, bf16[256,640]{1,0:T(8,128)(2,1)S(1)}, u32[]{:S(2)}, u32[]{:S(2)}) collective-permute-start(bf16[256,640]{1,0:T(8,128)(2,1)S(1)} %get-tuple-element.48), channel_id=1, source_target_pairs={{0,16},{16,0},{1,17},{17,1},{2,18},{18,2},{3,19},{19,3},{4,20},{20... | collective-permute-start | bytes 983048 | tf_op jit(solution)/shard_map/ppermute | solution.py:598
  6.0 11.3 %collective-permute-start.1 = (bf16[128,640]{1,0:T(8,128)(2,1)S(1)}, bf16[128,640]{1,0:T(8,128)(2,1)S(1)}, u32[]{:S(2)}, u32[]{:S(2)}) collective-permute-start(bf16[128,640]{1,0:T(8,128)(2,1)S(1)} %get-tuple-element.42), channel_id=1, source_target_pairs={{2,4},{6,8},{10,12},{4,2},{8,6},{12,10},{3,5},{7,9},{11,13},{5,3},... | collective-permute-start | bytes 491528 | tf_op jit(solution)/shard_map/ppermute | solution.py:599
  12.0 5.2 %collective-permute-start.7 = (bf16[128,640]{1,0:T(8,128)(2,1)S(1)}, bf16[128,640]{1,0:T(8,128)(2,1)S(1)}, u32[]{:S(2)}, u32[]{:S(2)}) collective-permute-start(bf16[128,640]{1,0:T(8,128)(2,1)S(1)} %shard_map.96.earlier_ref), channel_id=1, source_target_pairs={{0,2},{4,6},{8,10},{12,14},{2,0},{6,4},{10,8},{14,12},{1,3},{5,7},... | collective-permute-start | bytes 491528 | tf_op jit(solution)/shard_map/ppermute | solution.py:601
  13.1 9.8 %collective-permute-start.5 = (bf16[128,640]{1,0:T(8,128)(2,1)S(1)}, bf16[128,640]{1,0:T(8,128)(2,1)S(1)}, u32[]{:S(2)}, u32[]{:S(2)}) collective-permute-start(bf16[128,640]{1,0:T(8,128)(2,1)S(1)} %get-tuple-element.46), channel_id=1, source_target_pairs={{2,4},{6,8},{10,12},{4,2},{8,6},{12,10},{3,5},{7,9},{11,13},{5,3},... | collective-permute-start | bytes 491528 | tf_op jit(solution)/shard_map/ppermute | solution.py:608
  20.5 11.7 %collective-permute-start.8 = (bf16[144,640]{1,0:T(8,128)(2,1)S(1)}, bf16[144,640]{1,0:T(8,128)(2,1)S(1)}, u32[]{:S(2)}, u32[]{:S(2)}) collective-permute-start(bf16[144,640]{1,0:T(8,128)(2,1)S(1)} %get-tuple-element.53), channel_id=1, source_target_pairs={{0,2},{4,6},{8,10},{12,14},{2,0},{6,4},{10,8},{14,12},{1,3},{5,7},... | collective-permute-start | bytes 552968 | tf_op jit(solution)/shard_map/ppermute | solution.py:616
  20.8 11.4 %collective-permute-start.9 = (bf16[144,640]{1,0:T(8,128)(2,1)S(1)}, bf16[144,640]{1,0:T(8,128)(2,1)S(1)}, u32[]{:S(2)}, u32[]{:S(2)}) collective-permute-start(bf16[144,640]{1,0:T(8,128)(2,1)S(1)} %get-tuple-element.54), channel_id=1, source_target_pairs={{0,18},{4,22},{8,26},{12,30},{2,16},{6,20},{10,24},{14,28},{16,2},... | collective-permute-start | bytes 552968 | tf_op jit(solution)/shard_map/ppermute | solution.py:617
  24.3 7.1 %collective-permute-start.12 = (bf16[128,640]{1,0:T(8,128)(2,1)S(1)}, bf16[128,640]{1,0:T(8,128)(2,1)S(1)}, u32[]{:S(2)}, u32[]{:S(2)}) collective-permute-start(bf16[128,640]{1,0:T(8,128)(2,1)S(1)} %get-tuple-element.60), channel_id=1, source_target_pairs={{2,4},{6,8},{10,12},{4,2},{8,6},{12,10},{3,5},{7,9},{11,13},{5,3},... | collective-permute-start | bytes 491528 | tf_op jit(solution)/shard_map/ppermute | solution.py:625
  27.5 11.1 %collective-permute-start.11 = (bf16[256,640]{1,0:T(8,128)(2,1)S(1)}, bf16[256,640]{1,0:T(8,128)(2,1)S(1)}, u32[]{:S(2)}, u32[]{:S(2)}) collective-permute-start(bf16[256,640]{1,0:T(8,128)(2,1)S(1)} %get-tuple-element.57), channel_id=1, source_target_pairs={{0,16},{16,0},{1,17},{17,1},{2,18},{18,2},{3,19},{19,3},{4,20},{20... | collective-permute-start | bytes 983048 | tf_op jit(solution)/shard_map/ppermute | solution.py:626
  27.8 7.2 %collective-permute-start.10 = (bf16[128,640]{1,0:T(8,128)(2,1)S(1)}, bf16[128,640]{1,0:T(8,128)(2,1)S(1)}, u32[]{:S(2)}, u32[]{:S(2)}) collective-permute-start(bf16[128,640]{1,0:T(8,128)(2,1)S(1)} %get-tuple-element.56), channel_id=1, source_target_pairs={{2,4},{6,8},{10,12},{4,2},{8,6},{12,10},{3,5},{7,9},{11,13},{5,3},... | collective-permute-start | bytes 491528 | tf_op jit(solution)/shard_map/ppermute | solution.py:627
  31.4 7.2 %collective-permute-start.13 = (bf16[128,640]{1,0:T(8,128)(2,1)S(1)}, bf16[128,640]{1,0:T(8,128)(2,1)S(1)}, u32[]{:S(2)}, u32[]{:S(2)}) collective-permute-start(bf16[128,640]{1,0:T(8,128)(2,1)S(1)} %shard_map.101), channel_id=1, source_target_pairs={{0,16},{16,0},{1,17},{17,1},{2,18},{18,2},{3,19},{19,3},{4,20},{20... | collective-permute-start | bytes 491528 | tf_op jit(solution)/shard_map/ppermute | solution.py:634
  38.9 3.6 %collective-permute-start.14 = (f32[256,1]{1,0:T(8,128)S(1)}, f32[256,1]{1,0:T(8,128)S(1)}, u32[]{:S(2)}, u32[]{:S(2)}) collective-permute-start(f32[256,1]{1,0:T(8,128)S(1)} %get-tuple-element.64.sums_ref.earlier_ref), channel_id=1, source_target_pairs={{0,1},{1,0},{2,3},{3,2},{4,5},{5,4},{6,7},{7,6},{8,9},{9,8},{10,11... | collective-permute-start | bytes 3080 | tf_op jit(solution)/shard_map/ppermute | solution.py:640

commit v7 on v6

--- a/solution.py
+++ b/solution.py
@@ -460,39 +460,45 @@
     out_ref[...] = (a_ref[...] + b_ref[...].astype(F32)).astype(BF16)
 
 
-def gather_kernel(
+def gather_q_kernel(
+    width, q_ref, gain_ref, own_ref, swap_first_ref, earlier_ref, gated_ref, sums_ref
+):
+    mine, theirs = halves(q_ref.shape[1] // 2)
+    for index, rows in enumerate(sides(width)):
+        at = slice(index * width, (index + 1) * width)
+        gated_ref[rows, mine] = gain_ref[:, mine] * own_ref[at]
+        gated_ref[rows, theirs] = gain_ref[:, theirs] * swap_first_ref[at].astype(F32)
+    sums_ref[...] = jnp.sum(q_ref[...].astype(F32) * gated_ref[...], -1, keepdims=True)
+
+
+def gather_k_kernel(
     width,
-    q_ref,
     k_ref,
-    gain_q_ref,
-    gain_k_ref,
+    gain_ref,
     own_ref,
     near_ref,
     far_ref,
     swap_first_ref,
     swap_near_ref,
     swap_last_ref,
-    gated_q_ref,
-    gated_k_ref,
+    sum_q_ref,
+    gated_ref,
     sums_ref,
 ):
-    tokens, feat_dev = q_ref.shape
-    mine, theirs = halves(feat_dev // 2)
+    tokens = k_ref.shape[0]
+    mine, theirs = halves(k_ref.shape[1] // 2)
     near, far = sides(width)
 
     def term(ref, index):
         return ref[index * width : (index + 1) * width].astype(F32)
 
-    for index, rows in enumerate((near, far)):
-        gated_q_ref[rows, mine] = gain_q_ref[:, mine] * term(own_ref, index)
-        gated_q_ref[rows, theirs] = gain_q_ref[:, theirs] * term(swap_first_ref, index)
-    gated_k_ref[near, mine] = gain_k_ref[:, mine] * term(near_ref, 0)
-    gated_k_ref[far, mine] = gain_k_ref[:, mine] * (term(own_ref, 3) + term(far_ref, 0))
+    gated_ref[near, mine] = gain_ref[:, mine] * term(near_ref, 0)
+    gated_ref[far, mine] = gain_ref[:, mine] * (term(own_ref, 3) + term(far_ref, 0))
     near_dk = term(swap_first_ref, 2) + term(swap_near_ref, 0)
-    gated_k_ref[near, theirs] = gain_k_ref[:, theirs] * near_dk
-    gated_k_ref[far, theirs] = gain_k_ref[:, theirs] * term(swap_last_ref, 0)
-    sums_ref[:tokens] = jnp.sum(q_ref[...].astype(F32) * gated_q_ref[...], -1, keepdims=True)
-    sums_ref[tokens:] = jnp.sum(k_ref[...].astype(F32) * gated_k_ref[...], -1, keepdims=True)
+    gated_ref[near, theirs] = gain_ref[:, theirs] * near_dk
+    gated_ref[far, theirs] = gain_ref[:, theirs] * term(swap_last_ref, 0)
+    sums_ref[:tokens] = sum_q_ref[...]
+    sums_ref[tokens:] = jnp.sum(k_ref[...].astype(F32) * gated_ref[...], -1, keepdims=True)
 
 
 def value_kernel(
@@ -633,10 +639,15 @@
     last_out = call(add_kernel, edge, flops=1, moved=1)(last_terms, far_terms)
     swap_last = lax.ppermute(last_out, "frame", SWAP)
     terms = (own_total, near_total, far_total, swap_first, swap_near_total, swap_last)
-    gated_q, gated_k, sum_terms = call(
-        functools.partial(gather_kernel, width),
-        (shape(tokens, feat_dev, F32),) * 2 + (sum_pair,),
-    )(q_all, k_all, gain_q, gain_k, *terms)
+    gated = shape(tokens, feat_dev, F32)
+    gated_q, sum_q = call(
+        functools.partial(gather_q_kernel, width),
+        (gated, shape(tokens, 1, F32)),
+        flops=3 * 10**9,
+    )(q_all, gain_q, own_total, swap_first, near_total)
+    gated_k, sum_terms = call(functools.partial(gather_k_kernel, width), (gated, sum_pair))(
+        k_all, gain_k, *terms, sum_q
+    )
     sum_peer = lax.ppermute(sum_terms, "head", SWAP)
     grad_v = call(functools.partial(value_kernel, width), block)(*terms, sum_terms)
     grad_q, grad_k = call(

time: 43.7 us -> 43.6 us (level)
    ppermute x1, waiting for transfers between devices: 0.01 us -> 2.84 us  [swapped_device(): swap_first = lax.ppermute(first_out, 'frame', SWAP)]
    ppermute x1, waiting for transfers between devices: 2.75 us -> 0.01 us  [swapped_device(): far_total = lax.ppermute(far_out, 'row', far)]
where the time goes in v7:
time: 43.6 us; the launch traced here: 43.4 us
  starting transfers between devices  24.7 us (57%)
  waiting for transfers between devices  10.6 us (24%)
  Pallas kernels  7.44 us (17%)
  between operations  0.75 us (2%)
    ppermute x1, starting transfers between devices, swapped_device(): swap_far_in = lax.ppermute(relay_far, 'row', far)  4.16 us
    ppermute x1, starting transfers between devices, swapped_device(): far_in = lax.ppermute(far_out, 'row', far)  4.15 us
    ppermute x1, waiting for transfers between devices, swapped_device(): swap_last = lax.ppermute(last_out, 'frame', SWAP)  3.31 us
    ppermute x1, starting transfers between devices, swapped_device(): far_terms = lax.ppermute(swap_far_out, 'row', far)  3.15 us
    ppermute x1, starting transfers between devices, swapped_device(): far_total = lax.ppermute(far_out, 'row', far)  3.02 us
    ppermute x1, waiting for transfers between devices, swapped_device(): swap_first = lax.ppermute(first_out, 'frame', SWAP)  2.84 us
    ppermute x1, starting transfers between devices, swapped_device(): sum_peer = lax.ppermute(sum_terms, 'head', SWAP)  2.65 us
    ppermute x1, starting transfers between devices, swapped_device(): swap_near_total = lax.ppermute(swap_near_out, ('frame', 'row'), swap_near)  2.17 us
  transfers between devices with their start and end apart: 15, of which 6 were waited for; matrix products, arithmetic and copies ran while one was open for 0% of the time, Pallas kernels for 11%

profile of v7, /device:TPU:13, one launch (start us, length us, event | category | flops | bytes accessed | tf_op | source)
XLA Modules:
  0.0 43.4 jit_solution(11149066426936276339)
XLA Ops:
  0.6 0.0 copy-start
  0.6 1.3 %shard_map.94 = (bf16[128,1280]{1,0:T(8,128)(2,1)S(1)}, bf16[128,1280]{1,0:T(8,128)(2,1)S(1)}, bf16[128,1280]{1,0:T(8,128)(2,1)S(1)}, bf16[128,1280]{1,0:T(8,128...) custom-call(bf16[128,1280]{1,0:T(8,128)(2,1)} %bitcast.9, ...), custom_call_target="tpu_custom_call" | custom-call | flops 1000000 | bytes 1000000 | tf_op jit(solution)/shard_map/pallas_call | solution.py:590
  2.0 0.7 %collective-permute-start = (f32[256,1]{1,0:T(8,128)S(1)}, f32[256,1]{1,0:T(8,128)S(1)}, u32[]{:S(2)}, u32[]{:S(2)}) collective-permute-start(f32[256,1]{1,0:T(8,128)S(1)} %get-tuple-element.41.sums_ref), channel_id=1, source_target_pairs={{0,1},{1,0},{2,3},{3,2},{4,5},{5,4},{6,7},{7,6},{8,9},{9,8},{10,11... | collective-permute-start | bytes 3080 | tf_op jit(solution)/shard_map/ppermute | solution.py:597
  2.7 1.2 %collective-permute-start.3 = (bf16[128,640]{1,0:T(8,128)(2,1)S(1)}, bf16[128,640]{1,0:T(8,128)(2,1)S(1)}, u32[]{:S(2)}, u32[]{:S(2)}) collective-permute-start(bf16[128,640]{1,0:T(8,128)(2,1)S(1)} %get-tuple-element.45), channel_id=1, source_target_pairs={{0,16},{16,0},{1,17},{17,1},{2,18},{18,2},{3,19},{19,3},{4,20},{20... | collective-permute-start | bytes 491528 | tf_op jit(solution)/shard_map/ppermute | solution.py:596
  4.0 0.0 collective-permute-done.peer_ref
  4.0 0.3 shard_map.95
  4.2 1.0 %collective-permute-start.2 = (bf16[128,640]{1,0:T(8,128)(2,1)S(1)}, bf16[128,640]{1,0:T(8,128)(2,1)S(1)}, u32[]{:S(2)}, u32[]{:S(2)}) collective-permute-start(bf16[128,640]{1,0:T(8,128)(2,1)S(1)} %get-tuple-element.44), channel_id=1, source_target_pairs={{0,16},{16,0},{1,17},{17,1},{2,18},{18,2},{3,19},{19,3},{4,20},{20... | collective-permute-start | bytes 491528 | tf_op jit(solution)/shard_map/ppermute | solution.py:603
  5.3 0.2 collective-permute-start.4
  5.5 0.5 %collective-permute-start.6 = (bf16[256,640]{1,0:T(8,128)(2,1)S(1)}, bf16[256,640]{1,0:T(8,128)(2,1)S(1)}, u32[]{:S(2)}, u32[]{:S(2)}) collective-permute-start(bf16[256,640]{1,0:T(8,128)(2,1)S(1)} %get-tuple-element.49), channel_id=1, source_target_pairs={{0,16},{16,0},{1,17},{17,1},{2,18},{18,2},{3,19},{19,3},{4,20},{20... | collective-permute-start | bytes 983048 | tf_op jit(solution)/shard_map/ppermute | solution.py:604
  6.0 4.1 %collective-permute-start.1 = (bf16[128,640]{1,0:T(8,128)(2,1)S(1)}, bf16[128,640]{1,0:T(8,128)(2,1)S(1)}, u32[]{:S(2)}, u32[]{:S(2)}) collective-permute-start(bf16[128,640]{1,0:T(8,128)(2,1)S(1)} %get-tuple-element.43), channel_id=1, source_target_pairs={{2,4},{6,8},{10,12},{4,2},{8,6},{12,10},{3,5},{7,9},{11,13},{5,3},... | collective-permute-start | bytes 491528 | tf_op jit(solution)/shard_map/ppermute | solution.py:605
  10.1 0.0 collective-permute-done.3.v_ref.swap_v_ref
  10.1 1.9 %collective-permute-done.2.k_ref.swap_k_ref = bf16[128,640]{1,0:T(8,128)(2,1)S(1)} collective-permute-done((bf16[128,640]{1,0:T(8,128)(2,1)S(1)}, bf16[128,640]{1,0:T(8,128)(2,1)S(1)}, u32[]{:S(2)}, u32[]{:S(2)}) %collective-permute-start.2) | collective-permute-done | bytes 163872 | tf_op jit(solution)/shard_map/ppermute | solution.py:603
  12.0 0.0 collective-permute-done.4.earlier_ref.halo_ref
  12.0 0.3 collective-permute-start.7
  12.3 0.0 copy-done
  12.3 0.7 %shard_map.97 = (bf16[128,640]{1,0:T(8,128)(2,1)S(1)}, f32[384,128]{1,0:T(8,128)S(1)}, f32[384,128]{1,0:T(8,128)S(1)}) custom-call(s32[2,4,16]{2,1,0:T(4,128)S(1)} %bitcast.8, bf16[128,640]{1,0:T(8,128)(2,1)S(1)} %collective-permute-done.2.k_ref.swap_k_ref, bf16[128,640]{1,0:T(8,128)(2,1)S(1)} %collective-permute-done.3.v_ref.swap_v_ref, ...), custom_call_target="tpu_custom_call" | custom-call | flops 1000000 | bytes 1000000 | tf_op jit(solution)/shard_map/pallas_call | solution.py:608
  13.1 4.2 %collective-permute-start.5 = (bf16[128,640]{1,0:T(8,128)(2,1)S(1)}, bf16[128,640]{1,0:T(8,128)(2,1)S(1)}, u32[]{:S(2)}, u32[]{:S(2)}) collective-permute-start(bf16[128,640]{1,0:T(8,128)(2,1)S(1)} %get-tuple-element.47), channel_id=1, source_target_pairs={{2,4},{6,8},{10,12},{4,2},{8,6},{12,10},{3,5},{7,9},{11,13},{5,3},... | collective-permute-start | bytes 491528 | tf_op jit(solution)/shard_map/ppermute | solution.py:614
  17.2 0.0 collective-permute-done.1.earlier_ref.halo_ref
  17.3 0.0 collective-permute-done.7.swap_halo_ref
  17.3 1.8 %collective-permute-done.6.swap_qt_ref = bf16[256,640]{1,0:T(8,128)(2,1)S(1)} collective-permute-done((bf16[256,640]{1,0:T(8,128)(2,1)S(1)}, bf16[256,640]{1,0:T(8,128)(2,1)S(1)}, u32[]{:S(2)}, u32[]{:S(2)}) %collective-permute-start.6) | collective-permute-done | bytes 327712 | tf_op jit(solution)/shard_map/ppermute | solution.py:604
  19.0 1.4 %shard_map.98 = (bf16[144,640]{1,0:T(8,128)(2,1)S(1)}, bf16[144,640]{1,0:T(8,128)(2,1)S(1)}, f32[640,640]{1,0:T(8,128)S(1)}) custom-call(bf16[128,640]{1,0:T(8,128)(2,1)S(1)} %collective-permute-done.4.earlier_ref.halo_ref, bf16[128,640]{1,0:T(8,128)(2,1)S(1)} %collective-permute-done.7.swap_halo_ref, bf16[256,640]{1,0:T(8,128)(2,1)S(1)} %get-tuple-element.48.own_ref, ...), custom_call_target="tpu_custom_call" | custom-call | flops 500000000 | bytes 2000000 | tf_op jit(solution)/shard_map/pallas_call | solution.py:616
  20.5 0.3 collective-permute-start.9
  20.8 2.2 %collective-permute-start.10 = (bf16[144,640]{1,0:T(8,128)(2,1)S(1)}, bf16[144,640]{1,0:T(8,128)(2,1)S(1)}, u32[]{:S(2)}, u32[]{:S(2)}) collective-permute-start(bf16[144,640]{1,0:T(8,128)(2,1)S(1)} %get-tuple-element.56), channel_id=1, source_target_pairs={{0,18},{4,22},{8,26},{12,30},{2,16},{6,20},{10,24},{14,28},{16,2},... | collective-permute-start | bytes 552968 | tf_op jit(solution)/shard_map/ppermute | solution.py:623
  22.9 0.0 collective-permute-done.5.swap_halo_ref
  22.9 1.4 %shard_map.99 = (bf16[128,640]{1,0:T(8,128)(2,1)S(1)}, bf16[128,640]{1,0:T(8,128)(2,1)S(1)}, f32[384,640]{1,0:T(8,128)S(1)}, bf16[256,640]{1,0:T(8,128)(2,1)S(1)}, f32[128,640]{1,0:T(8,128)S(1)}) custom-call(bf16[128,640]{1,0:T(8,128)(2,1)S(1)} %collective-permute-done.1.earlier_ref.halo_ref, bf16[128,640]{1,0:T(8,128)(2,1)S(1)} %collective-permute-done.5.swap_halo_ref, ...), custom_call_target="tpu_custom_call" | custom-call | flops 500000000 | bytes 2000000 | tf_op jit(solution)/shard_map/pallas_call | solution.py:624
  24.3 3.1 %collective-permute-start.12 = (bf16[128,640]{1,0:T(8,128)(2,1)S(1)}, bf16[128,640]{1,0:T(8,128)(2,1)S(1)}, u32[]{:S(2)}, u32[]{:S(2)}) collective-permute-start(bf16[128,640]{1,0:T(8,128)(2,1)S(1)} %get-tuple-element.62), channel_id=1, source_target_pairs={{2,4},{6,8},{10,12},{4,2},{8,6},{12,10},{3,5},{7,9},{11,13},{5,3},... | collective-permute-start | bytes 491528 | tf_op jit(solution)/shard_map/ppermute | solution.py:631
  27.5 0.3 collective-permute-start.8
  27.8 3.0 %collective-permute-start.11 = (bf16[128,640]{1,0:T(8,128)(2,1)S(1)}, bf16[128,640]{1,0:T(8,128)(2,1)S(1)}, u32[]{:S(2)}, u32[]{:S(2)}) collective-permute-start(bf16[128,640]{1,0:T(8,128)(2,1)S(1)} %get-tuple-element.59), channel_id=1, source_target_pairs={{2,4},{6,8},{10,12},{4,2},{8,6},{12,10},{3,5},{7,9},{11,13},{5,3},... | collective-permute-start | bytes 491528 | tf_op jit(solution)/shard_map/ppermute | solution.py:633
  30.8 0.6 %collective-permute-done.12.b_ref = bf16[128,640]{1,0:T(8,128)(2,1)S(1)} collective-permute-done((bf16[128,640]{1,0:T(8,128)(2,1)S(1)}, bf16[128,640]{1,0:T(8,128)(2,1)S(1)}, u32[]{:S(2)}, u32[]{:S(2)}) %collective-permute-start.12) | collective-permute-done | bytes 163872 | tf_op jit(solution)/shard_map/ppermute | solution.py:631
  31.4 0.7 %collective-permute-start.13 = (bf16[128,640]{1,0:T(8,128)(2,1)S(1)}, bf16[128,640]{1,0:T(8,128)(2,1)S(1)}, u32[]{:S(2)}, u32[]{:S(2)}) collective-permute-start(bf16[128,640]{1,0:T(8,128)(2,1)S(1)} %shard_map.102), channel_id=1, source_target_pairs={{0,16},{16,0},{1,17},{17,1},{2,18},{18,2},{3,19},{19,3},{4,20},{20... | collective-permute-start | bytes 491528 | tf_op jit(solution)/shard_map/ppermute | solution.py:640
  32.2 0.0 collective-permute-done.9.near_ref
  32.2 0.0 collective-permute-done.10.swap_near_ref
  32.2 0.1 shard_map.100
  32.2 2.8 %collective-permute-done.8.swap_first_ref = bf16[256,640]{1,0:T(8,128)(2,1)S(1)} collective-permute-done((bf16[256,640]{1,0:T(8,128)(2,1)S(1)}, bf16[256,640]{1,0:T(8,128)(2,1)S(1)}, u32[]{:S(2)}, u32[]{:S(2)}) %collective-permute-start.8) | collective-permute-done | bytes 327712 | tf_op jit(solution)/shard_map/ppermute | solution.py:632
  35.1 0.2 shard_map.101
  35.3 0.0 collective-permute-done.11.far_ref
  35.3 3.3 %collective-permute-done.13.swap_last_ref = bf16[128,640]{1,0:T(8,128)(2,1)S(1)} collective-permute-done((bf16[128,640]{1,0:T(8,128)(2,1)S(1)}, bf16[128,640]{1,0:T(8,128)(2,1)S(1)}, u32[]{:S(2)}, u32[]{:S(2)}) %collective-permute-start.13) | collective-permute-done | bytes 163872 | tf_op jit(solution)/shard_map/ppermute | solution.py:640
  38.6 0.2 shard_map.103
  38.8 2.6 %collective-permute-start.14 = (f32[256,1]{1,0:T(8,128)S(1)}, f32[256,1]{1,0:T(8,128)S(1)}, u32[]{:S(2)}, u32[]{:S(2)}) collective-permute-start(f32[256,1]{1,0:T(8,128)S(1)} %get-tuple-element.66.sums_ref.earlier_ref), channel_id=1, source_target_pairs={{0,1},{1,0},{2,3},{3,2},{4,5},{5,4},{6,7},{7,6},{8,9},{9,8},{10,11... | collective-permute-start | bytes 3080 | tf_op jit(solution)/shard_map/ppermute | solution.py:651
  41.5 0.8 %shard_map.105 = bf16[128,1280]{1,0:T(8,128)(2,1)} custom-call(f32[384,640]{1,0:T(8,128)S(1)} %get-tuple-element.53.own_ref, f32[128,640]{1,0:T(8,128)S(1)} %get-tuple-element.57.earlier_ref.near_ref, bf16[128,640]{1,0:T(8,128)(2,1)S(1)} %collective-permute-done.11.far_ref, bf16[256,640]{1,0:T(8,128)(2,1)S(1)} %collective-permute-done.8.swap_first_ref, ...), custom_call_target="tpu_custom_call" | custom-call | flops 1000000 | bytes 1000000 | tf_op jit(solution)/shard_map/pallas_call | solution.py:652
  42.2 0.2 collective-permute-done.14.peer_ref
  42.4 1.0 %shard_map.104 = (bf16[128,1280]{1,0:T(8,128)(2,1)}, bf16[128,1280]{1,0:T(8,128)(2,1)}) custom-call(bf16[128,1280]{1,0:T(8,128)(2,1)S(1)} %get-tuple-element.36.q_ref, bf16[128,1280]{1,0:T(8,128)(2,1)S(1)} %get-tuple-element.37.k_ref, f32[128,1280]{1,0:T(8,128)S(1)} %get-tuple-element.58.gated_q_ref, f32[128,1280]{1,0:T(8,128)S(1)} %get-tuple-element.64.gated_k_ref, ...), custom_call_target="tpu_custom_call" | custom-call | flops 1000000 | bytes 1000000 | tf_op jit(solution)/shard_map/pallas_call | solution.py:653
  (2 shorter events, 0.0 us)
Async XLA Ops:
  0.6 11.7 %copy-start = (s32[2,16,4]{1,2,0:T(4,128)S(1)}, s32[2,16,4]{1,2,0:T(4,128)}, u32[]{:S(2)}) copy-start(s32[2,16,4]{1,2,0:T(4,128)} %param.13) | copy-start | bytes 1540
  2.0 2.0 %collective-permute-start = (f32[256,1]{1,0:T(8,128)S(1)}, f32[256,1]{1,0:T(8,128)S(1)}, u32[]{:S(2)}, u32[]{:S(2)}) collective-permute-start(f32[256,1]{1,0:T(8,128)S(1)} %get-tuple-element.41.sums_ref), channel_id=1, source_target_pairs={{0,1},{1,0},{2,3},{3,2},{4,5},{5,4},{6,7},{7,6},{8,9},{9,8},{10,11... | collective-permute-start | bytes 3080 | tf_op jit(solution)/shard_map/ppermute | solution.py:597
  2.7 7.4 %collective-permute-start.3 = (bf16[128,640]{1,0:T(8,128)(2,1)S(1)}, bf16[128,640]{1,0:T(8,128)(2,1)S(1)}, u32[]{:S(2)}, u32[]{:S(2)}) collective-permute-start(bf16[128,640]{1,0:T(8,128)(2,1)S(1)} %get-tuple-element.45), channel_id=1, source_target_pairs={{0,16},{16,0},{1,17},{17,1},{2,18},{18,2},{3,19},{19,3},{4,20},{20... | collective-permute-start | bytes 491528 | tf_op jit(solution)/shard_map/ppermute | solution.py:596
  4.2 7.8 %collective-permute-start.2 = (bf16[128,640]{1,0:T(8,128)(2,1)S(1)}, bf16[128,640]{1,0:T(8,128)(2,1)S(1)}, u32[]{:S(2)}, u32[]{:S(2)}) collective-permute-start(bf16[128,640]{1,0:T(8,128)(2,1)S(1)} %get-tuple-element.44), channel_id=1, source_target_pairs={{0,16},{16,0},{1,17},{17,1},{2,18},{18,2},{3,19},{19,3},{4,20},{20... | collective-permute-start | bytes 491528 | tf_op jit(solution)/shard_map/ppermute | solution.py:603
  5.3 6.8 %collective-permute-start.4 = (bf16[128,640]{1,0:T(8,128)(2,1)S(1)}, bf16[128,640]{1,0:T(8,128)(2,1)S(1)}, u32[]{:S(2)}, u32[]{:S(2)}) collective-permute-start(bf16[128,640]{1,0:T(8,128)(2,1)S(1)} %get-tuple-element.46), channel_id=1, source_target_pairs={{0,2},{4,6},{8,10},{12,14},{2,0},{6,4},{10,8},{14,12},{1,3},{5,7},... | collective-permute-start | bytes 491528 | tf_op jit(solution)/shard_map/ppermute | solution.py:602
  5.5 13.6 %collective-permute-start.6 = (bf16[256,640]{1,0:T(8,128)(2,1)S(1)}, bf16[256,640]{1,0:T(8,128)(2,1)S(1)}, u32[]{:S(2)}, u32[]{:S(2)}) collective-permute-start(bf16[256,640]{1,0:T(8,128)(2,1)S(1)} %get-tuple-element.49), channel_id=1, source_target_pairs={{0,16},{16,0},{1,17},{17,1},{2,18},{18,2},{3,19},{19,3},{4,20},{20... | collective-permute-start | bytes 983048 | tf_op jit(solution)/shard_map/ppermute | solution.py:604
  6.0 11.3 %collective-permute-start.1 = (bf16[128,640]{1,0:T(8,128)(2,1)S(1)}, bf16[128,640]{1,0:T(8,128)(2,1)S(1)}, u32[]{:S(2)}, u32[]{:S(2)}) collective-permute-start(bf16[128,640]{1,0:T(8,128)(2,1)S(1)} %get-tuple-element.43), channel_id=1, source_target_pairs={{2,4},{6,8},{10,12},{4,2},{8,6},{12,10},{3,5},{7,9},{11,13},{5,3},... | collective-permute-start | bytes 491528 | tf_op jit(solution)/shard_map/ppermute | solution.py:605
  12.0 5.2 %collective-permute-start.7 = (bf16[128,640]{1,0:T(8,128)(2,1)S(1)}, bf16[128,640]{1,0:T(8,128)(2,1)S(1)}, u32[]{:S(2)}, u32[]{:S(2)}) collective-permute-start(bf16[128,640]{1,0:T(8,128)(2,1)S(1)} %shard_map.96.earlier_ref), channel_id=1, source_target_pairs={{0,2},{4,6},{8,10},{12,14},{2,0},{6,4},{10,8},{14,12},{1,3},{5,7},... | collective-permute-start | bytes 491528 | tf_op jit(solution)/shard_map/ppermute | solution.py:607
  13.1 9.8 %collective-permute-start.5 = (bf16[128,640]{1,0:T(8,128)(2,1)S(1)}, bf16[128,640]{1,0:T(8,128)(2,1)S(1)}, u32[]{:S(2)}, u32[]{:S(2)}) collective-permute-start(bf16[128,640]{1,0:T(8,128)(2,1)S(1)} %get-tuple-element.47), channel_id=1, source_target_pairs={{2,4},{6,8},{10,12},{4,2},{8,6},{12,10},{3,5},{7,9},{11,13},{5,3},... | collective-permute-start | bytes 491528 | tf_op jit(solution)/shard_map/ppermute | solution.py:614
  20.5 11.7 %collective-permute-start.9 = (bf16[144,640]{1,0:T(8,128)(2,1)S(1)}, bf16[144,640]{1,0:T(8,128)(2,1)S(1)}, u32[]{:S(2)}, u32[]{:S(2)}) collective-permute-start(bf16[144,640]{1,0:T(8,128)(2,1)S(1)} %get-tuple-element.55), channel_id=1, source_target_pairs={{0,2},{4,6},{8,10},{12,14},{2,0},{6,4},{10,8},{14,12},{1,3},{5,7},... | collective-permute-start | bytes 552968 | tf_op jit(solution)/shard_map/ppermute | solution.py:622
  20.8 11.4 %collective-permute-start.10 = (bf16[144,640]{1,0:T(8,128)(2,1)S(1)}, bf16[144,640]{1,0:T(8,128)(2,1)S(1)}, u32[]{:S(2)}, u32[]{:S(2)}) collective-permute-start(bf16[144,640]{1,0:T(8,128)(2,1)S(1)} %get-tuple-element.56), channel_id=1, source_target_pairs={{0,18},{4,22},{8,26},{12,30},{2,16},{6,20},{10,24},{14,28},{16,2},... | collective-permute-start | bytes 552968 | tf_op jit(solution)/shard_map/ppermute | solution.py:623
  24.3 7.1 %collective-permute-start.12 = (bf16[128,640]{1,0:T(8,128)(2,1)S(1)}, bf16[128,640]{1,0:T(8,128)(2,1)S(1)}, u32[]{:S(2)}, u32[]{:S(2)}) collective-permute-start(bf16[128,640]{1,0:T(8,128)(2,1)S(1)} %get-tuple-element.62), channel_id=1, source_target_pairs={{2,4},{6,8},{10,12},{4,2},{8,6},{12,10},{3,5},{7,9},{11,13},{5,3},... | collective-permute-start | bytes 491528 | tf_op jit(solution)/shard_map/ppermute | solution.py:631
  27.5 7.6 %collective-permute-start.8 = (bf16[256,640]{1,0:T(8,128)(2,1)S(1)}, bf16[256,640]{1,0:T(8,128)(2,1)S(1)}, u32[]{:S(2)}, u32[]{:S(2)}) collective-permute-start(bf16[256,640]{1,0:T(8,128)(2,1)S(1)} %get-tuple-element.54), channel_id=1, source_target_pairs={{0,16},{16,0},{1,17},{17,1},{2,18},{18,2},{3,19},{19,3},{4,20},{20... | collective-permute-start | bytes 983048 | tf_op jit(solution)/shard_map/ppermute | solution.py:632
  27.8 7.5 %collective-permute-start.11 = (bf16[128,640]{1,0:T(8,128)(2,1)S(1)}, bf16[128,640]{1,0:T(8,128)(2,1)S(1)}, u32[]{:S(2)}, u32[]{:S(2)}) collective-permute-start(bf16[128,640]{1,0:T(8,128)(2,1)S(1)} %get-tuple-element.59), channel_id=1, source_target_pairs={{2,4},{6,8},{10,12},{4,2},{8,6},{12,10},{3,5},{7,9},{11,13},{5,3},... | collective-permute-start | bytes 491528 | tf_op jit(solution)/shard_map/ppermute | solution.py:633
  31.4 7.2 %collective-permute-start.13 = (bf16[128,640]{1,0:T(8,128)(2,1)S(1)}, bf16[128,640]{1,0:T(8,128)(2,1)S(1)}, u32[]{:S(2)}, u32[]{:S(2)}) collective-permute-start(bf16[128,640]{1,0:T(8,128)(2,1)S(1)} %shard_map.102), channel_id=1, source_target_pairs={{0,16},{16,0},{1,17},{17,1},{2,18},{18,2},{3,19},{19,3},{4,20},{20... | collective-permute-start | bytes 491528 | tf_op jit(solution)/shard_map/ppermute | solution.py:640
  38.8 3.6 %collective-permute-start.14 = (f32[256,1]{1,0:T(8,128)S(1)}, f32[256,1]{1,0:T(8,128)S(1)}, u32[]{:S(2)}, u32[]{:S(2)}) collective-permute-start(f32[256,1]{1,0:T(8,128)S(1)} %get-tuple-element.66.sums_ref.earlier_ref), channel_id=1, source_target_pairs={{0,1},{1,0},{2,3},{3,2},{4,5},{5,4},{6,7},{7,6},{8,9},{9,8},{10,11... | collective-permute-start | bytes 3080 | tf_op jit(solution)/shard_map/ppermute | solution.py:651

commit v8 on v7

--- a/solution.py
+++ b/solution.py
@@ -460,10 +460,28 @@
     out_ref[...] = (a_ref[...] + b_ref[...].astype(F32)).astype(BF16)
 
 
-def gather_q_kernel(
-    width, q_ref, gain_ref, own_ref, swap_first_ref, earlier_ref, gated_ref, sums_ref
+def gather_early_kernel(
+    width,
+    q_ref,
+    k_ref,
+    gain_ref,
+    gain_k_ref,
+    own_ref,
+    swap_first_ref,
+    near_ref,
+    swap_near_ref,
+    gated_ref,
+    gated_near_ref,
+    sums_ref,
+    sum_near_ref,
 ):
     mine, theirs = halves(q_ref.shape[1] // 2)
+    near, _ = sides(width)
+    near_dk = swap_first_ref[2 * width : 3 * width].astype(F32) + swap_near_ref[:width]
+    gated_near_ref[:, mine] = gain_k_ref[:, mine] * near_ref[:width]
+    gated_near_ref[:, theirs] = gain_k_ref[:, theirs] * near_dk
+    k_near = k_ref[near].astype(F32)
+    sum_near_ref[...] = jnp.sum(k_near * gated_near_ref[...], -1, keepdims=True)
     for index, rows in enumerate(sides(width)):
         at = slice(index * width, (index + 1) * width)
         gated_ref[rows, mine] = gain_ref[:, mine] * own_ref[at]
@@ -476,11 +494,10 @@
     k_ref,
     gain_ref,
     own_ref,
-    near_ref,
     far_ref,
-    swap_first_ref,
-    swap_near_ref,
     swap_last_ref,
+    gated_near_ref,
+    sum_near_ref,
     sum_q_ref,
     gated_ref,
     sums_ref,
@@ -488,17 +505,14 @@
     tokens = k_ref.shape[0]
     mine, theirs = halves(k_ref.shape[1] // 2)
     near, far = sides(width)
-
-    def term(ref, index):
-        return ref[index * width : (index + 1) * width].astype(F32)
-
-    gated_ref[near, mine] = gain_ref[:, mine] * term(near_ref, 0)
-    gated_ref[far, mine] = gain_ref[:, mine] * (term(own_ref, 3) + term(far_ref, 0))
-    near_dk = term(swap_first_ref, 2) + term(swap_near_ref, 0)
-    gated_ref[near, theirs] = gain_ref[:, theirs] * near_dk
-    gated_ref[far, theirs] = gain_ref[:, theirs] * term(swap_last_ref, 0)
+    far_dk = own_ref[3 * width : 4 * width] + far_ref[:width].astype(F32)
+    gated_ref[far, mine] = gain_ref[:, mine] * far_dk
+    gated_ref[far, theirs] = gain_ref[:, theirs] * swap_last_ref[:width].astype(F32)
+    sum_far = jnp.sum(k_ref[far].astype(F32) * gated_ref[far], -1, keepdims=True)
+    gated_ref[near] = gated_near_ref[...]
     sums_ref[:tokens] = sum_q_ref[...]
-    sums_ref[tokens:] = jnp.sum(k_ref[...].astype(F32) * gated_ref[...], -1, keepdims=True)
+    sums_ref[pl.ds(pl.multiple_of(tokens + near.start, width), width)] = sum_near_ref[...]
+    sums_ref[pl.ds(pl.multiple_of(tokens + far.start, width), width)] = sum_far
 
 
 def value_kernel(
@@ -640,13 +654,13 @@
     swap_last = lax.ppermute(last_out, "frame", SWAP)
     terms = (own_total, near_total, far_total, swap_first, swap_near_total, swap_last)
     gated = shape(tokens, feat_dev, F32)
-    gated_q, sum_q = call(
-        functools.partial(gather_q_kernel, width),
-        (gated, shape(tokens, 1, F32)),
+    gated_q, gated_near, sum_q, sum_near = call(
+        functools.partial(gather_early_kernel, width),
+        (gated, shape(width, feat_dev, F32), shape(tokens, 1, F32), shape(width, 1, F32)),
         flops=3 * 10**9,
-    )(q_all, gain_q, own_total, swap_first, near_total)
+    )(q_all, k_all, gain_q, gain_k, own_total, swap_first, near_total, swap_near_total)
     gated_k, sum_terms = call(functools.partial(gather_k_kernel, width), (gated, sum_pair))(
-        k_all, gain_k, *terms, sum_q
+        k_all, gain_k, own_total, far_total, swap_last, gated_near, sum_near, sum_q
     )
     sum_peer = lax.ppermute(sum_terms, "head", SWAP)
     grad_v = call(functools.partial(value_kernel, width), block)(*terms, sum_terms)

time: 43.6 us -> 43.6 us (level)
  no operation moved by 1% of the time
where the time goes in v8:
time: 43.6 us; the launch traced here: 43.4 us
  starting transfers between devices  24.6 us (56%)
  waiting for transfers between devices  10.5 us (24%)
  Pallas kernels  7.42 us (17%)
  between operations  0.75 us (2%)
    ppermute x1, starting transfers between devices, swapped_device(): swap_far_in = lax.ppermute(relay_far, 'row', far)  4.16 us
    ppermute x1, starting transfers between devices, swapped_device(): far_in = lax.ppermute(far_out, 'row', far)  4.15 us
    ppermute x1, waiting for transfers between devices, swapped_device(): swap_last = lax.ppermute(last_out, 'frame', SWAP)  3.25 us
    ppermute x1, starting transfers between devices, swapped_device(): far_terms = lax.ppermute(swap_far_out, 'row', far)  3.15 us
    ppermute x1, starting transfers between devices, swapped_device(): far_total = lax.ppermute(far_out, 'row', far)  3.02 us
    ppermute x1, waiting for transfers between devices, swapped_device(): swap_first = lax.ppermute(first_out, 'frame', SWAP)  2.85 us
    ppermute x1, starting transfers between devices, swapped_device(): sum_peer = lax.ppermute(sum_terms, 'head', SWAP)  2.64 us
    ppermute x1, starting transfers between devices, swapped_device(): swap_near_total = lax.ppermute(swap_near_out, ('frame', 'row'), swap_near)  2.17 us
  transfers between devices with their start and end apart: 15, of which 6 were waited for; matrix products, arithmetic and copies ran while one was open for 0% of the time, Pallas kernels for 11%

profile of v8, /device:TPU:13, one launch (start us, length us, event | category | flops | bytes accessed | tf_op | source)
XLA Modules:
  0.0 43.4 jit_solution(14386506906597685535)
XLA Ops:
  0.6 0.0 copy-start
  0.6 1.3 %shard_map.94 = (bf16[128,1280]{1,0:T(8,128)(2,1)S(1)}, bf16[128,1280]{1,0:T(8,128)(2,1)S(1)}, bf16[128,1280]{1,0:T(8,128)(2,1)S(1)}, bf16[128,1280]{1,0:T(8,128...) custom-call(bf16[128,1280]{1,0:T(8,128)(2,1)} %bitcast.9, ...), custom_call_target="tpu_custom_call" | custom-call | flops 1000000 | bytes 1000000 | tf_op jit(solution)/shard_map/pallas_call | solution.py:604
  2.0 0.7 %collective-permute-start = (f32[256,1]{1,0:T(8,128)S(1)}, f32[256,1]{1,0:T(8,128)S(1)}, u32[]{:S(2)}, u32[]{:S(2)}) collective-permute-start(f32[256,1]{1,0:T(8,128)S(1)} %get-tuple-element.44.sums_ref), channel_id=1, source_target_pairs={{0,1},{1,0},{2,3},{3,2},{4,5},{5,4},{6,7},{7,6},{8,9},{9,8},{10,11... | collective-permute-start | bytes 3080 | tf_op jit(solution)/shard_map/ppermute | solution.py:611
  2.7 1.2 %collective-permute-start.3 = (bf16[128,640]{1,0:T(8,128)(2,1)S(1)}, bf16[128,640]{1,0:T(8,128)(2,1)S(1)}, u32[]{:S(2)}, u32[]{:S(2)}) collective-permute-start(bf16[128,640]{1,0:T(8,128)(2,1)S(1)} %get-tuple-element.47), channel_id=1, source_target_pairs={{0,16},{16,0},{1,17},{17,1},{2,18},{18,2},{3,19},{19,3},{4,20},{20... | collective-permute-start | bytes 491528 | tf_op jit(solution)/shard_map/ppermute | solution.py:610
  4.0 0.0 collective-permute-done.peer_ref
  4.0 0.3 shard_map.95
  4.2 1.0 %collective-permute-start.2 = (bf16[128,640]{1,0:T(8,128)(2,1)S(1)}, bf16[128,640]{1,0:T(8,128)(2,1)S(1)}, u32[]{:S(2)}, u32[]{:S(2)}) collective-permute-start(bf16[128,640]{1,0:T(8,128)(2,1)S(1)} %get-tuple-element.46), channel_id=1, source_target_pairs={{0,16},{16,0},{1,17},{17,1},{2,18},{18,2},{3,19},{19,3},{4,20},{20... | collective-permute-start | bytes 491528 | tf_op jit(solution)/shard_map/ppermute | solution.py:617
  5.3 0.2 collective-permute-start.4
  5.5 0.5 %collective-permute-start.6 = (bf16[256,640]{1,0:T(8,128)(2,1)S(1)}, bf16[256,640]{1,0:T(8,128)(2,1)S(1)}, u32[]{:S(2)}, u32[]{:S(2)}) collective-permute-start(bf16[256,640]{1,0:T(8,128)(2,1)S(1)} %get-tuple-element.51), channel_id=1, source_target_pairs={{0,16},{16,0},{1,17},{17,1},{2,18},{18,2},{3,19},{19,3},{4,20},{20... | collective-permute-start | bytes 983048 | tf_op jit(solution)/shard_map/ppermute | solution.py:618
  6.0 4.1 %collective-permute-start.1 = (bf16[128,640]{1,0:T(8,128)(2,1)S(1)}, bf16[128,640]{1,0:T(8,128)(2,1)S(1)}, u32[]{:S(2)}, u32[]{:S(2)}) collective-permute-start(bf16[128,640]{1,0:T(8,128)(2,1)S(1)} %get-tuple-element.45), channel_id=1, source_target_pairs={{2,4},{6,8},{10,12},{4,2},{8,6},{12,10},{3,5},{7,9},{11,13},{5,3},... | collective-permute-start | bytes 491528 | tf_op jit(solution)/shard_map/ppermute | solution.py:619
  10.1 0.0 collective-permute-done.3.v_ref.swap_v_ref
  10.1 1.9 %collective-permute-done.2.k_ref.swap_k_ref = bf16[128,640]{1,0:T(8,128)(2,1)S(1)} collective-permute-done((bf16[128,640]{1,0:T(8,128)(2,1)S(1)}, bf16[128,640]{1,0:T(8,128)(2,1)S(1)}, u32[]{:S(2)}, u32[]{:S(2)}) %collective-permute-start.2) | collective-permute-done | bytes 163872 | tf_op jit(solution)/shard_map/ppermute | solution.py:617
  12.0 0.0 collective-permute-done.4.earlier_ref.halo_ref
  12.0 0.3 collective-permute-start.7
  12.3 0.0 copy-done
  12.3 0.7 %shard_map.97 = (bf16[128,640]{1,0:T(8,128)(2,1)S(1)}, f32[384,128]{1,0:T(8,128)S(1)}, f32[384,128]{1,0:T(8,128)S(1)}) custom-call(s32[2,4,16]{2,1,0:T(4,128)S(1)} %bitcast.8, bf16[128,640]{1,0:T(8,128)(2,1)S(1)} %collective-permute-done.2.k_ref.swap_k_ref, bf16[128,640]{1,0:T(8,128)(2,1)S(1)} %collective-permute-done.3.v_ref.swap_v_ref, ...), custom_call_target="tpu_custom_call" | custom-call | flops 1000000 | bytes 1000000 | tf_op jit(solution)/shard_map/pallas_call | solution.py:622
  13.1 4.2 %collective-permute-start.5 = (bf16[128,640]{1,0:T(8,128)(2,1)S(1)}, bf16[128,640]{1,0:T(8,128)(2,1)S(1)}, u32[]{:S(2)}, u32[]{:S(2)}) collective-permute-start(bf16[128,640]{1,0:T(8,128)(2,1)S(1)} %get-tuple-element.49), channel_id=1, source_target_pairs={{2,4},{6,8},{10,12},{4,2},{8,6},{12,10},{3,5},{7,9},{11,13},{5,3},... | collective-permute-start | bytes 491528 | tf_op jit(solution)/shard_map/ppermute | solution.py:628
  17.2 0.0 collective-permute-done.1.earlier_ref.halo_ref
  17.3 0.0 collective-permute-done.7.swap_halo_ref
  17.3 1.8 %collective-permute-done.6.swap_qt_ref = bf16[256,640]{1,0:T(8,128)(2,1)S(1)} collective-permute-done((bf16[256,640]{1,0:T(8,128)(2,1)S(1)}, bf16[256,640]{1,0:T(8,128)(2,1)S(1)}, u32[]{:S(2)}, u32[]{:S(2)}) %collective-permute-start.6) | collective-permute-done | bytes 327712 | tf_op jit(solution)/shard_map/ppermute | solution.py:618
  19.0 1.4 %shard_map.98 = (bf16[144,640]{1,0:T(8,128)(2,1)S(1)}, bf16[144,640]{1,0:T(8,128)(2,1)S(1)}, f32[640,640]{1,0:T(8,128)S(1)}) custom-call(bf16[128,640]{1,0:T(8,128)(2,1)S(1)} %collective-permute-done.4.earlier_ref.halo_ref, bf16[128,640]{1,0:T(8,128)(2,1)S(1)} %collective-permute-done.7.swap_halo_ref, bf16[256,640]{1,0:T(8,128)(2,1)S(1)} %get-tuple-element.50.own_ref, ...), custom_call_target="tpu_custom_call" | custom-call | flops 500000000 | bytes 2000000 | tf_op jit(solution)/shard_map/pallas_call | solution.py:630
  20.5 0.3 collective-permute-start.9
  20.8 2.2 %collective-permute-start.10 = (bf16[144,640]{1,0:T(8,128)(2,1)S(1)}, bf16[144,640]{1,0:T(8,128)(2,1)S(1)}, u32[]{:S(2)}, u32[]{:S(2)}) collective-permute-start(bf16[144,640]{1,0:T(8,128)(2,1)S(1)} %get-tuple-element.58), channel_id=1, source_target_pairs={{0,18},{4,22},{8,26},{12,30},{2,16},{6,20},{10,24},{14,28},{16,2},... | collective-permute-start | bytes 552968 | tf_op jit(solution)/shard_map/ppermute | solution.py:637
  22.9 0.0 collective-permute-done.5.swap_halo_ref
  22.9 1.4 %shard_map.99 = (bf16[128,640]{1,0:T(8,128)(2,1)S(1)}, bf16[128,640]{1,0:T(8,128)(2,1)S(1)}, f32[384,640]{1,0:T(8,128)S(1)}, bf16[256,640]{1,0:T(8,128)(2,1)S(1)}, f32[128,640]{1,0:T(8,128)S(1)}) custom-call(bf16[128,640]{1,0:T(8,128)(2,1)S(1)} %collective-permute-done.1.earlier_ref.halo_ref, bf16[128,640]{1,0:T(8,128)(2,1)S(1)} %collective-permute-done.5.swap_halo_ref, ...), custom_call_target="tpu_custom_call" | custom-call | flops 500000000 | bytes 2000000 | tf_op jit(solution)/shard_map/pallas_call | solution.py:638
  24.3 3.1 %collective-permute-start.12 = (bf16[128,640]{1,0:T(8,128)(2,1)S(1)}, bf16[128,640]{1,0:T(8,128)(2,1)S(1)}, u32[]{:S(2)}, u32[]{:S(2)}) collective-permute-start(bf16[128,640]{1,0:T(8,128)(2,1)S(1)} %get-tuple-element.64), channel_id=1, source_target_pairs={{2,4},{6,8},{10,12},{4,2},{8,6},{12,10},{3,5},{7,9},{11,13},{5,3},... | collective-permute-start | bytes 491528 | tf_op jit(solution)/shard_map/ppermute | solution.py:645
  27.5 0.3 collective-permute-start.8
  27.8 3.0 %collective-permute-start.11 = (bf16[128,640]{1,0:T(8,128)(2,1)S(1)}, bf16[128,640]{1,0:T(8,128)(2,1)S(1)}, u32[]{:S(2)}, u32[]{:S(2)}) collective-permute-start(bf16[128,640]{1,0:T(8,128)(2,1)S(1)} %get-tuple-element.62), channel_id=1, source_target_pairs={{2,4},{6,8},{10,12},{4,2},{8,6},{12,10},{3,5},{7,9},{11,13},{5,3},... | collective-permute-start | bytes 491528 | tf_op jit(solution)/shard_map/ppermute | solution.py:647
  30.8 0.6 %collective-permute-done.12.b_ref = bf16[128,640]{1,0:T(8,128)(2,1)S(1)} collective-permute-done((bf16[128,640]{1,0:T(8,128)(2,1)S(1)}, bf16[128,640]{1,0:T(8,128)(2,1)S(1)}, u32[]{:S(2)}, u32[]{:S(2)}) %collective-permute-start.12) | collective-permute-done | bytes 163872 | tf_op jit(solution)/shard_map/ppermute | solution.py:645
  31.4 0.7 %collective-permute-start.13 = (bf16[128,640]{1,0:T(8,128)(2,1)S(1)}, bf16[128,640]{1,0:T(8,128)(2,1)S(1)}, u32[]{:S(2)}, u32[]{:S(2)}) collective-permute-start(bf16[128,640]{1,0:T(8,128)(2,1)S(1)} %shard_map.102), channel_id=1, source_target_pairs={{0,16},{16,0},{1,17},{17,1},{2,18},{18,2},{3,19},{19,3},{4,20},{20... | collective-permute-start | bytes 491528 | tf_op jit(solution)/shard_map/ppermute | solution.py:654
  32.2 0.0 collective-permute-done.9.near_ref
  32.2 0.0 collective-permute-done.10.swap_near_ref
  32.2 0.1 shard_map.100
  32.2 2.8 %collective-permute-done.8.swap_first_ref = bf16[256,640]{1,0:T(8,128)(2,1)S(1)} collective-permute-done((bf16[256,640]{1,0:T(8,128)(2,1)S(1)}, bf16[256,640]{1,0:T(8,128)(2,1)S(1)}, u32[]{:S(2)}, u32[]{:S(2)}) %collective-permute-start.8) | collective-permute-done | bytes 327712 | tf_op jit(solution)/shard_map/ppermute | solution.py:646
  35.1 0.3 shard_map.101
  35.3 0.0 collective-permute-done.11.far_ref
  35.3 3.3 %collective-permute-done.13.swap_last_ref = bf16[128,640]{1,0:T(8,128)(2,1)S(1)} collective-permute-done((bf16[128,640]{1,0:T(8,128)(2,1)S(1)}, bf16[128,640]{1,0:T(8,128)(2,1)S(1)}, u32[]{:S(2)}, u32[]{:S(2)}) %collective-permute-start.13) | collective-permute-done | bytes 163872 | tf_op jit(solution)/shard_map/ppermute | solution.py:654
  38.6 0.2 shard_map.103
  38.7 2.6 %collective-permute-start.14 = (f32[256,1]{1,0:T(8,128)S(1)}, f32[256,1]{1,0:T(8,128)S(1)}, u32[]{:S(2)}, u32[]{:S(2)}) collective-permute-start(f32[256,1]{1,0:T(8,128)S(1)} %get-tuple-element.70.sums_ref.earlier_ref), channel_id=1, source_target_pairs={{0,1},{1,0},{2,3},{3,2},{4,5},{5,4},{6,7},{7,6},{8,9},{9,8},{10,11... | collective-permute-start | bytes 3080 | tf_op jit(solution)/shard_map/ppermute | solution.py:665
  41.4 0.8 %shard_map.105 = bf16[128,1280]{1,0:T(8,128)(2,1)} custom-call(f32[384,640]{1,0:T(8,128)S(1)} %get-tuple-element.55.own_ref, f32[128,640]{1,0:T(8,128)S(1)} %get-tuple-element.59.near_ref, bf16[128,640]{1,0:T(8,128)(2,1)S(1)} %collective-permute-done.11.far_ref, bf16[256,640]{1,0:T(8,128)(2,1)S(1)} %collective-permute-done.8.swap_first_ref, ...), custom_call_target="tpu_custom_call" | custom-call | flops 1000000 | bytes 1000000 | tf_op jit(solution)/shard_map/pallas_call | solution.py:666
  42.2 0.2 collective-permute-done.14.peer_ref
  42.4 1.0 %shard_map.104 = (bf16[128,1280]{1,0:T(8,128)(2,1)}, bf16[128,1280]{1,0:T(8,128)(2,1)}) custom-call(bf16[128,1280]{1,0:T(8,128)(2,1)S(1)} %get-tuple-element.38.q_ref, bf16[128,1280]{1,0:T(8,128)(2,1)S(1)} %get-tuple-element.39.k_ref, f32[128,1280]{1,0:T(8,128)S(1)} %get-tuple-element.61.gated_q_ref, f32[128,1280]{1,0:T(8,128)S(1)} %get-tuple-element.68.gated_k_ref, ...), custom_call_target="tpu_custom_call" | custom-call | flops 1000000 | bytes 1000000 | tf_op jit(solution)/shard_map/pallas_call | solution.py:667
  (2 shorter events, 0.0 us)
Async XLA Ops:
  0.6 11.7 %copy-start = (s32[2,16,4]{1,2,0:T(4,128)S(1)}, s32[2,16,4]{1,2,0:T(4,128)}, u32[]{:S(2)}) copy-start(s32[2,16,4]{1,2,0:T(4,128)} %param.13) | copy-start | bytes 1540
  2.0 2.0 %collective-permute-start = (f32[256,1]{1,0:T(8,128)S(1)}, f32[256,1]{1,0:T(8,128)S(1)}, u32[]{:S(2)}, u32[]{:S(2)}) collective-permute-start(f32[256,1]{1,0:T(8,128)S(1)} %get-tuple-element.44.sums_ref), channel_id=1, source_target_pairs={{0,1},{1,0},{2,3},{3,2},{4,5},{5,4},{6,7},{7,6},{8,9},{9,8},{10,11... | collective-permute-start | bytes 3080 | tf_op jit(solution)/shard_map/ppermute | solution.py:611
  2.7 7.4 %collective-permute-start.3 = (bf16[128,640]{1,0:T(8,128)(2,1)S(1)}, bf16[128,640]{1,0:T(8,128)(2,1)S(1)}, u32[]{:S(2)}, u32[]{:S(2)}) collective-permute-start(bf16[128,640]{1,0:T(8,128)(2,1)S(1)} %get-tuple-element.47), channel_id=1, source_target_pairs={{0,16},{16,0},{1,17},{17,1},{2,18},{18,2},{3,19},{19,3},{4,20},{20... | collective-permute-start | bytes 491528 | tf_op jit(solution)/shard_map/ppermute | solution.py:610
  4.2 7.8 %collective-permute-start.2 = (bf16[128,640]{1,0:T(8,128)(2,1)S(1)}, bf16[128,640]{1,0:T(8,128)(2,1)S(1)}, u32[]{:S(2)}, u32[]{:S(2)}) collective-permute-start(bf16[128,640]{1,0:T(8,128)(2,1)S(1)} %get-tuple-element.46), channel_id=1, source_target_pairs={{0,16},{16,0},{1,17},{17,1},{2,18},{18,2},{3,19},{19,3},{4,20},{20... | collective-permute-start | bytes 491528 | tf_op jit(solution)/shard_map/ppermute | solution.py:617
  5.3 6.8 %collective-permute-start.4 = (bf16[128,640]{1,0:T(8,128)(2,1)S(1)}, bf16[128,640]{1,0:T(8,128)(2,1)S(1)}, u32[]{:S(2)}, u32[]{:S(2)}) collective-permute-start(bf16[128,640]{1,0:T(8,128)(2,1)S(1)} %get-tuple-element.48), channel_id=1, source_target_pairs={{0,2},{4,6},{8,10},{12,14},{2,0},{6,4},{10,8},{14,12},{1,3},{5,7},... | collective-permute-start | bytes 491528 | tf_op jit(solution)/shard_map/ppermute | solution.py:616
  5.5 13.6 %collective-permute-start.6 = (bf16[256,640]{1,0:T(8,128)(2,1)S(1)}, bf16[256,640]{1,0:T(8,128)(2,1)S(1)}, u32[]{:S(2)}, u32[]{:S(2)}) collective-permute-start(bf16[256,640]{1,0:T(8,128)(2,1)S(1)} %get-tuple-element.51), channel_id=1, source_target_pairs={{0,16},{16,0},{1,17},{17,1},{2,18},{18,2},{3,19},{19,3},{4,20},{20... | collective-permute-start | bytes 983048 | tf_op jit(solution)/shard_map/ppermute | solution.py:618
  6.0 11.3 %collective-permute-start.1 = (bf16[128,640]{1,0:T(8,128)(2,1)S(1)}, bf16[128,640]{1,0:T(8,128)(2,1)S(1)}, u32[]{:S(2)}, u32[]{:S(2)}) collective-permute-start(bf16[128,640]{1,0:T(8,128)(2,1)S(1)} %get-tuple-element.45), channel_id=1, source_target_pairs={{2,4},{6,8},{10,12},{4,2},{8,6},{12,10},{3,5},{7,9},{11,13},{5,3},... | collective-permute-start | bytes 491528 | tf_op jit(solution)/shard_map/ppermute | solution.py:619
  12.0 5.2 %collective-permute-start.7 = (bf16[128,640]{1,0:T(8,128)(2,1)S(1)}, bf16[128,640]{1,0:T(8,128)(2,1)S(1)}, u32[]{:S(2)}, u32[]{:S(2)}) collective-permute-start(bf16[128,640]{1,0:T(8,128)(2,1)S(1)} %shard_map.96.earlier_ref), channel_id=1, source_target_pairs={{0,2},{4,6},{8,10},{12,14},{2,0},{6,4},{10,8},{14,12},{1,3},{5,7},... | collective-permute-start | bytes 491528 | tf_op jit(solution)/shard_map/ppermute | solution.py:621
  13.1 9.8 %collective-permute-start.5 = (bf16[128,640]{1,0:T(8,128)(2,1)S(1)}, bf16[128,640]{1,0:T(8,128)(2,1)S(1)}, u32[]{:S(2)}, u32[]{:S(2)}) collective-permute-start(bf16[128,640]{1,0:T(8,128)(2,1)S(1)} %get-tuple-element.49), channel_id=1, source_target_pairs={{2,4},{6,8},{10,12},{4,2},{8,6},{12,10},{3,5},{7,9},{11,13},{5,3},... | collective-permute-start | bytes 491528 | tf_op jit(solution)/shard_map/ppermute | solution.py:628
  20.5 11.7 %collective-permute-start.9 = (bf16[144,640]{1,0:T(8,128)(2,1)S(1)}, bf16[144,640]{1,0:T(8,128)(2,1)S(1)}, u32[]{:S(2)}, u32[]{:S(2)}) collective-permute-start(bf16[144,640]{1,0:T(8,128)(2,1)S(1)} %get-tuple-element.57), channel_id=1, source_target_pairs={{0,2},{4,6},{8,10},{12,14},{2,0},{6,4},{10,8},{14,12},{1,3},{5,7},... | collective-permute-start | bytes 552968 | tf_op jit(solution)/shard_map/ppermute | solution.py:636
  20.8 11.4 %collective-permute-start.10 = (bf16[144,640]{1,0:T(8,128)(2,1)S(1)}, bf16[144,640]{1,0:T(8,128)(2,1)S(1)}, u32[]{:S(2)}, u32[]{:S(2)}) collective-permute-start(bf16[144,640]{1,0:T(8,128)(2,1)S(1)} %get-tuple-element.58), channel_id=1, source_target_pairs={{0,18},{4,22},{8,26},{12,30},{2,16},{6,20},{10,24},{14,28},{16,2},... | collective-permute-start | bytes 552968 | tf_op jit(solution)/shard_map/ppermute | solution.py:637
  24.3 7.1 %collective-permute-start.12 = (bf16[128,640]{1,0:T(8,128)(2,1)S(1)}, bf16[128,640]{1,0:T(8,128)(2,1)S(1)}, u32[]{:S(2)}, u32[]{:S(2)}) collective-permute-start(bf16[128,640]{1,0:T(8,128)(2,1)S(1)} %get-tuple-element.64), channel_id=1, source_target_pairs={{2,4},{6,8},{10,12},{4,2},{8,6},{12,10},{3,5},{7,9},{11,13},{5,3},... | collective-permute-start | bytes 491528 | tf_op jit(solution)/shard_map/ppermute | solution.py:645
  27.5 7.6 %collective-permute-start.8 = (bf16[256,640]{1,0:T(8,128)(2,1)S(1)}, bf16[256,640]{1,0:T(8,128)(2,1)S(1)}, u32[]{:S(2)}, u32[]{:S(2)}) collective-permute-start(bf16[256,640]{1,0:T(8,128)(2,1)S(1)} %get-tuple-element.56), channel_id=1, source_target_pairs={{0,16},{16,0},{1,17},{17,1},{2,18},{18,2},{3,19},{19,3},{4,20},{20... | collective-permute-start | bytes 983048 | tf_op jit(solution)/shard_map/ppermute | solution.py:646
  27.8 7.5 %collective-permute-start.11 = (bf16[128,640]{1,0:T(8,128)(2,1)S(1)}, bf16[128,640]{1,0:T(8,128)(2,1)S(1)}, u32[]{:S(2)}, u32[]{:S(2)}) collective-permute-start(bf16[128,640]{1,0:T(8,128)(2,1)S(1)} %get-tuple-element.62), channel_id=1, source_target_pairs={{2,4},{6,8},{10,12},{4,2},{8,6},{12,10},{3,5},{7,9},{11,13},{5,3},... | collective-permute-start | bytes 491528 | tf_op jit(solution)/shard_map/ppermute | solution.py:647
  31.4 7.2 %collective-permute-start.13 = (bf16[128,640]{1,0:T(8,128)(2,1)S(1)}, bf16[128,640]{1,0:T(8,128)(2,1)S(1)}, u32[]{:S(2)}, u32[]{:S(2)}) collective-permute-start(bf16[128,640]{1,0:T(8,128)(2,1)S(1)} %shard_map.102), channel_id=1, source_target_pairs={{0,16},{16,0},{1,17},{17,1},{2,18},{18,2},{3,19},{19,3},{4,20},{20... | collective-permute-start | bytes 491528 | tf_op jit(solution)/shard_map/ppermute | solution.py:654
  38.7 3.6 %collective-permute-start.14 = (f32[256,1]{1,0:T(8,128)S(1)}, f32[256,1]{1,0:T(8,128)S(1)}, u32[]{:S(2)}, u32[]{:S(2)}) collective-permute-start(f32[256,1]{1,0:T(8,128)S(1)} %get-tuple-element.70.sums_ref.earlier_ref), channel_id=1, source_target_pairs={{0,1},{1,0},{2,3},{3,2},{4,5},{5,4},{6,7},{7,6},{8,9},{9,8},{10,11... | collective-permute-start | bytes 3080 | tf_op jit(solution)/shard_map/ppermute | solution.py:665

commit v9 on v8

--- a/solution.py
+++ b/solution.py
@@ -164,6 +164,7 @@
 F32 = jnp.float32
 BF16 = jnp.bfloat16
 VMEM_LIMIT = 48 * 1024 * 1024
+LOG2_E = 1.4426950408889634
 
 
 def call(body, out_shape, flops=10**6, moved=10**6, **kw):
@@ -340,8 +341,8 @@
         return (query, target, key, value)
 
     def weights(query, key):
-        scores = product(key, query, 1, 1) * score_scale + bias
-        expo = jnp.exp(scores - jnp.max(scores, 0, keepdims=True))
+        scores = product(key, query, 1, 1) * (score_scale * LOG2_E) + bias
+        expo = jnp.exp2(scores - jnp.max(scores, 0, keepdims=True))
         return expo * (1.0 / jnp.sum(expo, 0, keepdims=True))
 
     def output_grad(prob_b, target, value):

time: 43.6 us -> 43.5 us (level)
  no operation moved by 1% of the time
where the time goes in v9:
time: 43.5 us; the launch traced here: 43.3 us
  starting transfers between devices  24.6 us (57%)
  waiting for transfers between devices  10.5 us (24%)
  Pallas kernels  7.38 us (17%)
  between operations  0.75 us (2%)
    ppermute x1, starting transfers between devices, swapped_device(): swap_far_in = lax.ppermute(relay_far, 'row', far)  4.16 us
    ppermute x1, starting transfers between devices, swapped_device(): far_in = lax.ppermute(far_out, 'row', far)  4.15 us
    ppermute x1, waiting for transfers between devices, swapped_device(): swap_last = lax.ppermute(last_out, 'frame', SWAP)  3.25 us
    ppermute x1, starting transfers between devices, swapped_device(): far_terms = lax.ppermute(swap_far_out, 'row', far)  3.16 us
    ppermute x1, starting transfers between devices, swapped_device(): far_total = lax.ppermute(far_out, 'row', far)  3.02 us
    ppermute x1, waiting for transfers between devices, swapped_device(): swap_first = lax.ppermute(first_out, 'frame', SWAP)  2.85 us
    ppermute x1, starting transfers between devices, swapped_device(): sum_peer = lax.ppermute(sum_terms, 'head', SWAP)  2.64 us
    ppermute x1, starting transfers between devices, swapped_device(): swap_near_total = lax.ppermute(swap_near_out, ('frame', 'row'), swap_near)  2.15 us
  transfers between devices with their start and end apart: 15, of which 6 were waited for; matrix products, arithmetic and copies ran while one was open for 0% of the time, Pallas kernels for 11%

profile of v9, /device:TPU:13, one launch (start us, length us, event | category | flops | bytes accessed | tf_op | source)
XLA Modules:
  0.0 43.3 jit_solution(13768615841802109018)
XLA Ops:
  0.6 0.0 copy-start
  0.6 1.3 %shard_map.94 = (bf16[128,1280]{1,0:T(8,128)(2,1)S(1)}, bf16[128,1280]{1,0:T(8,128)(2,1)S(1)}, bf16[128,1280]{1,0:T(8,128)(2,1)S(1)}, bf16[128,1280]{1,0:T(8,128...) custom-call(bf16[128,1280]{1,0:T(8,128)(2,1)} %bitcast.9, ...), custom_call_target="tpu_custom_call" | custom-call | flops 1000000 | bytes 1000000 | tf_op jit(solution)/shard_map/pallas_call | solution.py:605
  2.0 0.7 %collective-permute-start = (f32[256,1]{1,0:T(8,128)S(1)}, f32[256,1]{1,0:T(8,128)S(1)}, u32[]{:S(2)}, u32[]{:S(2)}) collective-permute-start(f32[256,1]{1,0:T(8,128)S(1)} %get-tuple-element.44.sums_ref), channel_id=1, source_target_pairs={{0,1},{1,0},{2,3},{3,2},{4,5},{5,4},{6,7},{7,6},{8,9},{9,8},{10,11... | collective-permute-start | bytes 3080 | tf_op jit(solution)/shard_map/ppermute | solution.py:612
  2.7 1.2 %collective-permute-start.3 = (bf16[128,640]{1,0:T(8,128)(2,1)S(1)}, bf16[128,640]{1,0:T(8,128)(2,1)S(1)}, u32[]{:S(2)}, u32[]{:S(2)}) collective-permute-start(bf16[128,640]{1,0:T(8,128)(2,1)S(1)} %get-tuple-element.47), channel_id=1, source_target_pairs={{0,16},{16,0},{1,17},{17,1},{2,18},{18,2},{3,19},{19,3},{4,20},{20... | collective-permute-start | bytes 491528 | tf_op jit(solution)/shard_map/ppermute | solution.py:611
  4.0 0.0 collective-permute-done.peer_ref
  4.0 0.3 shard_map.95
  4.2 1.0 %collective-permute-start.2 = (bf16[128,640]{1,0:T(8,128)(2,1)S(1)}, bf16[128,640]{1,0:T(8,128)(2,1)S(1)}, u32[]{:S(2)}, u32[]{:S(2)}) collective-permute-start(bf16[128,640]{1,0:T(8,128)(2,1)S(1)} %get-tuple-element.46), channel_id=1, source_target_pairs={{0,16},{16,0},{1,17},{17,1},{2,18},{18,2},{3,19},{19,3},{4,20},{20... | collective-permute-start | bytes 491528 | tf_op jit(solution)/shard_map/ppermute | solution.py:618
  5.3 0.2 collective-permute-start.4
  5.5 0.5 %collective-permute-start.6 = (bf16[256,640]{1,0:T(8,128)(2,1)S(1)}, bf16[256,640]{1,0:T(8,128)(2,1)S(1)}, u32[]{:S(2)}, u32[]{:S(2)}) collective-permute-start(bf16[256,640]{1,0:T(8,128)(2,1)S(1)} %get-tuple-element.51), channel_id=1, source_target_pairs={{0,16},{16,0},{1,17},{17,1},{2,18},{18,2},{3,19},{19,3},{4,20},{20... | collective-permute-start | bytes 983048 | tf_op jit(solution)/shard_map/ppermute | solution.py:619
  6.0 4.1 %collective-permute-start.1 = (bf16[128,640]{1,0:T(8,128)(2,1)S(1)}, bf16[128,640]{1,0:T(8,128)(2,1)S(1)}, u32[]{:S(2)}, u32[]{:S(2)}) collective-permute-start(bf16[128,640]{1,0:T(8,128)(2,1)S(1)} %get-tuple-element.45), channel_id=1, source_target_pairs={{2,4},{6,8},{10,12},{4,2},{8,6},{12,10},{3,5},{7,9},{11,13},{5,3},... | collective-permute-start | bytes 491528 | tf_op jit(solution)/shard_map/ppermute | solution.py:620
  10.1 0.0 collective-permute-done.3.v_ref.swap_v_ref
  10.1 1.9 %collective-permute-done.2.k_ref.swap_k_ref = bf16[128,640]{1,0:T(8,128)(2,1)S(1)} collective-permute-done((bf16[128,640]{1,0:T(8,128)(2,1)S(1)}, bf16[128,640]{1,0:T(8,128)(2,1)S(1)}, u32[]{:S(2)}, u32[]{:S(2)}) %collective-permute-start.2) | collective-permute-done | bytes 163872 | tf_op jit(solution)/shard_map/ppermute | solution.py:618
  12.0 0.0 collective-permute-done.4.earlier_ref.halo_ref
  12.0 0.3 collective-permute-start.7
  12.3 0.0 copy-done
  12.3 0.7 %shard_map.97 = (bf16[128,640]{1,0:T(8,128)(2,1)S(1)}, f32[384,128]{1,0:T(8,128)S(1)}, f32[384,128]{1,0:T(8,128)S(1)}) custom-call(s32[2,4,16]{2,1,0:T(4,128)S(1)} %bitcast.8, bf16[128,640]{1,0:T(8,128)(2,1)S(1)} %collective-permute-done.2.k_ref.swap_k_ref, bf16[128,640]{1,0:T(8,128)(2,1)S(1)} %collective-permute-done.3.v_ref.swap_v_ref, ...), custom_call_target="tpu_custom_call" | custom-call | flops 1000000 | bytes 1000000 | tf_op jit(solution)/shard_map/pallas_call | solution.py:623
  13.1 4.2 %collective-permute-start.5 = (bf16[128,640]{1,0:T(8,128)(2,1)S(1)}, bf16[128,640]{1,0:T(8,128)(2,1)S(1)}, u32[]{:S(2)}, u32[]{:S(2)}) collective-permute-start(bf16[128,640]{1,0:T(8,128)(2,1)S(1)} %get-tuple-element.49), channel_id=1, source_target_pairs={{2,4},{6,8},{10,12},{4,2},{8,6},{12,10},{3,5},{7,9},{11,13},{5,3},... | collective-permute-start | bytes 491528 | tf_op jit(solution)/shard_map/ppermute | solution.py:629
  17.2 0.0 collective-permute-done.1.earlier_ref.halo_ref
  17.3 0.0 collective-permute-done.7.swap_halo_ref
  17.3 1.8 %collective-permute-done.6.swap_qt_ref = bf16[256,640]{1,0:T(8,128)(2,1)S(1)} collective-permute-done((bf16[256,640]{1,0:T(8,128)(2,1)S(1)}, bf16[256,640]{1,0:T(8,128)(2,1)S(1)}, u32[]{:S(2)}, u32[]{:S(2)}) %collective-permute-start.6) | collective-permute-done | bytes 327712 | tf_op jit(solution)/shard_map/ppermute | solution.py:619
  19.0 1.4 %shard_map.98 = (bf16[144,640]{1,0:T(8,128)(2,1)S(1)}, bf16[144,640]{1,0:T(8,128)(2,1)S(1)}, f32[640,640]{1,0:T(8,128)S(1)}) custom-call(bf16[128,640]{1,0:T(8,128)(2,1)S(1)} %collective-permute-done.4.earlier_ref.halo_ref, bf16[128,640]{1,0:T(8,128)(2,1)S(1)} %collective-permute-done.7.swap_halo_ref, bf16[256,640]{1,0:T(8,128)(2,1)S(1)} %get-tuple-element.50.own_ref, ...), custom_call_target="tpu_custom_call" | custom-call | flops 500000000 | bytes 2000000 | tf_op jit(solution)/shard_map/pallas_call | solution.py:631
  20.4 0.3 collective-permute-start.9
  20.7 2.2 %collective-permute-start.10 = (bf16[144,640]{1,0:T(8,128)(2,1)S(1)}, bf16[144,640]{1,0:T(8,128)(2,1)S(1)}, u32[]{:S(2)}, u32[]{:S(2)}) collective-permute-start(bf16[144,640]{1,0:T(8,128)(2,1)S(1)} %get-tuple-element.58), channel_id=1, source_target_pairs={{0,18},{4,22},{8,26},{12,30},{2,16},{6,20},{10,24},{14,28},{16,2},... | collective-permute-start | bytes 552968 | tf_op jit(solution)/shard_map/ppermute | solution.py:638
  22.9 0.0 collective-permute-done.5.swap_halo_ref
  22.9 1.4 %shard_map.99 = (bf16[128,640]{1,0:T(8,128)(2,1)S(1)}, bf16[128,640]{1,0:T(8,128)(2,1)S(1)}, f32[384,640]{1,0:T(8,128)S(1)}, bf16[256,640]{1,0:T(8,128)(2,1)S(1)}, f32[128,640]{1,0:T(8,128)S(1)}) custom-call(bf16[128,640]{1,0:T(8,128)(2,1)S(1)} %collective-permute-done.1.earlier_ref.halo_ref, bf16[128,640]{1,0:T(8,128)(2,1)S(1)} %collective-permute-done.5.swap_halo_ref, ...), custom_call_target="tpu_custom_call" | custom-call | flops 500000000 | bytes 2000000 | tf_op jit(solution)/shard_map/pallas_call | solution.py:639
  24.3 3.2 %collective-permute-start.12 = (bf16[128,640]{1,0:T(8,128)(2,1)S(1)}, bf16[128,640]{1,0:T(8,128)(2,1)S(1)}, u32[]{:S(2)}, u32[]{:S(2)}) collective-permute-start(bf16[128,640]{1,0:T(8,128)(2,1)S(1)} %get-tuple-element.64), channel_id=1, source_target_pairs={{2,4},{6,8},{10,12},{4,2},{8,6},{12,10},{3,5},{7,9},{11,13},{5,3},... | collective-permute-start | bytes 491528 | tf_op jit(solution)/shard_map/ppermute | solution.py:646
  27.5 0.3 collective-permute-start.8
  27.8 3.0 %collective-permute-start.11 = (bf16[128,640]{1,0:T(8,128)(2,1)S(1)}, bf16[128,640]{1,0:T(8,128)(2,1)S(1)}, u32[]{:S(2)}, u32[]{:S(2)}) collective-permute-start(bf16[128,640]{1,0:T(8,128)(2,1)S(1)} %get-tuple-element.62), channel_id=1, source_target_pairs={{2,4},{6,8},{10,12},{4,2},{8,6},{12,10},{3,5},{7,9},{11,13},{5,3},... | collective-permute-start | bytes 491528 | tf_op jit(solution)/shard_map/ppermute | solution.py:648
  30.8 0.6 %collective-permute-done.12.b_ref = bf16[128,640]{1,0:T(8,128)(2,1)S(1)} collective-permute-done((bf16[128,640]{1,0:T(8,128)(2,1)S(1)}, bf16[128,640]{1,0:T(8,128)(2,1)S(1)}, u32[]{:S(2)}, u32[]{:S(2)}) %collective-permute-start.12) | collective-permute-done | bytes 163872 | tf_op jit(solution)/shard_map/ppermute | solution.py:646
  31.4 0.7 %collective-permute-start.13 = (bf16[128,640]{1,0:T(8,128)(2,1)S(1)}, bf16[128,640]{1,0:T(8,128)(2,1)S(1)}, u32[]{:S(2)}, u32[]{:S(2)}) collective-permute-start(bf16[128,640]{1,0:T(8,128)(2,1)S(1)} %shard_map.102), channel_id=1, source_target_pairs={{0,16},{16,0},{1,17},{17,1},{2,18},{18,2},{3,19},{19,3},{4,20},{20... | collective-permute-start | bytes 491528 | tf_op jit(solution)/shard_map/ppermute | solution.py:655
  32.1 0.0 collective-permute-done.9.near_ref
  32.1 0.0 collective-permute-done.10.swap_near_ref
  32.1 0.1 shard_map.100
  32.2 2.8 %collective-permute-done.8.swap_first_ref = bf16[256,640]{1,0:T(8,128)(2,1)S(1)} collective-permute-done((bf16[256,640]{1,0:T(8,128)(2,1)S(1)}, bf16[256,640]{1,0:T(8,128)(2,1)S(1)}, u32[]{:S(2)}, u32[]{:S(2)}) %collective-permute-start.8) | collective-permute-done | bytes 327712 | tf_op jit(solution)/shard_map/ppermute | solution.py:647
  35.0 0.3 shard_map.101
  35.3 0.0 collective-permute-done.11.far_ref
  35.3 3.3 %collective-permute-done.13.swap_last_ref = bf16[128,640]{1,0:T(8,128)(2,1)S(1)} collective-permute-done((bf16[128,640]{1,0:T(8,128)(2,1)S(1)}, bf16[128,640]{1,0:T(8,128)(2,1)S(1)}, u32[]{:S(2)}, u32[]{:S(2)}) %collective-permute-start.13) | collective-permute-done | bytes 163872 | tf_op jit(solution)/shard_map/ppermute | solution.py:655
  38.5 0.2 shard_map.103
  38.7 2.6 %collective-permute-start.14 = (f32[256,1]{1,0:T(8,128)S(1)}, f32[256,1]{1,0:T(8,128)S(1)}, u32[]{:S(2)}, u32[]{:S(2)}) collective-permute-start(f32[256,1]{1,0:T(8,128)S(1)} %get-tuple-element.70.sums_ref.earlier_ref), channel_id=1, source_target_pairs={{0,1},{1,0},{2,3},{3,2},{4,5},{5,4},{6,7},{7,6},{8,9},{9,8},{10,11... | collective-permute-start | bytes 3080 | tf_op jit(solution)/shard_map/ppermute | solution.py:666
  41.3 0.8 %shard_map.105 = bf16[128,1280]{1,0:T(8,128)(2,1)} custom-call(f32[384,640]{1,0:T(8,128)S(1)} %get-tuple-element.55.own_ref, f32[128,640]{1,0:T(8,128)S(1)} %get-tuple-element.59.near_ref, bf16[128,640]{1,0:T(8,128)(2,1)S(1)} %collective-permute-done.11.far_ref, bf16[256,640]{1,0:T(8,128)(2,1)S(1)} %collective-permute-done.8.swap_first_ref, ...), custom_call_target="tpu_custom_call" | custom-call | flops 1000000 | bytes 1000000 | tf_op jit(solution)/shard_map/pallas_call | solution.py:667
  42.1 0.2 collective-permute-done.14.peer_ref
  42.3 1.0 %shard_map.104 = (bf16[128,1280]{1,0:T(8,128)(2,1)}, bf16[128,1280]{1,0:T(8,128)(2,1)}) custom-call(bf16[128,1280]{1,0:T(8,128)(2,1)S(1)} %get-tuple-element.38.q_ref, bf16[128,1280]{1,0:T(8,128)(2,1)S(1)} %get-tuple-element.39.k_ref, f32[128,1280]{1,0:T(8,128)S(1)} %get-tuple-element.61.gated_q_ref, f32[128,1280]{1,0:T(8,128)S(1)} %get-tuple-element.68.gated_k_ref, ...), custom_call_target="tpu_custom_call" | custom-call | flops 1000000 | bytes 1000000 | tf_op jit(solution)/shard_map/pallas_call | solution.py:668
  (2 shorter events, 0.0 us)
Async XLA Ops:
  0.6 11.7 %copy-start = (s32[2,16,4]{1,2,0:T(4,128)S(1)}, s32[2,16,4]{1,2,0:T(4,128)}, u32[]{:S(2)}) copy-start(s32[2,16,4]{1,2,0:T(4,128)} %param.13) | copy-start | bytes 1540
  2.0 2.0 %collective-permute-start = (f32[256,1]{1,0:T(8,128)S(1)}, f32[256,1]{1,0:T(8,128)S(1)}, u32[]{:S(2)}, u32[]{:S(2)}) collective-permute-start(f32[256,1]{1,0:T(8,128)S(1)} %get-tuple-element.44.sums_ref), channel_id=1, source_target_pairs={{0,1},{1,0},{2,3},{3,2},{4,5},{5,4},{6,7},{7,6},{8,9},{9,8},{10,11... | collective-permute-start | bytes 3080 | tf_op jit(solution)/shard_map/ppermute | solution.py:612
  2.7 7.4 %collective-permute-start.3 = (bf16[128,640]{1,0:T(8,128)(2,1)S(1)}, bf16[128,640]{1,0:T(8,128)(2,1)S(1)}, u32[]{:S(2)}, u32[]{:S(2)}) collective-permute-start(bf16[128,640]{1,0:T(8,128)(2,1)S(1)} %get-tuple-element.47), channel_id=1, source_target_pairs={{0,16},{16,0},{1,17},{17,1},{2,18},{18,2},{3,19},{19,3},{4,20},{20... | collective-permute-start | bytes 491528 | tf_op jit(solution)/shard_map/ppermute | solution.py:611
  4.2 7.8 %collective-permute-start.2 = (bf16[128,640]{1,0:T(8,128)(2,1)S(1)}, bf16[128,640]{1,0:T(8,128)(2,1)S(1)}, u32[]{:S(2)}, u32[]{:S(2)}) collective-permute-start(bf16[128,640]{1,0:T(8,128)(2,1)S(1)} %get-tuple-element.46), channel_id=1, source_target_pairs={{0,16},{16,0},{1,17},{17,1},{2,18},{18,2},{3,19},{19,3},{4,20},{20... | collective-permute-start | bytes 491528 | tf_op jit(solution)/shard_map/ppermute | solution.py:618
  5.3 6.8 %collective-permute-start.4 = (bf16[128,640]{1,0:T(8,128)(2,1)S(1)}, bf16[128,640]{1,0:T(8,128)(2,1)S(1)}, u32[]{:S(2)}, u32[]{:S(2)}) collective-permute-start(bf16[128,640]{1,0:T(8,128)(2,1)S(1)} %get-tuple-element.48), channel_id=1, source_target_pairs={{0,2},{4,6},{8,10},{12,14},{2,0},{6,4},{10,8},{14,12},{1,3},{5,7},... | collective-permute-start | bytes 491528 | tf_op jit(solution)/shard_map/ppermute | solution.py:617
  5.5 13.6 %collective-permute-start.6 = (bf16[256,640]{1,0:T(8,128)(2,1)S(1)}, bf16[256,640]{1,0:T(8,128)(2,1)S(1)}, u32[]{:S(2)}, u32[]{:S(2)}) collective-permute-start(bf16[256,640]{1,0:T(8,128)(2,1)S(1)} %get-tuple-element.51), channel_id=1, source_target_pairs={{0,16},{16,0},{1,17},{17,1},{2,18},{18,2},{3,19},{19,3},{4,20},{20... | collective-permute-start | bytes 983048 | tf_op jit(solution)/shard_map/ppermute | solution.py:619
  6.0 11.3 %collective-permute-start.1 = (bf16[128,640]{1,0:T(8,128)(2,1)S(1)}, bf16[128,640]{1,0:T(8,128)(2,1)S(1)}, u32[]{:S(2)}, u32[]{:S(2)}) collective-permute-start(bf16[128,640]{1,0:T(8,128)(2,1)S(1)} %get-tuple-element.45), channel_id=1, source_target_pairs={{2,4},{6,8},{10,12},{4,2},{8,6},{12,10},{3,5},{7,9},{11,13},{5,3},... | collective-permute-start | bytes 491528 | tf_op jit(solution)/shard_map/ppermute | solution.py:620
  12.0 5.2 %collective-permute-start.7 = (bf16[128,640]{1,0:T(8,128)(2,1)S(1)}, bf16[128,640]{1,0:T(8,128)(2,1)S(1)}, u32[]{:S(2)}, u32[]{:S(2)}) collective-permute-start(bf16[128,640]{1,0:T(8,128)(2,1)S(1)} %shard_map.96.earlier_ref), channel_id=1, source_target_pairs={{0,2},{4,6},{8,10},{12,14},{2,0},{6,4},{10,8},{14,12},{1,3},{5,7},... | collective-permute-start | bytes 491528 | tf_op jit(solution)/shard_map/ppermute | solution.py:622
  13.1 9.8 %collective-permute-start.5 = (bf16[128,640]{1,0:T(8,128)(2,1)S(1)}, bf16[128,640]{1,0:T(8,128)(2,1)S(1)}, u32[]{:S(2)}, u32[]{:S(2)}) collective-permute-start(bf16[128,640]{1,0:T(8,128)(2,1)S(1)} %get-tuple-element.49), channel_id=1, source_target_pairs={{2,4},{6,8},{10,12},{4,2},{8,6},{12,10},{3,5},{7,9},{11,13},{5,3},... | collective-permute-start | bytes 491528 | tf_op jit(solution)/shard_map/ppermute | solution.py:629
  20.4 11.7 %collective-permute-start.9 = (bf16[144,640]{1,0:T(8,128)(2,1)S(1)}, bf16[144,640]{1,0:T(8,128)(2,1)S(1)}, u32[]{:S(2)}, u32[]{:S(2)}) collective-permute-start(bf16[144,640]{1,0:T(8,128)(2,1)S(1)} %get-tuple-element.57), channel_id=1, source_target_pairs={{0,2},{4,6},{8,10},{12,14},{2,0},{6,4},{10,8},{14,12},{1,3},{5,7},... | collective-permute-start | bytes 552968 | tf_op jit(solution)/shard_map/ppermute | solution.py:637
  20.7 11.4 %collective-permute-start.10 = (bf16[144,640]{1,0:T(8,128)(2,1)S(1)}, bf16[144,640]{1,0:T(8,128)(2,1)S(1)}, u32[]{:S(2)}, u32[]{:S(2)}) collective-permute-start(bf16[144,640]{1,0:T(8,128)(2,1)S(1)} %get-tuple-element.58), channel_id=1, source_target_pairs={{0,18},{4,22},{8,26},{12,30},{2,16},{6,20},{10,24},{14,28},{16,2},... | collective-permute-start | bytes 552968 | tf_op jit(solution)/shard_map/ppermute | solution.py:638
  24.3 7.1 %collective-permute-start.12 = (bf16[128,640]{1,0:T(8,128)(2,1)S(1)}, bf16[128,640]{1,0:T(8,128)(2,1)S(1)}, u32[]{:S(2)}, u32[]{:S(2)}) collective-permute-start(bf16[128,640]{1,0:T(8,128)(2,1)S(1)} %get-tuple-element.64), channel_id=1, source_target_pairs={{2,4},{6,8},{10,12},{4,2},{8,6},{12,10},{3,5},{7,9},{11,13},{5,3},... | collective-permute-start | bytes 491528 | tf_op jit(solution)/shard_map/ppermute | solution.py:646
  27.5 7.6 %collective-permute-start.8 = (bf16[256,640]{1,0:T(8,128)(2,1)S(1)}, bf16[256,640]{1,0:T(8,128)(2,1)S(1)}, u32[]{:S(2)}, u32[]{:S(2)}) collective-permute-start(bf16[256,640]{1,0:T(8,128)(2,1)S(1)} %get-tuple-element.56), channel_id=1, source_target_pairs={{0,16},{16,0},{1,17},{17,1},{2,18},{18,2},{3,19},{19,3},{4,20},{20... | collective-permute-start | bytes 983048 | tf_op jit(solution)/shard_map/ppermute | solution.py:647
  27.8 7.5 %collective-permute-start.11 = (bf16[128,640]{1,0:T(8,128)(2,1)S(1)}, bf16[128,640]{1,0:T(8,128)(2,1)S(1)}, u32[]{:S(2)}, u32[]{:S(2)}) collective-permute-start(bf16[128,640]{1,0:T(8,128)(2,1)S(1)} %get-tuple-element.62), channel_id=1, source_target_pairs={{2,4},{6,8},{10,12},{4,2},{8,6},{12,10},{3,5},{7,9},{11,13},{5,3},... | collective-permute-start | bytes 491528 | tf_op jit(solution)/shard_map/ppermute | solution.py:648
  31.4 7.2 %collective-permute-start.13 = (bf16[128,640]{1,0:T(8,128)(2,1)S(1)}, bf16[128,640]{1,0:T(8,128)(2,1)S(1)}, u32[]{:S(2)}, u32[]{:S(2)}) collective-permute-start(bf16[128,640]{1,0:T(8,128)(2,1)S(1)} %shard_map.102), channel_id=1, source_target_pairs={{0,16},{16,0},{1,17},{17,1},{2,18},{18,2},{3,19},{19,3},{4,20},{20... | collective-permute-start | bytes 491528 | tf_op jit(solution)/shard_map/ppermute | solution.py:655
  38.7 3.6 %collective-permute-start.14 = (f32[256,1]{1,0:T(8,128)S(1)}, f32[256,1]{1,0:T(8,128)S(1)}, u32[]{:S(2)}, u32[]{:S(2)}) collective-permute-start(f32[256,1]{1,0:T(8,128)S(1)} %get-tuple-element.70.sums_ref.earlier_ref), channel_id=1, source_target_pairs={{0,1},{1,0},{2,3},{3,2},{4,5},{5,4},{6,7},{7,6},{8,9},{9,8},{10,11... | collective-permute-start | bytes 3080 | tf_op jit(solution)/shard_map/ppermute | solution.py:666
